TPU v7x, 512 devices: a whole 4x4x16 slice. The times are simulated.
512 devices in a mesh: dom: 128 (over y, z, core), cls: 4 (over x).
Axes of the slice: x: 4, y: 4, z: 16, core: 2. Of those that a mesh axis runs over, the one named last changes fastest.
Arguments:
- images: bfloat16 [16384, 64, 256], P('dom', 'cls'), may hold values from -80 to 80
- references: bfloat16 [256, 64, 256], P('dom', 'cls'), may hold values from -6 to 6
- sharpness: bfloat16 [256], P('dom'), may hold values from 20 to 200
- classes: int32 [16384, 1], P('dom'), may hold values from 0 to 255; in each aligned block of 128 rows (0 to 127, 128 to 255, ...) at most 4 rows name the same one
- rotations: int32 [16384], P('dom'), may hold values from 0 to 255
- shifts: int32 [16384], P('dom'), may hold values from 0 to 24
- shift_phase: float32 [25, 64, 128], P(None, 'cls'), may hold values from -3.140625 to 3.140625
Outputs:
- class_sums: float32 [256, 64, 256], P('dom', 'cls')
- class_weights: float32 [256], P('dom')
Inputs may be any that keep to these rules, and one draw needn't show every extreme that they name: `classes`: within the rows of one device (aligned blocks of 128 particles) no class is named by more than 4 particles, a bound that some block reaches; every class is named by some particle.
All inputs are finite; a program needn't handle non-finite values.
Results may differ from a plain program's by a relative error of at most 0.0048.
Values may be sent and summed in bfloat16 or wider, within the bound.
No kernel may reach another device: no remote copies, remote signals or barrier semaphores. Data moves between devices by JAX's collectives and lax.ppermute only.
A program may use at most 64 MiB of HBM per device.

v0:
```python
import math

import jax
import jax.numpy as jnp
from jax import lax
from jax.sharding import PartitionSpec as P

C = 256
MOST = 4


EPSILON = 1e-06


def spectral_table(length):
    half_len = length // 2
    angle_index = jnp.arange(length, dtype=jnp.int32)
    freq_index = jnp.arange(half_len, dtype=jnp.int32)
    turn_count = angle_index[:, None] * freq_index[None, :] % length
    radians = turn_count.astype(jnp.float32) * (2.0 * math.pi / length)
    norm_scale = 1.0 / math.sqrt(length)
    both = jnp.concatenate([jnp.cos(radians), -jnp.sin(radians)], 1) * norm_scale
    return both.astype(jnp.bfloat16)


def score_particles(flat_rows, power, labels, references, sharpness):
    panel = lax.all_gather(references, "dom", axis=0, tiled=True)
    sharp_piece = lax.all_gather(sharpness, "dom", axis=0, tiled=True)
    panel_rows = panel.shape[0]
    panel_flat = panel.reshape(panel_rows, -1)
    scores = lax.dot_general(
        flat_rows, panel_flat, (((1,), (1,)), ((), ())), preferred_element_type=jnp.float32
    )
    member = (labels[:, None] == jnp.arange(panel_rows, dtype=jnp.int32)[None, :]).astype(
        jnp.float32
    )
    panel_norms = jnp.einsum("nf,nf->n", panel_flat, panel_flat, preferred_element_type=jnp.float32)
    inner_sum = jnp.sum(scores * member, 1)
    ref_power = jnp.sum(member * panel_norms[None, :], 1)
    sharp_sum = jnp.sum(member * sharp_piece.astype(jnp.float32)[None, :], 1)
    inner_sum, ref_power, sharp_sum = (inner_sum, ref_power, sharp_sum)
    inner_sum, power_all, ref_all = lax.psum((inner_sum, power, ref_power), "cls")
    correlation = inner_sum / jnp.sqrt((power_all + EPSILON) * (ref_all + EPSILON))
    return jax.nn.sigmoid(sharp_sum * correlation).astype(jnp.bfloat16)


def body(images, references, sharpness, classes, rotations, shifts, shift_phase):
    rows_dev, cycle_count, length = images.shape
    half_len = length // 2
    width = cycle_count * length
    owners = lax.axis_size("dom")
    per_owner = C // owners
    dft_table = spectral_table(length)
    spectra = jnp.dot(
        images.reshape(rows_dev * cycle_count, length),
        dft_table,
        preferred_element_type=jnp.float32,
    )
    spectra = spectra.reshape(rows_dev, cycle_count, length)
    shift_total = shift_phase.shape[0]
    shift_pick = (shifts[:, None] == jnp.arange(shift_total, dtype=jnp.int32)[None, :]).astype(
        jnp.float32
    )
    phases = jnp.dot(
        shift_pick,
        shift_phase.reshape(shift_total, cycle_count * half_len),
        precision=lax.Precision.HIGHEST,
    )
    phases = phases.reshape(rows_dev, cycle_count, half_len)
    freq_index = jnp.arange(half_len, dtype=jnp.int32)
    turn_count = rotations[:, None] * freq_index[None, :] % length
    phase_angle = turn_count.astype(jnp.float32)[:, None, :] * (2.0 * math.pi / length) + phases
    cosine = jnp.cos(phase_angle)
    sine_val = jnp.sin(phase_angle)
    real_part = spectra[:, :, :half_len]
    imag_part = spectra[:, :, half_len:]
    aligned = jnp.concatenate(
        [real_part * cosine - imag_part * sine_val, real_part * sine_val + imag_part * cosine], -1
    ).astype(jnp.bfloat16)
    flat_rows = aligned.reshape(rows_dev, width)
    labels = classes[:, 0]
    power = jnp.einsum("pf,pf->p", flat_rows, flat_rows, preferred_element_type=jnp.float32)
    member_all = (labels[:, None] == jnp.arange(C, dtype=jnp.int32)[None, :]).astype(jnp.int32)
    before = jnp.cumsum(member_all, 0) - member_all
    rank_in_class = jnp.sum(before * member_all, 1)
    slot_index = labels * MOST + rank_in_class
    slot_rows = jnp.zeros((C * MOST, width), jnp.bfloat16).at[slot_index].set(flat_rows)
    slot_rows = slot_rows.reshape(owners, per_owner, MOST, width)
    weight = score_particles(flat_rows, power, labels, references, sharpness)
    weight_slots = jnp.zeros((C * MOST,), jnp.bfloat16).at[slot_index].set(weight)
    weight_slots = weight_slots.reshape(owners, per_owner, MOST)
    got_rows = lax.all_to_all(slot_rows, "dom", split_axis=0, concat_axis=0, tiled=True)
    got_weight = lax.all_to_all(weight_slots, "dom", split_axis=0, concat_axis=0, tiled=True)
    row_total = jnp.einsum("sjm,sjmf->jf", got_weight, got_rows, preferred_element_type=jnp.float32)
    totals = jnp.sum(got_weight.astype(jnp.float32), axis=(0, 2))
    return (row_total.reshape(per_owner, cycle_count, length), totals)


def solution(mesh):
    return jax.shard_map(
        body,
        mesh=mesh,
        in_specs=(
            P("dom", "cls", None),
            P("dom", "cls", None),
            P("dom"),
            P("dom", None),
            P("dom"),
            P("dom"),
            P(None, "cls", None),
        ),
        out_specs=(P("dom", "cls", None), P("dom")),
        check_vma=False,
    )
```

profile of v0, /device:TPU:40, one launch (start us, length us, event | category | flops | bytes accessed | tf_op | source)
XLA Modules:
  0.0 736.2 jit_solution(11397654470349702689)
XLA Ops:
  7.2 0.7 all-gather.2.cloned.1.call-update
  7.9 1.3 dynamic-slice
  9.8 0.9 dynamic-update-slice
  10.7 212.9 %all-reduce = bf16[256]{0:T(256)(128)(2,1)S(1)} all-reduce(bf16[256]{0:T(256)(128)(2,1)S(1)} %dynamic-update-slice), channel_id=1, replica_groups=mesh['dom'=128,'cls'=4] {'dom'}, use_global_device_ids=true, to_apply=%add | all-reduce | flops 256 | bytes 1024
  223.7 0.5 sine_negate_fusion
  224.2 1.8 convolution_bitcast_fusion
  226.0 1.9 copy.21
  227.9 1.5 fusion.34
  229.4 1.6 copy.42
  231.0 1.6 copy.43
  232.7 0.2 reduce_window_sum.11
  232.9 0.9 slice_bitcast_fusion
  234.1 4.4 fusion.35
  238.4 0.4 multiply_subtract_fusion
  238.8 0.8 copy-done.2
  239.8 0.6 fusion.5
  240.5 4.4 copy.41
  244.8 2.3 fusion.2
  247.2 0.7 fusion.7
  247.8 0.2 select_reduce_fusion
  248.0 10.7 %all-reduce.1 = (f32[128]{0:T(128)S(1)}, f32[128]{0:T(128)S(1)}, f32[128]{0:T(128)S(1)}) all-reduce(f32[128]{0:T(128)S(1)} %fusion.7, f32[128]{0:T(128)S(1)} %get-tuple-element.2, f32[128]{0:T(128)S(1)} %fusion.5), channel_id=1, replica_groups=mesh['dom'=128,'cls'=4] {'cls'}, use_global_device_ids=true, to_apply=%region_4.5 | all-reduce | flops 384 | bytes 3072 | tf_op jit(solution)/shard_map/psum | solution.py:42
  258.7 1.4 scatter_custom_fusion
  260.1 0.8 reshape.69
  260.8 50.9 %all-to-all-start = ((bf16[128,2,4]{2,1,0:T(2,128)(2,1)}), bf16[128,2,4]{2,1,0:T(2,128)(2,1)S(1)}, u32[]{:S(2)}, u32[]{:S(2)}) async-start(bf16[128,2,4]{2,1,0:T(2,128)(2,1)} %reshape.69), calls=%async_computation | async-start | bytes 131072 | tf_op jit(solution)/shard_map/all_to_all | solution.py:93
  311.7 0.5 copy.28
  312.3 6.9 scatter_custom_fusion.1
  319.2 13.1 %reshape.70 = bf16[128,2,4,4096]{3,2,1,0:T(4,128)(2,1)} reshape(bf16[1024,4096]{1,0:T(8,128)(2,1)} %scatter_custom_fusion.1) | data formatting | bytes 16777216 | tf_op jit(solution)/shard_map/reshape | solution.py:88
  332.3 16.7 %all-to-all-start.1 = ((bf16[128,2,4,4096]{3,2,1,0:T(4,128)(2,1)}), bf16[128,2,4,4096]{3,2,1,0:T(4,128)(2,1)}, u32[]{:S(2)}, u32[]{:S(2)}) async-start(bf16[128,2,4,4096]{3,2,1,0:T(4,128)(2,1)} %reshape.70), calls=%async_computation.1 | async-start | bytes 16777216 | tf_op jit(solution)/shard_map/all_to_all | solution.py:92
  349.0 0.8 convert_reduce_fusion
  349.8 366.7 %all-to-all-done.1 = bf16[128,2,4,4096]{3,2,1,0:T(4,128)(2,1)} async-done(((bf16[128,2,4,4096]{3,2,1,0:T(4,128)(2,1)}), bf16[128,2,4,4096]{3,2,1,0:T(4,128)(2,1)}, u32[]{:S(2)}, u32[]{:S(2)}) %all-to-all-start.1) | async-done | bytes 8388640 | tf_op jit(solution)/shard_map/all_to_all | solution.py:92
  716.5 12.2 %fusion = f32[2,1,4096,1]{2,1,3,0:T(1,128)S(1)} fusion(bf16[128,2,4,1]{0,3,2,1:T(2,128)(2,1)S(1)} %copy.36, bf16[128,2,4,4096]{3,2,1,0:T(4,128)(2,1)} %all-to-all-done.1), kind=kOutput, calls=%fused_computation.2 | convolution fusion | flops 8388608 | bytes 8423424 | tf_op jit(solution)/shard_map/sjm,sjmf->jf/dot_general | solution.py:94
  728.7 0.6 copy.54
  (30 shorter events, 0.7 us)
Async XLA Ops:
  7.2 217.0 %copy-start = (bf16[128,16,256]{2,1,0:T(8,128)(2,1)S(1)}, bf16[128,16,256]{2,1,0:T(8,128)(2,1)}, u32[]{:S(2)}) copy-start(bf16[128,16,256]{2,1,0:T(8,128)(2,1)} %param.7) | copy-start | bytes 3145732
  7.2 233.3 %all-gather.2.cloned.1.call-start = ((), (), s32[]{:S(2)}) async-start(), calls=%async_computation.2 | async-start | bytes 2113536 | tf_op jit(solution)/shard_map/all_gather | solution.py:27
  229.4 3.2 copy-start.6
  229.4 4.6 copy-start.7
  229.4 4.7 copy-start.8
  238.8 0.8 copy-start.2
  238.8 1.0 copy-start.4
  240.5 6.7 copy-start.3
  240.5 6.7 copy-start.5
  244.8 2.3 copy-start.1
  260.8 71.4 %all-to-all-start = ((bf16[128,2,4]{2,1,0:T(2,128)(2,1)}), bf16[128,2,4]{2,1,0:T(2,128)(2,1)S(1)}, u32[]{:S(2)}, u32[]{:S(2)}) async-start(bf16[128,2,4]{2,1,0:T(2,128)(2,1)} %reshape.69), calls=%async_computation | async-start | bytes 131072 | tf_op jit(solution)/shard_map/all_to_all | solution.py:93
  332.3 384.2 %all-to-all-start.1 = ((bf16[128,2,4,4096]{3,2,1,0:T(4,128)(2,1)}), bf16[128,2,4,4096]{3,2,1,0:T(4,128)(2,1)}, u32[]{:S(2)}, u32[]{:S(2)}) async-start(bf16[128,2,4,4096]{3,2,1,0:T(4,128)(2,1)} %reshape.70), calls=%async_computation.1 | async-start | bytes 16777216 | tf_op jit(solution)/shard_map/all_to_all | solution.py:92
Sparse Core Ops, SparseCore 0:
  11.2 142.6 all-gather.1
where the time goes:
time: 737 us; the launch traced here: 736 us
  waiting for transfers between devices  367 us (50%)
  blocking collectives  224 us (30%)
  starting transfers between devices  67.6 us (9%)
  local copies, waits for them, and re-layouts  38.3 us (5%)
  matrix products  19 us (3%)
  between operations  14.9 us (2%)
    all_to_all x1, waiting for transfers between devices, body(): lax.all_to_all(slot_rows, 'dom', split_axis=0, concat_axis=0, tiled=True)  367 us
    unnamed x1, blocking collectives  213 us
    all_to_all x1, starting transfers between devices, body(): lax.all_to_all(weight_slots, 'dom', split_axis=0, concat_axis=0, tiled=True)  50.9 us
    all_to_all x1, starting transfers between devices, body(): lax.all_to_all(slot_rows, 'dom', split_axis=0, concat_axis=0, tiled=True)  16.7 us
  transfers between devices with their start and end apart: 3, of which 1 were waited for; matrix products, arithmetic and copies ran while one was open for 5% of the time, Pallas kernels for 0%

commit v1 on v0

v1 whole, which is shorter than its diff:
```python
import math

import jax
import jax.numpy as jnp
from jax import lax
from jax.experimental import pallas as pl
from jax.experimental.pallas import tpu as pltpu
from jax.sharding import Mesh
from jax.sharding import PartitionSpec as P

C = 256
EPSILON = 1e-06
NY, NZ, NX = 4, 16, 4
P_DEV = 128
R_DEV = 16
A = 256
FREQS = 128
R_OWN = R_DEV // NY
WIDE = R_OWN * A
FULL = WIDE + 128
SHIFT_ROWS = 32
VMEM_LIMIT = 40 * 1024 * 1024


def spectral_table(length):
    half_len = length // 2
    angle_index = jnp.arange(length, dtype=jnp.int32)
    freq_index = jnp.arange(half_len, dtype=jnp.int32)
    turn_count = angle_index[:, None] * freq_index[None, :] % length
    radians = turn_count.astype(jnp.float32) * (2.0 * math.pi / length)
    norm_scale = 1.0 / math.sqrt(length)
    both = jnp.concatenate([jnp.cos(radians), -jnp.sin(radians)], 1) * norm_scale
    return both.astype(jnp.bfloat16)


def iota(shape, axis):
    return lax.broadcasted_iota(jnp.int32, shape, axis)


def align_kernel(
    y_ref, images, table, rot, shift, label_row, phases, out0, out1, out2, out3, parts, turn, grid
):
    y = y_ref[0]
    for r in range(R_DEV):
        phase = phases[r]
        for at, value in ((0, jnp.cos(phase)), (FREQS, jnp.sin(phase))):
            high = value.astype(jnp.bfloat16)
            low = (value - high.astype(jnp.float32)).astype(jnp.bfloat16)
            lanes = slice(r * A + at, r * A + at + FREQS)
            parts[0:SHIFT_ROWS, lanes] = high
            parts[SHIFT_ROWS : 2 * SHIFT_ROWS, lanes] = low
    pick = (iota((P_DEV, 2 * SHIFT_ROWS), 1) & (SHIFT_ROWS - 1)) == shift[...]
    pick = pick.astype(jnp.float32).astype(jnp.bfloat16)
    turn[:, : R_DEV * A] = jnp.dot(pick, parts[...], preferred_element_type=jnp.float32)
    angle = ((rot[...] * iota((P_DEV, FREQS), 1)) & (A - 1)).astype(jnp.float32) * (2.0 * math.pi / A)
    turn[:, R_DEV * A : R_DEV * A + FREQS] = jnp.cos(angle)
    turn[:, R_DEV * A + FREQS :] = jnp.sin(angle)
    row, col = iota((A, A), 0), iota((A, A), 1)
    swap = (col == ((row & 15) * 16 + (row >> 4))).astype(jnp.float32).astype(jnp.bfloat16)
    dft = table[...]

    def block(b, _):
        rows = pl.ds(pl.multiple_of(b * 16, 16), 16)
        x = images[pl.ds(pl.multiple_of(b * 256, 256), 256), :]
        x = jnp.dot(swap, x, preferred_element_type=jnp.float32).astype(jnp.bfloat16)
        spectra = jnp.dot(x, dft, preferred_element_type=jnp.float32)
        cos_rot = turn[rows, R_DEV * A : R_DEV * A + FREQS]
        sin_rot = turn[rows, R_DEV * A + FREQS :]
        for r in range(R_DEV):
            cos_shift = turn[rows, r * A : r * A + FREQS]
            sin_shift = turn[rows, r * A + FREQS : r * A + A]
            cosine = cos_shift * cos_rot - sin_shift * sin_rot
            sine = sin_shift * cos_rot + cos_shift * sin_rot
            real = spectra[r * 16 : r * 16 + 16, :FREQS]
            imag = spectra[r * 16 : r * 16 + 16, FREQS:]
            grid[r, rows, :FREQS] = (real * cosine - imag * sine).astype(jnp.bfloat16)
            grid[r, rows, FREQS:] = (real * sine + imag * cosine).astype(jnp.bfloat16)
        return 0

    lax.fori_loop(0, P_DEV // 16, block, 0)
    label = label_row[...]
    label = ((label >> 1) & 1) * 128 + (label >> 2) * 2 + (label & 1)
    tail = jnp.broadcast_to(label.astype(jnp.float32), (P_DEV, 128)).astype(jnp.bfloat16)
    for d, out in enumerate((out0, out1, out2, out3)):
        first = ((y + d) & (NY - 1)) * R_OWN
        for i in range(R_OWN):
            out[:, i * A : i * A + A] = grid[first + i]
        out[:, WIDE:] = tail


def score_kernel(y_ref, a0, a1, a2, a3, panel, out, rows_out, stats):
    y = y_ref[0]
    refs = panel[:, :WIDE]
    wide = refs.astype(jnp.float32)
    norm = jnp.sum(wide * wide, axis=1, keepdims=True)
    sharp = panel[:, WIDE:].astype(jnp.float32)
    diagonal = iota((P_DEV, P_DEV), 0) == iota((P_DEV, P_DEV), 1)
    for d, rows in enumerate((a0, a1, a2, a3)):
        source = (y - d) & (NY - 1)
        flat = rows[:, :WIDE]
        label = rows[0:16, WIDE:].astype(jnp.float32)[0:1].astype(jnp.int32)
        member = iota((C, P_DEV), 0) == label
        scores = lax.dot_general(
            refs, flat, (((1,), (1,)), ((), ())), preferred_element_type=jnp.float32
        )
        gram = lax.dot_general(
            flat, flat, (((1,), (1,)), ((), ())), preferred_element_type=jnp.float32
        )
        inner = jnp.sum(jnp.where(member, scores, 0.0), axis=0, keepdims=True)
        power = jnp.sum(jnp.where(diagonal, gram, 0.0), axis=0, keepdims=True)
        ref_power = jnp.sum(jnp.where(member, norm, 0.0), axis=0, keepdims=True)
        own_sharp = jnp.sum(jnp.where(member, sharp, 0.0), axis=0, keepdims=True)
        for at, value in enumerate((inner, power, ref_power, own_sharp)):
            stats[pl.ds(at * NY + source, 1), :] = value
    value = stats[...]
    rows_out[...] = value
    for i in range(NX * NY):
        out[i] = value


def sum_kernel(at_ref, got, own, a0, a1, a2, a3, keep, send, weights):
    y, core = at_ref[0], at_ref[1]
    total = got[0]
    for i in range(1, NX * NY):
        total = total + got[i]
    inner, power, ref_power = total[0:NY], total[NY : 2 * NY], total[2 * NY : 3 * NY]
    sharp = own[3 * NY : 4 * NY, :]
    correlation = inner / jnp.sqrt((power + EPSILON) * (ref_power + EPSILON))
    weight = 1.0 / (1.0 + jnp.exp(-(sharp * correlation)))
    weights[0:NY, :] = weight.astype(jnp.bfloat16).astype(jnp.float32)
    parts = []
    for d, rows in enumerate((a0, a1, a2, a3)):
        source = (y - d) & (NY - 1)
        label = rows[0:16, WIDE:].astype(jnp.float32)[0:1].astype(jnp.int32) ^ (core * 128)
        member = iota((C, P_DEV), 0) == label
        parts.append(jnp.where(member, weights[pl.ds(source, 1), :], 0.0).astype(jnp.bfloat16))
    spread = jnp.concatenate(parts, axis=1)
    for i in range(R_OWN):
        lanes = slice(i * A, i * A + A)
        flat = jnp.concatenate([a0[:, lanes], a1[:, lanes], a2[:, lanes], a3[:, lanes]], axis=0)
        sums = jnp.dot(spread, flat, preferred_element_type=jnp.float32)
        keep[:, lanes] = sums[:128]
        send[:, lanes] = sums[128:]
    ones = jnp.ones((NY * P_DEV, 128), jnp.bfloat16)
    sums = jnp.dot(spread, ones, preferred_element_type=jnp.float32)
    keep[:, WIDE:] = sums[:128]
    send[:, WIDE:] = sums[128:]


def call(kernel, name, outs, scratch, flops, nbytes, n_scalar, n_vector):
    vmem = pl.BlockSpec(memory_space=pltpu.VMEM)
    smem = pl.BlockSpec(memory_space=pltpu.SMEM)
    return pl.pallas_call(
        kernel,
        out_shape=outs,
        in_specs=[smem] * n_scalar + [vmem] * n_vector,
        out_specs=jax.tree.map(lambda _: vmem, outs),
        scratch_shapes=scratch,
        compiler_params=pltpu.CompilerParams(vmem_limit_bytes=VMEM_LIMIT),
        cost_estimate=pl.CostEstimate(flops=flops, bytes_accessed=nbytes, transcendentals=0),
        name=name,
    )


def body(images, references, sharpness, classes, rotations, shifts, shift_phase):
    y = lax.axis_index("y").astype(jnp.int32)
    core = lax.axis_index("core").astype(jnp.int32)
    shape = jax.ShapeDtypeStruct

    pieces = references.reshape(2, NY, WIDE).transpose(1, 0, 2)
    sharp_tile = jnp.broadcast_to(sharpness[None, :, None], (NY, 2, 128))
    pieces = jnp.concatenate([pieces, sharp_tile], axis=2)
    pieces = jnp.broadcast_to(pieces[:, None], (NY, NZ, 2, FULL)).reshape(NY * NZ, 2, FULL)
    panel = lax.all_to_all(pieces, ("y", "z"), split_axis=0, concat_axis=0, tiled=True)

    phases = jnp.pad(shift_phase.transpose(1, 0, 2), ((0, 0), (0, SHIFT_ROWS - 25), (0, 0)))
    block = shape((P_DEV, FULL), jnp.bfloat16)
    aligned = call(
        align_kernel,
        "align",
        [block] * NY,
        [
            pltpu.VMEM((2 * SHIFT_ROWS, R_DEV * A), jnp.bfloat16),
            pltpu.VMEM((P_DEV, R_DEV * A + A), jnp.float32),
            pltpu.VMEM((R_DEV, P_DEV, A), jnp.bfloat16),
        ],
        800_000_000,
        4_000_000,
        1,
        6,
    )(
        y[None],
        images.reshape(P_DEV * R_DEV, A),
        spectral_table(A),
        rotations[:, None],
        shifts[:, None],
        classes.reshape(1, P_DEV),
        phases,
    )
    rows = [aligned[0]]
    for d in range(1, NY):
        rows.append(lax.ppermute(aligned[d], "y", [(i, (i + d) % NY) for i in range(NY)]))

    panel = lax.all_gather(panel.reshape(NY * NZ * 2, FULL), "core", axis=0, tiled=True)
    payload, stats = call(
        score_kernel,
        "score",
        [shape((NX * NY, 4 * NY, P_DEV), jnp.float32), shape((4 * NY, P_DEV), jnp.float32)],
        [pltpu.VMEM((4 * NY, P_DEV), jnp.float32)],
        600_000_000,
        2_000_000,
        1,
        5,
    )(y[None], *rows, panel)
    got = lax.all_to_all(payload, ("x", "y"), split_axis=0, concat_axis=0, tiled=True)
    half = shape((128, FULL), jnp.float32)
    keep, send = call(
        sum_kernel,
        "sum",
        [half, half],
        [pltpu.VMEM((8, P_DEV), jnp.float32)],
        300_000_000,
        3_000_000,
        1,
        6,
    )(jnp.stack([y, core]), got, stats, *rows)
    sums = keep + lax.ppermute(send, "core", [(0, 1), (1, 0)])
    totals = sums[:, WIDE : WIDE + 64]
    high = totals.astype(jnp.bfloat16)
    low = (totals - high.astype(jnp.float32)).astype(jnp.bfloat16)
    sums = jnp.concatenate([sums[:, :WIDE].astype(jnp.bfloat16), high, low], axis=1)
    sums = lax.all_to_all(
        sums.reshape(NY * NZ, 2, FULL), ("y", "z"), split_axis=0, concat_axis=0, tiled=True
    )
    sums = jnp.sum(sums.reshape(NY, NZ, 2, FULL).astype(jnp.float32), axis=1)
    class_sums = sums[:, :, :WIDE].reshape(NY, 2, R_OWN, A).transpose(1, 0, 2, 3)
    class_weights = sums[0, :, WIDE] + sums[0, :, WIDE + 64]
    return class_sums.reshape(2, R_DEV, A), class_weights


def solution(mesh):
    whole = Mesh(mesh.devices.reshape(NY, NZ, 2, NX), ("y", "z", "core", "x"))
    dom = ("y", "z", "core")
    return jax.shard_map(
        body,
        mesh=whole,
        in_specs=(
            P(dom, "x", None),
            P(dom, "x", None),
            P(dom),
            P(dom, None),
            P(dom),
            P(dom),
            P(None, "x", None),
        ),
        out_specs=(P(dom, "x", None), P(dom)),
        check_vma=False,
    )
```

time: 737 us -> 107 us (0.15)
  the two profiles are of different devices: /device:TPU:40 before, /device:TPU:8 now
where the time goes in v1:
time: 107 us
  blocking collectives  38.4 us (36%)
  starting transfers between devices  37.8 us (35%)
  waiting for transfers between devices  17.2 us (16%)
  Pallas kernels  7.15 us (7%)
  local copies, waits for them, and re-layouts  3.79 us (4%)
  other arithmetic  1.68 us (2%)
    all_to_all x1, blocking collectives, body(): lax.all_to_all(sums.reshape(NY * NZ, 2, FULL), ('y', 'z'), split_axis=0,...  36.1 us
    all_to_all x1, starting transfers between devices, body(): lax.all_to_all(pieces, ('y', 'z'), split_axis=0, concat_axis=0, tiled=True)  18.9 us
    ppermute x3, starting transfers between devices, body(): lax.ppermute(aligned[d], 'y', [(i, (i + d) % NY) for i in range(NY)])  10.6 us
    all_to_all x1, starting transfers between devices, body(): lax.all_to_all(payload, ('x', 'y'), split_axis=0, concat_axis=0, tiled=True)  6.43 us
    all_to_all x1, waiting for transfers between devices, body(): lax.all_to_all(payload, ('x', 'y'), split_axis=0, concat_axis=0, tiled=True)  6.32 us
    all_to_all x1, waiting for transfers between devices, body(): lax.all_to_all(pieces, ('y', 'z'), split_axis=0, concat_axis=0, tiled=True)  5.52 us
    pallas_call x1, Pallas kernels, body(): call(align_kernel, 'align', [block] * NY, [pltpu.VMEM((2 * SHIFT_ROWS, R_...  4.4 us
    ppermute x3, waiting for transfers between devices, body(): lax.ppermute(aligned[d], 'y', [(i, (i + d) % NY) for i in range(NY)])  3.4 us
  transfers between devices with their start and end apart: 6, of which 4 were waited for; matrix products, arithmetic and copies ran while one was open for 1% of the time, Pallas kernels for 4%

profile of v1, /device:TPU:8, one launch (start us, length us, event | category | flops | bytes accessed | tf_op | source)
XLA Modules:
  0.0 106.9 jit_solution(1428262989993359634)
XLA Ops:
  0.6 0.7 reshape.36
  1.4 0.1 broadcast_in_dim.10
  1.5 0.9 broadcast_in_dim.11
  2.4 18.9 %all-to-all-start = ((bf16[64,2,1152]{2,1,0:T(2,128)(2,1)}), bf16[64,2,1152]{2,1,0:T(2,128)(2,1)S(1)}, u32[]{:S(2)}, u32[]{:S(2)}) async-start(bf16[64,2,1152]{2,1,0:T(2,128)(2,1)} %bitcast.8), calls=%async_computation | async-start | bytes 589824 | tf_op jit(solution)/shard_map/all_to_all | solution.py:174
  21.3 0.1 copy.20.rot
  21.4 0.1 copy.21.shift
  21.5 0.1 copy.25
  21.6 0.5 sine_negate_fusion
  22.2 0.3 copy-done
  22.5 0.4 copy-done.1
  22.9 4.4 %align.1 = (bf16[128,1152]{1,0:T(8,128)(2,1)S(1)}, bf16[128,1152]{1,0:T(8,128)(2,1)S(1)}, bf16[128,1152]{1,0:T(8,128)(2,1)S(1)}, bf16[128,1152]{1,0:T(8,128)(2,1)S(1)}) custom-call(s32[1]{0:T(128)} %bitcast.y_ref, bf16[2048,256]{1,0:T(8,128)(2,1)S(1)} %bitcast.15, bf16[256,256]{1,0:T(8,128)(2,1)S(1)} %fusion.table, s32[128,1]{1,0:T(8,128)S(1)} %copy.20.rot, ...), custom_call_target="tpu_custom_call" | custom-call | flops 800000000 | bytes 4000000 | tf_op jit(solution)/shard_map/align/pallas_call | solution.py:178
  27.3 3.5 %collective-permute-start = (bf16[128,1152]{1,0:T(8,128)(2,1)S(1)}, bf16[128,1152]{1,0:T(8,128)(2,1)S(1)}, u32[]{:S(2)}, u32[]{:S(2)}) collective-permute-start(bf16[128,1152]{1,0:T(8,128)(2,1)S(1)} %get-tuple-element.11), channel_id=1, source_target_pairs={{0,128},{128,256},{256,384},{384,0},{1,129},{129,257},{257,385},{3... | collective-permute-start | bytes 884744 | tf_op jit(solution)/shard_map/ppermute | solution.py:202
  30.8 2.9 %collective-permute-start.1 = (bf16[128,1152]{1,0:T(8,128)(2,1)S(1)}, bf16[128,1152]{1,0:T(8,128)(2,1)S(1)}, u32[]{:S(2)}, u32[]{:S(2)}) collective-permute-start(bf16[128,1152]{1,0:T(8,128)(2,1)S(1)} %get-tuple-element.12), channel_id=1, source_target_pairs={{0,256},{128,384},{256,0},{384,128},{1,257},{129,385},{257,1},{385... | collective-permute-start | bytes 884744 | tf_op jit(solution)/shard_map/ppermute | solution.py:202
  33.7 4.3 %collective-permute-start.2 = (bf16[128,1152]{1,0:T(8,128)(2,1)S(1)}, bf16[128,1152]{1,0:T(8,128)(2,1)S(1)}, u32[]{:S(2)}, u32[]{:S(2)}) collective-permute-start(bf16[128,1152]{1,0:T(8,128)(2,1)S(1)} %get-tuple-element.13), channel_id=1, source_target_pairs={{0,384},{128,0},{256,128},{384,256},{1,385},{129,1},{257,129},{385... | collective-permute-start | bytes 884744 | tf_op jit(solution)/shard_map/ppermute | solution.py:202
  38.0 5.5 %all-to-all-done = bf16[64,2,1152]{2,1,0:T(2,128)(2,1)S(1)} async-done(((bf16[64,2,1152]{2,1,0:T(2,128)(2,1)}), bf16[64,2,1152]{2,1,0:T(2,128)(2,1)S(1)}, u32[]{:S(2)}, u32[]{:S(2)}) %all-to-all-start) | async-done | bytes 294944 | tf_op jit(solution)/shard_map/all_to_all | solution.py:174
  43.5 0.1 reshape.38
  43.6 2.2 %all_gather.3.panel = bf16[256,1152]{1,0:T(8,128)(2,1)S(1)} all-gather(bf16[128,1152]{1,0:T(8,128)(2,1)S(1)} %reshape.38), channel_id=1, replica_groups=mesh['y'=4,'z'=16,'core'=2,'x'=4] {'core'}, dimensions={0}, use_global_device_ids=true | all-gather | bytes 884736 | tf_op jit(solution)/shard_map/all_gather | solution.py:204
  45.8 3.4 %collective-permute-done.2.a3 = bf16[128,1152]{1,0:T(8,128)(2,1)S(1)} collective-permute-done((bf16[128,1152]{1,0:T(8,128)(2,1)S(1)}, bf16[128,1152]{1,0:T(8,128)(2,1)S(1)}, u32[]{:S(2)}, u32[]{:S(2)}) %collective-permute-start.2) | collective-permute-done | bytes 294944 | tf_op jit(solution)/shard_map/ppermute | solution.py:202
  49.2 1.7 %score.1 = (f32[16,16,128]{2,1,0:T(8,128)}, f32[16,128]{1,0:T(8,128)S(1)}) custom-call(s32[1]{0:T(128)} %bitcast.y_ref, bf16[128,1152]{1,0:T(8,128)(2,1)S(1)} %get-tuple-element.10.a0, bf16[128,1152]{1,0:T(8,128)(2,1)S(1)} %collective-permute-done.a1, bf16[128,1152]{1,0:T(8,128)(2,1)S(1)} %collective-permute-done.1.a2, ...), custom_call_target="tpu_custom_call" | custom-call | flops 600000000 | bytes 2000000 | tf_op jit(solution)/shard_map/score/pallas_call | solution.py:205
  50.9 6.4 %all-to-all-start.1 = ((f32[16,16,128]{2,1,0:T(8,128)}), f32[16,16,128]{2,1,0:T(8,128)S(1)}, u32[]{:S(2)}, u32[]{:S(2)}) async-start(f32[16,16,128]{2,1,0:T(8,128)} %get-tuple-element.14), calls=%async_computation.1 | async-start | bytes 262144 | tf_op jit(solution)/shard_map/all_to_all | solution.py:215
  57.3 0.1 pad_add_fusion.at_ref
  57.4 6.3 %all-to-all-done.1.got = f32[16,16,128]{2,1,0:T(8,128)S(1)} async-done(((f32[16,16,128]{2,1,0:T(8,128)}), f32[16,16,128]{2,1,0:T(8,128)S(1)}, u32[]{:S(2)}, u32[]{:S(2)}) %all-to-all-start.1) | async-done | bytes 131104 | tf_op jit(solution)/shard_map/all_to_all | solution.py:215
  63.7 1.1 %sum.1 = (f32[128,1152]{1,0:T(8,128)S(1)}, f32[128,1152]{1,0:T(8,128)S(1)}) custom-call(s32[2]{0:T(128)S(1)} %pad_add_fusion.at_ref, f32[16,16,128]{2,1,0:T(8,128)S(1)} %all-to-all-done.1.got, f32[16,128]{1,0:T(8,128)S(1)} %get-tuple-element.15.own, bf16[128,1152]{1,0:T(8,128)(2,1)S(1)} %get-tuple-element.10.a0, ...), custom_call_target="tpu_custom_call" | custom-call | flops 300000000 | bytes 3000000 | tf_op jit(solution)/shard_map/sum/pallas_call | solution.py:217
  64.8 1.9 %collective-permute-start.3 = (f32[128,1152]{1,0:T(8,128)S(1)}, f32[128,1152]{1,0:T(8,128)S(1)}, u32[]{:S(2)}, u32[]{:S(2)}) collective-permute-start(f32[128,1152]{1,0:T(8,128)S(1)} %get-tuple-element.17), channel_id=1, source_target_pairs={{0,4},{4,0},{1,5},{5,1},{2,6},{6,2},{3,7},{7,3},{8,12},{12,8},{9,1... | collective-permute-start | bytes 1769480 | tf_op jit(solution)/shard_map/ppermute | solution.py:227
  66.8 2.0 %collective-permute-done.3 = f32[128,1152]{1,0:T(8,128)S(1)} collective-permute-done((f32[128,1152]{1,0:T(8,128)S(1)}, f32[128,1152]{1,0:T(8,128)S(1)}, u32[]{:S(2)}, u32[]{:S(2)}) %collective-permute-start.3) | collective-permute-done | bytes 589856 | tf_op jit(solution)/shard_map/ppermute | solution.py:227
  68.7 0.1 add.20
  68.9 0.1 concatenate.11
  69.0 0.1 reshape.39
  69.1 36.1 %all_to_all.15 = bf16[64,2,1152]{2,1,0:T(2,128)(2,1)S(1)} all-to-all(bf16[64,2,1152]{2,1,0:T(2,128)(2,1)S(1)} %reshape.39), channel_id=1, replica_groups=mesh['y'=4,'z'=16,'core'=2,'x'=4] {'y','z'}, dimensions={0} | all-to-all | bytes 589824 | tf_op jit(solution)/shard_map/all_to_all | solution.py:232
  105.2 0.2 convert_reduce_fusion
  105.5 0.7 fusion.8
  106.2 0.6 reshape.41
  (21 shorter events, 0.2 us)
Async XLA Ops:
  0.6 0.7 copy-start.5
  2.4 18.9 %copy-start.3 = (s32[128]{0:T(128)S(1)}, s32[128]{0:T(128)}, u32[]{:S(2)}) copy-start(s32[128]{0:T(128)} %param.11) | copy-start | bytes 1540
  2.4 19.0 %copy-start.4 = (s32[128]{0:T(128)S(1)}, s32[128]{0:T(128)}, u32[]{:S(2)}) copy-start(s32[128]{0:T(128)} %param.12) | copy-start | bytes 1540
  2.4 19.1 %copy-start.2 = (f32[25,16,128]{2,1,0:T(8,128)S(1)}, f32[25,16,128]{2,1,0:T(8,128)}, u32[]{:S(2)}) copy-start(f32[25,16,128]{2,1,0:T(8,128)} %param.13) | copy-start | bytes 614404
  2.4 41.1 %all-to-all-start = ((bf16[64,2,1152]{2,1,0:T(2,128)(2,1)}), bf16[64,2,1152]{2,1,0:T(2,128)(2,1)S(1)}, u32[]{:S(2)}, u32[]{:S(2)}) async-start(bf16[64,2,1152]{2,1,0:T(2,128)(2,1)} %bitcast.8), calls=%async_computation | async-start | bytes 589824 | tf_op jit(solution)/shard_map/all_to_all | solution.py:174
  21.3 1.2 %copy-start = (bf16[128,16,256]{2,1,0:T(8,128)(2,1)S(1)}, bf16[128,16,256]{2,1,0:T(8,128)(2,1)}, u32[]{:S(2)}) copy-start(bf16[128,16,256]{2,1,0:T(8,128)(2,1)} %param.7) | copy-start | bytes 3145732
  22.2 0.7 copy-start.1
  27.3 18.5 %collective-permute-start = (bf16[128,1152]{1,0:T(8,128)(2,1)S(1)}, bf16[128,1152]{1,0:T(8,128)(2,1)S(1)}, u32[]{:S(2)}, u32[]{:S(2)}) collective-permute-start(bf16[128,1152]{1,0:T(8,128)(2,1)S(1)} %get-tuple-element.11), channel_id=1, source_target_pairs={{0,128},{128,256},{256,384},{384,0},{1,129},{129,257},{257,385},{3... | collective-permute-start | bytes 884744 | tf_op jit(solution)/shard_map/ppermute | solution.py:202
  30.8 15.1 %collective-permute-start.1 = (bf16[128,1152]{1,0:T(8,128)(2,1)S(1)}, bf16[128,1152]{1,0:T(8,128)(2,1)S(1)}, u32[]{:S(2)}, u32[]{:S(2)}) collective-permute-start(bf16[128,1152]{1,0:T(8,128)(2,1)S(1)} %get-tuple-element.12), channel_id=1, source_target_pairs={{0,256},{128,384},{256,0},{384,128},{1,257},{129,385},{257,1},{385... | collective-permute-start | bytes 884744 | tf_op jit(solution)/shard_map/ppermute | solution.py:202
  33.7 15.6 %collective-permute-start.2 = (bf16[128,1152]{1,0:T(8,128)(2,1)S(1)}, bf16[128,1152]{1,0:T(8,128)(2,1)S(1)}, u32[]{:S(2)}, u32[]{:S(2)}) collective-permute-start(bf16[128,1152]{1,0:T(8,128)(2,1)S(1)} %get-tuple-element.13), channel_id=1, source_target_pairs={{0,384},{128,0},{256,128},{384,256},{1,385},{129,1},{257,129},{385... | collective-permute-start | bytes 884744 | tf_op jit(solution)/shard_map/ppermute | solution.py:202
  50.9 12.8 %all-to-all-start.1 = ((f32[16,16,128]{2,1,0:T(8,128)}), f32[16,16,128]{2,1,0:T(8,128)S(1)}, u32[]{:S(2)}, u32[]{:S(2)}) async-start(f32[16,16,128]{2,1,0:T(8,128)} %get-tuple-element.14), calls=%async_computation.1 | async-start | bytes 262144 | tf_op jit(solution)/shard_map/all_to_all | solution.py:215
  64.8 3.9 %collective-permute-start.3 = (f32[128,1152]{1,0:T(8,128)S(1)}, f32[128,1152]{1,0:T(8,128)S(1)}, u32[]{:S(2)}, u32[]{:S(2)}) collective-permute-start(f32[128,1152]{1,0:T(8,128)S(1)} %get-tuple-element.17), channel_id=1, source_target_pairs={{0,4},{4,0},{1,5},{5,1},{2,6},{6,2},{3,7},{7,3},{8,12},{12,8},{9,1... | collective-permute-start | bytes 1769480 | tf_op jit(solution)/shard_map/ppermute | solution.py:227

commit v2 on v1

v2 whole, which is shorter than its diff:
```python
import math

import jax
import jax.numpy as jnp
from jax import lax
from jax.experimental import pallas as pl
from jax.experimental.pallas import tpu as pltpu
from jax.sharding import Mesh
from jax.sharding import PartitionSpec as P

C = 256
EPSILON = 1e-06
NY, NZ, NX = 4, 16, 4
P_DEV = 128
R_DEV = 16
A = 256
FREQS = 128
R_OWN = R_DEV // NY
WIDE = R_OWN * A
FULL = WIDE + 128
SHIFT_ROWS = 32
VMEM_LIMIT = 40 * 1024 * 1024


def spectral_table(length):
    half_len = length // 2
    angle_index = jnp.arange(length, dtype=jnp.int32)
    freq_index = jnp.arange(half_len, dtype=jnp.int32)
    turn_count = angle_index[:, None] * freq_index[None, :] % length
    radians = turn_count.astype(jnp.float32) * (2.0 * math.pi / length)
    norm_scale = 1.0 / math.sqrt(length)
    both = jnp.concatenate([jnp.cos(radians), -jnp.sin(radians)], 1) * norm_scale
    return both.astype(jnp.bfloat16)


def iota(shape, axis):
    return lax.broadcasted_iota(jnp.int32, shape, axis)


def deal_kernel(
    y_ref, images, label_row, rot_row, shift_row, out0, out1, out2, out3, grid
):
    y = y_ref[0]
    row, col = iota((A, A), 0), iota((A, A), 1)
    swap = (col == ((row & 15) * 16 + (row >> 4))).astype(jnp.float32).astype(jnp.bfloat16)
    for b in range(P_DEV // 16):
        x = jnp.dot(swap, images[b * A : b * A + A, :], preferred_element_type=jnp.float32)
        x = x.astype(jnp.bfloat16)
        for r in range(R_DEV):
            grid[r, b * 16 : b * 16 + 16, :] = x[r * 16 : r * 16 + 16]
    label = label_row[...]
    label = ((label >> 1) & 1) * 128 + (label >> 2) * 2 + (label & 1)
    at = iota((P_DEV, P_DEV), 0)
    tail = jnp.where(at == 0, label, jnp.where(at == 1, rot_row[...], shift_row[...]))
    tail = tail.astype(jnp.float32).astype(jnp.bfloat16)
    for d, out in enumerate((out0, out1, out2, out3)):
        first = ((y + d) & (NY - 1)) * R_OWN
        for i in range(R_OWN):
            out[:, i * A : i * A + A] = grid[first + i]
        out[:, WIDE:] = tail


def align_kernel(in0, in1, in2, in3, table, phases, out, parts):
    for r in range(R_OWN):
        phase = phases[r]
        for at, value in ((0, jnp.cos(phase)), (FREQS, jnp.sin(phase))):
            high = value.astype(jnp.bfloat16)
            low = (value - high.astype(jnp.float32)).astype(jnp.bfloat16)
            lanes = slice(r * A + at, r * A + at + FREQS)
            parts[0:SHIFT_ROWS, lanes] = high
            parts[SHIFT_ROWS : 2 * SHIFT_ROWS, lanes] = low
    dft = table[...]
    diagonal = iota((P_DEV, P_DEV), 0) == iota((P_DEV, P_DEV), 1)
    lane = iota((P_DEV, P_DEV), 1)
    for d, block in enumerate((in0, in1, in2, in3)):
        rows = slice(d * P_DEV, d * P_DEV + P_DEV)
        tail = block[0:16, WIDE:].astype(jnp.float32)
        rot = jnp.sum(jnp.where(diagonal, tail[1:2], 0.0), axis=1, keepdims=True)
        shift = jnp.sum(jnp.where(diagonal, tail[2:3], 0.0), axis=1, keepdims=True)
        angle = ((rot.astype(jnp.int32) * lane) & (A - 1)).astype(jnp.float32) * (2.0 * math.pi / A)
        cos_rot, sin_rot = jnp.cos(angle), jnp.sin(angle)
        pick = (lane[:, : 2 * SHIFT_ROWS] & (SHIFT_ROWS - 1)) == shift.astype(jnp.int32)
        pick = pick.astype(jnp.float32).astype(jnp.bfloat16)
        for i in range(R_OWN):
            lanes = slice(i * A, i * A + A)
            turn = jnp.dot(pick, parts[:, lanes], preferred_element_type=jnp.float32)
            spectra = jnp.dot(block[:, lanes], dft, preferred_element_type=jnp.float32)
            cosine = turn[:, :FREQS] * cos_rot - turn[:, FREQS:] * sin_rot
            sine = turn[:, FREQS:] * cos_rot + turn[:, :FREQS] * sin_rot
            real, imag = spectra[:, :FREQS], spectra[:, FREQS:]
            out[rows, i * A : i * A + FREQS] = (real * cosine - imag * sine).astype(jnp.bfloat16)
            out[rows, i * A + FREQS : i * A + A] = (real * sine + imag * cosine).astype(jnp.bfloat16)
        out[rows, WIDE:] = block[:, WIDE:]


def score_kernel(y_ref, rows, panel, out, stats):
    y = y_ref[0]
    refs = panel[:, :WIDE]
    wide = refs.astype(jnp.float32)
    norm = jnp.sum(wide * wide, axis=1, keepdims=True)
    sharp = panel[:, WIDE:].astype(jnp.float32)
    diagonal = iota((P_DEV, P_DEV), 0) == iota((P_DEV, P_DEV), 1)
    for d in range(NY):
        source = (y - d) & (NY - 1)
        flat = rows[d * P_DEV : d * P_DEV + P_DEV, :WIDE]
        label = rows[d * P_DEV : d * P_DEV + 16, WIDE:].astype(jnp.float32)[0:1].astype(jnp.int32)
        member = iota((C, P_DEV), 0) == label
        scores = lax.dot_general(
            refs, flat, (((1,), (1,)), ((), ())), preferred_element_type=jnp.float32
        )
        gram = lax.dot_general(
            flat, flat, (((1,), (1,)), ((), ())), preferred_element_type=jnp.float32
        )
        inner = jnp.sum(jnp.where(member, scores, 0.0), axis=0, keepdims=True)
        power = jnp.sum(jnp.where(diagonal, gram, 0.0), axis=0, keepdims=True)
        ref_power = jnp.sum(jnp.where(member, norm, 0.0), axis=0, keepdims=True)
        own_sharp = jnp.sum(jnp.where(member, sharp, 0.0), axis=0, keepdims=True)
        for at, value in enumerate((inner, power, ref_power, own_sharp)):
            stats[pl.ds(at * NY + source, 1), :] = value
    value = stats[...]
    for i in range(NX * NY * 2):
        out[i] = value


def sum_kernel(at_ref, got, own, other, out, weights):
    y, core = at_ref[0], at_ref[1]
    for c in range(2):
        total = got[c]
        for i in range(1, NX * NY):
            total = total + got[2 * i + c]
        inner, power, ref_power = total[0:NY], total[NY : 2 * NY], total[2 * NY : 3 * NY]
        sharp = got[c][3 * NY : 4 * NY]
        correlation = inner / jnp.sqrt((power + EPSILON) * (ref_power + EPSILON))
        weight = jax.nn.sigmoid(sharp * correlation)
        weights[c * NY : c * NY + NY, :] = weight.astype(jnp.bfloat16).astype(jnp.float32)
    spread = []
    for rows, side in ((own, core), (other, 1 - core)):
        parts = []
        for d in range(NY):
            source = (y - d) & (NY - 1)
            first = d * P_DEV
            label = rows[first : first + 16, WIDE:].astype(jnp.float32)[0:1].astype(jnp.int32)
            member = iota((P_DEV, P_DEV), 0) == (label ^ (core * 128))
            weight = weights[pl.ds(side * NY + source, 1), :]
            parts.append(jnp.where(member, weight, 0.0).astype(jnp.bfloat16))
        spread.append(jnp.concatenate(parts, axis=1))
    for i in range(R_OWN):
        lanes = slice(i * A, i * A + A)
        sums = jnp.dot(spread[0], own[:, lanes], preferred_element_type=jnp.float32)
        sums = sums + jnp.dot(spread[1], other[:, lanes], preferred_element_type=jnp.float32)
        out[:, lanes] = sums.astype(jnp.bfloat16)
    ones = jnp.ones((NY * P_DEV, P_DEV), jnp.bfloat16)
    sums = jnp.dot(spread[0], ones, preferred_element_type=jnp.float32)
    sums = sums + jnp.dot(spread[1], ones, preferred_element_type=jnp.float32)
    high = sums.astype(jnp.bfloat16).astype(jnp.float32)
    sums = jnp.where(iota((P_DEV, P_DEV), 1) < 64, high, sums - high)
    out[:, WIDE:] = sums.astype(jnp.bfloat16)


def call(kernel, name, outs, scratch, flops, nbytes, n_scalar, n_vector):
    vmem = pl.BlockSpec(memory_space=pltpu.VMEM)
    smem = pl.BlockSpec(memory_space=pltpu.SMEM)
    return pl.pallas_call(
        kernel,
        out_shape=outs,
        in_specs=[smem] * n_scalar + [vmem] * n_vector,
        out_specs=jax.tree.map(lambda _: vmem, outs),
        scratch_shapes=scratch,
        compiler_params=pltpu.CompilerParams(vmem_limit_bytes=VMEM_LIMIT),
        cost_estimate=pl.CostEstimate(flops=flops, bytes_accessed=nbytes, transcendentals=0),
        name=name,
    )


def body(images, references, sharpness, classes, rotations, shifts, shift_phase):
    y = lax.axis_index("y").astype(jnp.int32)
    core = lax.axis_index("core").astype(jnp.int32)
    shape = jax.ShapeDtypeStruct

    pieces = references.reshape(2, NY, WIDE).transpose(1, 0, 2)
    sharp_tile = jnp.broadcast_to(sharpness[None, :, None], (NY, 2, 128))
    pieces = jnp.concatenate([pieces, sharp_tile], axis=2)
    pieces = jnp.broadcast_to(pieces[:, None], (NY, NZ, 2, FULL)).reshape(NY * NZ, 2, FULL)
    panel = lax.all_to_all(pieces, ("y", "z"), split_axis=0, concat_axis=0, tiled=True)

    block = shape((P_DEV, FULL), jnp.bfloat16)
    dealt = call(
        deal_kernel,
        "deal",
        [block] * NY,
        [pltpu.VMEM((R_DEV, P_DEV, A), jnp.bfloat16)],
        300_000_000,
        3_000_000,
        1,
        4,
    )(
        y[None],
        images.reshape(P_DEV * R_DEV, A),
        classes.reshape(1, P_DEV),
        rotations.reshape(1, P_DEV),
        shifts.reshape(1, P_DEV),
    )
    blocks = [dealt[0]]
    for d in range(1, NY):
        blocks.append(lax.ppermute(dealt[d], "y", [(i, (i + d) % NY) for i in range(NY)]))
    phases = lax.dynamic_slice_in_dim(shift_phase, y * R_OWN, R_OWN, 1).transpose(1, 0, 2)
    phases = jnp.pad(phases, ((0, 0), (0, SHIFT_ROWS - 25), (0, 0)))
    rows = call(
        align_kernel,
        "align",
        shape((NY * P_DEV, FULL), jnp.bfloat16),
        [pltpu.VMEM((2 * SHIFT_ROWS, WIDE), jnp.bfloat16)],
        800_000_000,
        4_000_000,
        0,
        6,
    )(*blocks, spectral_table(A), phases)

    panel = lax.all_gather(panel.reshape(NY * NZ * 2, FULL), "core", axis=0, tiled=True)
    payload = call(
        score_kernel,
        "score",
        shape((NX * NY * 2, 4 * NY, P_DEV), jnp.float32),
        [pltpu.VMEM((4 * NY, P_DEV), jnp.float32)],
        600_000_000,
        2_000_000,
        1,
        2,
    )(y[None], rows, panel)
    got = lax.all_to_all(payload, ("x", "y", "core"), split_axis=0, concat_axis=0, tiled=True)
    other = lax.ppermute(rows, "core", [(0, 1), (1, 0)])
    sums = call(
        sum_kernel,
        "sum",
        shape((P_DEV, FULL), jnp.bfloat16),
        [pltpu.VMEM((2 * NY, P_DEV), jnp.float32)],
        300_000_000,
        3_000_000,
        1,
        3,
    )(jnp.stack([y, core]), got, rows, other)
    sums = lax.all_to_all(
        sums.reshape(NY * NZ, 2, FULL), ("y", "z"), split_axis=0, concat_axis=0, tiled=True
    )
    sums = jnp.sum(sums.reshape(NY, NZ, 2, FULL).astype(jnp.float32), axis=1)
    class_sums = sums[:, :, :WIDE].reshape(NY, 2, R_OWN, A).transpose(1, 0, 2, 3)
    class_weights = sums[0, :, WIDE] + sums[0, :, WIDE + 64]
    return class_sums.reshape(2, R_DEV, A), class_weights


def solution(mesh):
    whole = Mesh(mesh.devices.reshape(NY, NZ, 2, NX), ("y", "z", "core", "x"))
    dom = ("y", "z", "core")
    return jax.shard_map(
        body,
        mesh=whole,
        in_specs=(
            P(dom, "x", None),
            P(dom, "x", None),
            P(dom),
            P(dom, None),
            P(dom),
            P(dom),
            P(None, "x", None),
        ),
        out_specs=(P(dom, "x", None), P(dom)),
        check_vma=False,
    )
```

time: 107 us -> 110 us (1.028)
  local copies, waits for them, and re-layouts: 3.79 us -> 6.51 us
  Pallas kernels: 7.15 us -> 5.29 us
  waiting for transfers between devices: 17.2 us -> 18.4 us
    ppermute x4, waiting for transfers between devices: 5.37 us -> 11.2 us  [the longest x3 11.2 us: body(): lax.ppermute(dealt[d], 'y', [(i, (i + d) % NY) for i in range(NY)])]
    all_to_all x1, waiting for transfers between devices: 5.52 us -> 0.01 us  [body(): lax.all_to_all(pieces, ('y', 'z'), split_axis=0, concat_axis=0, tiled=True)]
    unnamed x13 -> x11, local copies, waits for them, and re-layouts: 0.81 us -> 3.2 us
    pallas_call x3 -> x4, Pallas kernels: 7.15 us -> 5.29 us  [the longest x1 1.98 us: body(): call(align_kernel, 'align', shape((NY * P_DEV, FULL), jnp.bfloat16), [plt...]
where the time goes in v2:
time: 110 us
  blocking collectives  39.3 us (36%)
  starting transfers between devices  37.8 us (34%)
  waiting for transfers between devices  18.4 us (17%)
  local copies, waits for them, and re-layouts  6.51 us (6%)
  Pallas kernels  5.29 us (5%)
  other arithmetic  1.58 us (1%)
    all_to_all x1, blocking collectives, body(): lax.all_to_all(sums.reshape(NY * NZ, 2, FULL), ('y', 'z'), split_axis=0,...  36.2 us
    all_to_all x1, starting transfers between devices, body(): lax.all_to_all(pieces, ('y', 'z'), split_axis=0, concat_axis=0, tiled=True)  18.7 us
    ppermute x3, waiting for transfers between devices, body(): lax.ppermute(dealt[d], 'y', [(i, (i + d) % NY) for i in range(NY)])  11.2 us
    ppermute x3, starting transfers between devices, body(): lax.ppermute(dealt[d], 'y', [(i, (i + d) % NY) for i in range(NY)])  10.6 us
    all_to_all x1, waiting for transfers between devices, body(): lax.all_to_all(payload, ('x', 'y', 'core'), split_axis=0, concat_axis=0,...  7.26 us
    all_to_all x1, starting transfers between devices, body(): lax.all_to_all(payload, ('x', 'y', 'core'), split_axis=0, concat_axis=0,...  6.56 us
    unnamed x11, local copies, waits for them, and re-layouts  3.2 us
    all_gather x1, blocking collectives, body(): lax.all_gather(panel.reshape(NY * NZ * 2, FULL), 'core', axis=0, tiled=True)  3.1 us
  transfers between devices with their start and end apart: 6, of which 4 were waited for; matrix products, arithmetic and copies ran while one was open for 1% of the time, Pallas kernels for 4%

profile of v2, /device:TPU:8, one launch (start us, length us, event | category | flops | bytes accessed | tf_op | source)
XLA Modules:
  0.0 109.8 jit_solution(9743974188759438798)
XLA Ops:
  0.6 0.0 copy-start
  0.6 0.8 reshape.44
  1.4 0.7 broadcast_in_dim.4
  2.2 0.9 broadcast_in_dim.5
  3.1 18.7 %all-to-all-start = ((bf16[64,2,1152]{2,1,0:T(2,128)(2,1)}), bf16[64,2,1152]{2,1,0:T(2,128)(2,1)S(1)}, u32[]{:S(2)}, u32[]{:S(2)}) async-start(bf16[64,2,1152]{2,1,0:T(2,128)(2,1)} %bitcast.8), calls=%async_computation | async-start | bytes 589824 | tf_op jit(solution)/shard_map/all_to_all | solution.py:184
  21.8 0.0 copy-start.1
  21.8 1.2 %copy-done.1 = bf16[128,16,256]{2,1,0:T(8,128)(2,1)S(1)} copy-done((bf16[128,16,256]{2,1,0:T(8,128)(2,1)S(1)}, bf16[128,16,256]{2,1,0:T(8,128)(2,1)}, u32[]{:S(2)}) %copy-start.1) | copy-done | bytes 1048600
  23.0 0.7 copy-done.2
  23.7 0.7 copy-done.3
  24.3 0.7 copy-done.4
  25.0 0.5 deal.1
  25.5 3.5 %collective-permute-start = (bf16[128,1152]{1,0:T(8,128)(2,1)S(1)}, bf16[128,1152]{1,0:T(8,128)(2,1)S(1)}, u32[]{:S(2)}, u32[]{:S(2)}) collective-permute-start(bf16[128,1152]{1,0:T(8,128)(2,1)S(1)} %get-tuple-element.7), channel_id=1, source_target_pairs={{0,128},{128,256},{256,384},{384,0},{1,129},{129,257},{257,385},{3... | collective-permute-start | bytes 884744 | tf_op jit(solution)/shard_map/ppermute | solution.py:205
  28.9 2.9 %collective-permute-start.1 = (bf16[128,1152]{1,0:T(8,128)(2,1)S(1)}, bf16[128,1152]{1,0:T(8,128)(2,1)S(1)}, u32[]{:S(2)}, u32[]{:S(2)}) collective-permute-start(bf16[128,1152]{1,0:T(8,128)(2,1)S(1)} %get-tuple-element.8), channel_id=1, source_target_pairs={{0,256},{128,384},{256,0},{384,128},{1,257},{129,385},{257,1},{385... | collective-permute-start | bytes 884744 | tf_op jit(solution)/shard_map/ppermute | solution.py:205
  31.8 4.3 %collective-permute-start.2 = (bf16[128,1152]{1,0:T(8,128)(2,1)S(1)}, bf16[128,1152]{1,0:T(8,128)(2,1)S(1)}, u32[]{:S(2)}, u32[]{:S(2)}) collective-permute-start(bf16[128,1152]{1,0:T(8,128)(2,1)S(1)} %get-tuple-element.9), channel_id=1, source_target_pairs={{0,384},{128,0},{256,128},{384,256},{1,385},{129,1},{257,129},{385... | collective-permute-start | bytes 884744 | tf_op jit(solution)/shard_map/ppermute | solution.py:205
  36.2 0.5 sine_negate_fusion
  36.8 2.3 %collective-permute-done.in1 = bf16[128,1152]{1,0:T(8,128)(2,1)S(1)} collective-permute-done((bf16[128,1152]{1,0:T(8,128)(2,1)S(1)}, bf16[128,1152]{1,0:T(8,128)(2,1)S(1)}, u32[]{:S(2)}, u32[]{:S(2)}) %collective-permute-start) | collective-permute-done | bytes 294944 | tf_op jit(solution)/shard_map/ppermute | solution.py:205
  39.0 4.2 %collective-permute-done.1.in2 = bf16[128,1152]{1,0:T(8,128)(2,1)S(1)} collective-permute-done((bf16[128,1152]{1,0:T(8,128)(2,1)S(1)}, bf16[128,1152]{1,0:T(8,128)(2,1)S(1)}, u32[]{:S(2)}, u32[]{:S(2)}) %collective-permute-start.1) | collective-permute-done | bytes 294944 | tf_op jit(solution)/shard_map/ppermute | solution.py:205
  43.2 4.7 %collective-permute-done.2.in3 = bf16[128,1152]{1,0:T(8,128)(2,1)S(1)} collective-permute-done((bf16[128,1152]{1,0:T(8,128)(2,1)S(1)}, bf16[128,1152]{1,0:T(8,128)(2,1)S(1)}, u32[]{:S(2)}, u32[]{:S(2)}) %collective-permute-start.2) | collective-permute-done | bytes 294944 | tf_op jit(solution)/shard_map/ppermute | solution.py:205
  47.9 2.0 %align.1.rows.own = bf16[512,1152]{1,0:T(8,128)(2,1)S(1)} custom-call(bf16[128,1152]{1,0:T(8,128)(2,1)S(1)} %get-tuple-element.6.in0, bf16[128,1152]{1,0:T(8,128)(2,1)S(1)} %collective-permute-done.in1, bf16[128,1152]{1,0:T(8,128)(2,1)S(1)} %collective-permute-done.1.in2, bf16[128,1152]{1,0:T(8,128)(2,1)S(1)} %collective-permute-done.2.in3, ...), custom_call_target="tpu_custom_call" | custom-call | flops 800000000 | bytes 4000000 | tf_op jit(solution)/shard_map/align/pallas_call | solution.py:208
  49.9 1.9 %collective-permute-start.3 = (bf16[512,1152]{1,0:T(8,128)(2,1)S(1)}, bf16[512,1152]{1,0:T(8,128)(2,1)S(1)}, u32[]{:S(2)}, u32[]{:S(2)}) collective-permute-start(bf16[512,1152]{1,0:T(8,128)(2,1)S(1)} %align.1.rows.own), channel_id=1, source_target_pairs={{0,4},{4,0},{1,5},{5,1},{2,6},{6,2},{3,7},{7,3},{8,12},{12,8},{9,1... | collective-permute-start | bytes 3538952 | tf_op jit(solution)/shard_map/ppermute | solution.py:231
  51.8 0.1 reshape.46
  52.0 3.1 %all_gather.3.panel = bf16[256,1152]{1,0:T(8,128)(2,1)S(1)} all-gather(bf16[128,1152]{1,0:T(8,128)(2,1)S(1)} %reshape.46), channel_id=1, replica_groups=mesh['y'=4,'z'=16,'core'=2,'x'=4] {'core'}, dimensions={0}, use_global_device_ids=true | all-gather | bytes 884736 | tf_op jit(solution)/shard_map/all_gather | solution.py:219
  55.1 1.7 %score.1 = f32[32,16,128]{2,1,0:T(8,128)} custom-call(s32[1]{0:T(128)} %bitcast.y_ref, bf16[512,1152]{1,0:T(8,128)(2,1)S(1)} %align.1.rows.own, bf16[256,1152]{1,0:T(8,128)(2,1)S(1)} %all_gather.3.panel), custom_call_target="tpu_custom_call" | custom-call | flops 600000000 | bytes 2000000 | tf_op jit(solution)/shard_map/score/pallas_call | solution.py:220
  56.8 6.6 %all-to-all-start.1 = ((f32[32,16,128]{2,1,0:T(8,128)}), f32[32,16,128]{2,1,0:T(8,128)S(1)}, u32[]{:S(2)}, u32[]{:S(2)}) async-start(f32[32,16,128]{2,1,0:T(8,128)} %score.1), calls=%async_computation.1 | async-start | bytes 524288 | tf_op jit(solution)/shard_map/all_to_all | solution.py:230
  63.4 0.1 pad_add_fusion.at_ref
  63.5 7.3 %all-to-all-done.1.got = f32[32,16,128]{2,1,0:T(8,128)S(1)} async-done(((f32[32,16,128]{2,1,0:T(8,128)}), f32[32,16,128]{2,1,0:T(8,128)S(1)}, u32[]{:S(2)}, u32[]{:S(2)}) %all-to-all-start.1) | async-done | bytes 262176 | tf_op jit(solution)/shard_map/all_to_all | solution.py:230
  70.7 1.1 %sum.1 = bf16[128,1152]{1,0:T(8,128)(2,1)S(1)} custom-call(s32[2]{0:T(128)S(1)} %pad_add_fusion.at_ref, f32[32,16,128]{2,1,0:T(8,128)S(1)} %all-to-all-done.1.got, bf16[512,1152]{1,0:T(8,128)(2,1)S(1)} %align.1.rows.own, bf16[512,1152]{1,0:T(8,128)(2,1)S(1)} %collective-permute-done.3.other), custom_call_target="tpu_custom_call" | custom-call | flops 300000000 | bytes 3000000 | tf_op jit(solution)/shard_map/sum/pallas_call | solution.py:232
  71.8 0.1 reshape.47
  72.0 36.2 %all_to_all.15 = bf16[64,2,1152]{2,1,0:T(2,128)(2,1)S(1)} all-to-all(bf16[64,2,1152]{2,1,0:T(2,128)(2,1)S(1)} %reshape.47), channel_id=1, replica_groups=mesh['y'=4,'z'=16,'core'=2,'x'=4] {'y','z'}, dimensions={0} | all-to-all | bytes 589824 | tf_op jit(solution)/shard_map/all_to_all | solution.py:242
  108.2 0.2 convert_reduce_fusion
  108.5 0.7 fusion.8
  109.2 0.6 reshape.49
  (15 shorter events, 0.1 us)
Async XLA Ops:
  0.6 35.5 %copy-start = (f32[25,16,128]{2,1,0:T(8,128)S(1)}, f32[25,16,128]{2,1,0:T(8,128)}, u32[]{:S(2)}) copy-start(f32[25,16,128]{2,1,0:T(8,128)} %param.13) | copy-start | bytes 614404
  3.1 48.8 %all-to-all-start = ((bf16[64,2,1152]{2,1,0:T(2,128)(2,1)}), bf16[64,2,1152]{2,1,0:T(2,128)(2,1)S(1)}, u32[]{:S(2)}, u32[]{:S(2)}) async-start(bf16[64,2,1152]{2,1,0:T(2,128)(2,1)} %bitcast.8), calls=%async_computation | async-start | bytes 589824 | tf_op jit(solution)/shard_map/all_to_all | solution.py:184
  21.8 1.2 %copy-start.1 = (bf16[128,16,256]{2,1,0:T(8,128)(2,1)S(1)}, bf16[128,16,256]{2,1,0:T(8,128)(2,1)}, u32[]{:S(2)}) copy-start(bf16[128,16,256]{2,1,0:T(8,128)(2,1)} %param.7) | copy-start | bytes 3145732
  23.0 0.7 copy-start.2
  23.7 0.7 copy-start.3
  24.3 0.7 copy-start.4
  25.5 13.6 %collective-permute-start = (bf16[128,1152]{1,0:T(8,128)(2,1)S(1)}, bf16[128,1152]{1,0:T(8,128)(2,1)S(1)}, u32[]{:S(2)}, u32[]{:S(2)}) collective-permute-start(bf16[128,1152]{1,0:T(8,128)(2,1)S(1)} %get-tuple-element.7), channel_id=1, source_target_pairs={{0,128},{128,256},{256,384},{384,0},{1,129},{129,257},{257,385},{3... | collective-permute-start | bytes 884744 | tf_op jit(solution)/shard_map/ppermute | solution.py:205
  28.9 14.3 %collective-permute-start.1 = (bf16[128,1152]{1,0:T(8,128)(2,1)S(1)}, bf16[128,1152]{1,0:T(8,128)(2,1)S(1)}, u32[]{:S(2)}, u32[]{:S(2)}) collective-permute-start(bf16[128,1152]{1,0:T(8,128)(2,1)S(1)} %get-tuple-element.8), channel_id=1, source_target_pairs={{0,256},{128,384},{256,0},{384,128},{1,257},{129,385},{257,1},{385... | collective-permute-start | bytes 884744 | tf_op jit(solution)/shard_map/ppermute | solution.py:205
  31.8 16.1 %collective-permute-start.2 = (bf16[128,1152]{1,0:T(8,128)(2,1)S(1)}, bf16[128,1152]{1,0:T(8,128)(2,1)S(1)}, u32[]{:S(2)}, u32[]{:S(2)}) collective-permute-start(bf16[128,1152]{1,0:T(8,128)(2,1)S(1)} %get-tuple-element.9), channel_id=1, source_target_pairs={{0,384},{128,0},{256,128},{384,256},{1,385},{129,1},{257,129},{385... | collective-permute-start | bytes 884744 | tf_op jit(solution)/shard_map/ppermute | solution.py:205
  49.9 20.8 %collective-permute-start.3 = (bf16[512,1152]{1,0:T(8,128)(2,1)S(1)}, bf16[512,1152]{1,0:T(8,128)(2,1)S(1)}, u32[]{:S(2)}, u32[]{:S(2)}) collective-permute-start(bf16[512,1152]{1,0:T(8,128)(2,1)S(1)} %align.1.rows.own), channel_id=1, source_target_pairs={{0,4},{4,0},{1,5},{5,1},{2,6},{6,2},{3,7},{7,3},{8,12},{12,8},{9,1... | collective-permute-start | bytes 3538952 | tf_op jit(solution)/shard_map/ppermute | solution.py:231
  56.8 13.9 %all-to-all-start.1 = ((f32[32,16,128]{2,1,0:T(8,128)}), f32[32,16,128]{2,1,0:T(8,128)S(1)}, u32[]{:S(2)}, u32[]{:S(2)}) async-start(f32[32,16,128]{2,1,0:T(8,128)} %score.1), calls=%async_computation.1 | async-start | bytes 524288 | tf_op jit(solution)/shard_map/all_to_all | solution.py:230

commit v3 on v2

--- a/solution.py
+++ b/solution.py
@@ -38,20 +38,71 @@
 
 
 def deal_kernel(
-    y_ref, images, label_row, rot_row, shift_row, out0, out1, out2, out3, grid
+    y_ref,
+    images_hbm,
+    refs_hbm,
+    label_hbm,
+    rot_hbm,
+    shift_hbm,
+    sharp,
+    pieces,
+    out0,
+    out1,
+    out2,
+    out3,
+    images,
+    refs,
+    ints,
+    row_of,
+    grid,
+    sems,
 ):
     y = y_ref[0]
+    copies = [
+        pltpu.make_async_copy(source, target, sems.at[at])
+        for at, (source, target) in enumerate(
+            (
+                (refs_hbm, refs),
+                (label_hbm, ints.at[pl.ds(0, 1)]),
+                (rot_hbm, ints.at[pl.ds(1, 1)]),
+                (shift_hbm, ints.at[pl.ds(2, 1)]),
+            )
+        )
+    ]
+    quarter = P_DEV * R_DEV // 4
+    for i in range(4):
+        rows = pl.ds(i * quarter, quarter)
+        copies.append(pltpu.make_async_copy(images_hbm.at[rows], images.at[rows], sems.at[4 + i]))
+    for copy in copies:
+        copy.start()
+    for copy in copies[:4]:
+        copy.wait()
+    odd = (iota((2 * NZ, FULL), 0) & 1) == 1
+    for j in range(2):
+        wide = refs[j].astype(jnp.float32)
+        for r in range(R_DEV):
+            at = r // R_OWN * 2 + j
+            lanes = slice(r % R_OWN * A, r % R_OWN * A + A)
+            row_of[at : at + 1, lanes] = wide[r : r + 1]
+        tile = jnp.broadcast_to(sharp[0:1, j : j + 1], (1, 128))
+        for r in range(NY):
+            row_of[2 * r + j : 2 * r + j + 1, WIDE:] = tile
+    for r in range(NY):
+        pair = jnp.where(odd, row_of[2 * r + 1 : 2 * r + 2, :], row_of[2 * r : 2 * r + 1, :])
+        pieces[r * 2 * NZ : (r + 1) * 2 * NZ, :] = pair.astype(jnp.bfloat16)
     row, col = iota((A, A), 0), iota((A, A), 1)
     swap = (col == ((row & 15) * 16 + (row >> 4))).astype(jnp.float32).astype(jnp.bfloat16)
     for b in range(P_DEV // 16):
+        if b % 2 == 0:
+            copies[4 + b // 2].wait()
         x = jnp.dot(swap, images[b * A : b * A + A, :], preferred_element_type=jnp.float32)
         x = x.astype(jnp.bfloat16)
         for r in range(R_DEV):
             grid[r, b * 16 : b * 16 + 16, :] = x[r * 16 : r * 16 + 16]
-    label = label_row[...]
+    label = ints[0:1, :]
     label = ((label >> 1) & 1) * 128 + (label >> 2) * 2 + (label & 1)
     at = iota((P_DEV, P_DEV), 0)
-    tail = jnp.where(at == 0, label, jnp.where(at == 1, rot_row[...], shift_row[...]))
+    tail = jnp.where(at == 0, label, jnp.where(at == 1, ints[1:2, :], ints[2:3, :]))
     tail = tail.astype(jnp.float32).astype(jnp.bfloat16)
     for d, out in enumerate((out0, out1, out2, out3)):
         first = ((y + d) & (NY - 1)) * R_OWN
@@ -115,7 +166,7 @@
         power = jnp.sum(jnp.where(diagonal, gram, 0.0), axis=0, keepdims=True)
         ref_power = jnp.sum(jnp.where(member, norm, 0.0), axis=0, keepdims=True)
         own_sharp = jnp.sum(jnp.where(member, sharp, 0.0), axis=0, keepdims=True)
-        for at, value in enumerate((inner, power, ref_power, own_sharp)):
+        for at, value in enumerate((own_sharp * inner, power, ref_power)):
             stats[pl.ds(at * NY + source, 1), :] = value
     value = stats[...]
     for i in range(NX * NY * 2):
@@ -129,9 +180,7 @@
         for i in range(1, NX * NY):
             total = total + got[2 * i + c]
         inner, power, ref_power = total[0:NY], total[NY : 2 * NY], total[2 * NY : 3 * NY]
-        sharp = got[c][3 * NY : 4 * NY]
-        correlation = inner / jnp.sqrt((power + EPSILON) * (ref_power + EPSILON))
-        weight = jax.nn.sigmoid(sharp * correlation)
+        weight = jax.nn.sigmoid(inner / jnp.sqrt((power + EPSILON) * (ref_power + EPSILON)))
         weights[c * NY : c * NY + NY, :] = weight.astype(jnp.bfloat16).astype(jnp.float32)
     spread = []
     for rows, side in ((own, core), (other, 1 - core)):
@@ -157,14 +206,29 @@
     out[:, WIDE:] = sums.astype(jnp.bfloat16)
 
 
-def call(kernel, name, outs, scratch, flops, nbytes, n_scalar, n_vector):
-    vmem = pl.BlockSpec(memory_space=pltpu.VMEM)
-    smem = pl.BlockSpec(memory_space=pltpu.SMEM)
+def finish_kernel(got, out, out_weights):
+    odd = (iota((2 * NZ, FULL), 0) & 1) == 1
+    for r in range(NY):
+        part = got[r * 2 * NZ : (r + 1) * 2 * NZ, :].astype(jnp.float32)
+        for j in range(2):
+            total = jnp.sum(jnp.where(odd == (j == 1), part, 0.0), axis=0, keepdims=True)
+            for i in range(R_OWN):
+                out[j, r * R_OWN + i : r * R_OWN + i + 1, :] = total[:, i * A : i * A + A]
+            if r == 0:
+                out_weights[j] = jnp.sum(total[:, WIDE:]) * (1.0 / 64.0)
+
+
+VMEM = pl.BlockSpec(memory_space=pltpu.VMEM)
+SMEM = pl.BlockSpec(memory_space=pltpu.SMEM)
+HBM = pl.BlockSpec(memory_space=pltpu.HBM)
+
+
+def call(kernel, name, outs, scratch, flops, nbytes, in_specs, out_specs):
     return pl.pallas_call(
         kernel,
         out_shape=outs,
-        in_specs=[smem] * n_scalar + [vmem] * n_vector,
-        out_specs=jax.tree.map(lambda _: vmem, outs),
+        in_specs=in_specs,
+        out_specs=out_specs,
         scratch_shapes=scratch,
         compiler_params=pltpu.CompilerParams(vmem_limit_bytes=VMEM_LIMIT),
         cost_estimate=pl.CostEstimate(flops=flops, bytes_accessed=nbytes, transcendentals=0),
@@ -177,28 +241,39 @@
     core = lax.axis_index("core").astype(jnp.int32)
     shape = jax.ShapeDtypeStruct
 
-    pieces = references.reshape(2, NY, WIDE).transpose(1, 0, 2)
-    sharp_tile = jnp.broadcast_to(sharpness[None, :, None], (NY, 2, 128))
-    pieces = jnp.concatenate([pieces, sharp_tile], axis=2)
-    pieces = jnp.broadcast_to(pieces[:, None], (NY, NZ, 2, FULL)).reshape(NY * NZ, 2, FULL)
-    panel = lax.all_to_all(pieces, ("y", "z"), split_axis=0, concat_axis=0, tiled=True)
-
     block = shape((P_DEV, FULL), jnp.bfloat16)
-    dealt = call(
+    pieces, *dealt = call(
         deal_kernel,
         "deal",
-        [block] * NY,
-        [pltpu.VMEM((R_DEV, P_DEV, A), jnp.bfloat16)],
+        [block] * (1 + NY),
+        [
+            pltpu.VMEM((P_DEV * R_DEV, A), jnp.bfloat16),
+            pltpu.VMEM((2, R_DEV, A), jnp.bfloat16),
+            pltpu.VMEM((8, P_DEV), jnp.int32),
+            pltpu.VMEM((2 * NY, FULL), jnp.float32),
+            pltpu.VMEM((R_DEV, P_DEV, A), jnp.bfloat16),
+            pltpu.SemaphoreType.DMA((8,)),
+        ],
         300_000_000,
         3_000_000,
-        1,
-        4,
+        [SMEM] + [HBM] * 5 + [VMEM],
+        [VMEM] * (1 + NY),
     )(
         y[None],
-        images.reshape(P_DEV * R_DEV, A),
-        classes.reshape(1, P_DEV),
-        rotations.reshape(1, P_DEV),
-        shifts.reshape(1, P_DEV),
+        *[
+            pltpu.with_memory_space_constraint(x, pltpu.HBM)
+            for x in (
+                images.reshape(P_DEV * R_DEV, A),
+                references,
+                classes.reshape(1, P_DEV),
+                rotations.reshape(1, P_DEV),
+                shifts.reshape(1, P_DEV),
+            )
+        ],
+        sharpness.astype(jnp.float32).reshape(1, 2),
+    )
+    panel = lax.all_to_all(
+        pieces.reshape(NY * NZ, 2, FULL), ("y", "z"), split_axis=0, concat_axis=0, tiled=True
     )
     blocks = [dealt[0]]
     for d in range(1, NY):
@@ -212,21 +287,22 @@
         [pltpu.VMEM((2 * SHIFT_ROWS, WIDE), jnp.bfloat16)],
         800_000_000,
         4_000_000,
-        0,
-        6,
+        [VMEM] * 6,
+        VMEM,
     )(*blocks, spectral_table(A), phases)
 
     panel = lax.all_gather(panel.reshape(NY * NZ * 2, FULL), "core", axis=0, tiled=True)
     payload = call(
         score_kernel,
         "score",
-        shape((NX * NY * 2, 4 * NY, P_DEV), jnp.float32),
-        [pltpu.VMEM((4 * NY, P_DEV), jnp.float32)],
+        shape((NX * NY * 2, 3 * NY, P_DEV), jnp.float32),
+        [pltpu.VMEM((3 * NY, P_DEV), jnp.float32)],
         600_000_000,
         2_000_000,
-        1,
-        2,
+        [SMEM] + [VMEM] * 2,
+        VMEM,
     )(y[None], rows, panel)
+    rows, payload = lax.optimization_barrier((rows, payload))
     got = lax.all_to_all(payload, ("x", "y", "core"), split_axis=0, concat_axis=0, tiled=True)
     other = lax.ppermute(rows, "core", [(0, 1), (1, 0)])
     sums = call(
@@ -236,16 +312,23 @@
         [pltpu.VMEM((2 * NY, P_DEV), jnp.float32)],
         300_000_000,
         3_000_000,
-        1,
-        3,
+        [SMEM] + [VMEM] * 3,
+        VMEM,
     )(jnp.stack([y, core]), got, rows, other)
     sums = lax.all_to_all(
         sums.reshape(NY * NZ, 2, FULL), ("y", "z"), split_axis=0, concat_axis=0, tiled=True
     )
-    sums = jnp.sum(sums.reshape(NY, NZ, 2, FULL).astype(jnp.float32), axis=1)
-    class_sums = sums[:, :, :WIDE].reshape(NY, 2, R_OWN, A).transpose(1, 0, 2, 3)
-    class_weights = sums[0, :, WIDE] + sums[0, :, WIDE + 64]
-    return class_sums.reshape(2, R_DEV, A), class_weights
+    class_sums, class_weights = call(
+        finish_kernel,
+        "finish",
+        [shape((2, R_DEV, A), jnp.float32), shape((2,), jnp.float32)],
+        [],
+        1_000_000,
+        400_000,
+        [VMEM],
+        [VMEM, SMEM],
+    )(sums.reshape(NY * NZ * 2, FULL))
+    return class_sums, class_weights
 
 
 def solution(mesh):

time: 110 us -> 108 us (0.982)
  local copies, waits for them, and re-layouts: 6.51 us -> 1.2 us
  Pallas kernels: 5.29 us -> 7.68 us
    unnamed x11 -> x3, local copies, waits for them, and re-layouts: 3.2 us -> 0.02 us
    pallas_call x2 -> x3, Pallas kernels: 2.2 us -> 4.58 us  [the longest x1 2.03 us: body(): call(deal_kernel, 'deal', [block] * (1 + NY), [pltpu.VMEM((P_DEV * R_DEV,...]
    broadcast_in_dim x2 -> x0, local copies, waits for them, and re-layouts: 1.6 us -> none  [the longest x1 0.87 us: body(): jnp.broadcast_to(pieces[:, None], (NY, NZ, 2, FULL))]
  transfers between devices with their start and end apart: 6 -> 6, of which waited for: 4 -> 4; matrix products, arithmetic and copies ran while one was open for 1% -> 1% of each run, Pallas kernels for 4% -> 2%
where the time goes in v3:
time: 108 us; the launch traced here: 107 us
  blocking collectives  38.9 us (36%)
  starting transfers between devices  38 us (35%)
  waiting for transfers between devices  19.3 us (18%)
  Pallas kernels  7.68 us (7%)
  other arithmetic  1.32 us (1%)
  local copies, waits for them, and re-layouts  1.2 us (1%)
    all_to_all x1, blocking collectives, body(): lax.all_to_all(sums.reshape(NY * NZ, 2, FULL), ('y', 'z'), split_axis=0,...  36.7 us
    all_to_all x1, starting transfers between devices, body(): lax.all_to_all(pieces.reshape(NY * NZ, 2, FULL), ('y', 'z'), split_axis=0...  18.7 us
    ppermute x3, waiting for transfers between devices, body(): lax.ppermute(dealt[d], 'y', [(i, (i + d) % NY) for i in range(NY)])  12 us
    ppermute x3, starting transfers between devices, body(): lax.ppermute(dealt[d], 'y', [(i, (i + d) % NY) for i in range(NY)])  10.6 us
    all_to_all x1, waiting for transfers between devices, body(): lax.all_to_all(payload, ('x', 'y', 'core'), split_axis=0, concat_axis=0,...  7.26 us
    all_to_all x1, starting transfers between devices, body(): lax.all_to_all(payload, ('x', 'y', 'core'), split_axis=0, concat_axis=0,...  6.6 us
    all_gather x1, blocking collectives, body(): lax.all_gather(panel.reshape(NY * NZ * 2, FULL), 'core', axis=0, tiled=True)  2.23 us
  transfers between devices with their start and end apart: 6, of which 4 were waited for; matrix products, arithmetic and copies ran while one was open for 1% of the time, Pallas kernels for 2%

profile of v3, /device:TPU:8, one launch (start us, length us, event | category | flops | bytes accessed | tf_op | source)
XLA Modules:
  0.0 107.2 jit_solution(15790325202128716498)
XLA Ops:
  0.6 0.0 copy-start
  0.7 0.7 bitcast_convert_fusion.sharp
  1.3 2.0 %deal.1 = (bf16[128,1152]{1,0:T(8,128)(2,1)S(1)}, bf16[128,1152]{1,0:T(8,128)(2,1)S(1)}, bf16[128,1152]{1,0:T(8,128)(2,1)S(1)}, bf16[128,1152]{1,0:T(8,128)(2,1)S(1)}, bf16[128,1152]{1,0:T(8,128)(2,1)S(1)}) custom-call(s32[1]{0:T(128)} %bitcast.y_ref, bf16[2048,256]{1,0:T(8,128)(2,1)} %bitcast.13, bf16[2,16,256]{2,1,0:T(8,128)(2,1)} %refs_hbm.1, ...), custom_call_target="tpu_custom_call" | custom-call | flops 300000000 | bytes 3000000 | tf_op jit(solution)/shard_map/deal/pallas_call | solution.py:245
  3.4 0.8 reshape.39
  4.2 18.7 %all-to-all-start = ((bf16[64,2,1152]{2,1,0:T(2,128)(2,1)}), bf16[64,2,1152]{2,1,0:T(2,128)(2,1)S(1)}, u32[]{:S(2)}, u32[]{:S(2)}) async-start(bf16[64,2,1152]{2,1,0:T(2,128)(2,1)} %reshape.39), calls=%async_computation | async-start | bytes 589824 | tf_op jit(solution)/shard_map/all_to_all | solution.py:275
  22.9 3.5 %collective-permute-start = (bf16[128,1152]{1,0:T(8,128)(2,1)S(1)}, bf16[128,1152]{1,0:T(8,128)(2,1)S(1)}, u32[]{:S(2)}, u32[]{:S(2)}) collective-permute-start(bf16[128,1152]{1,0:T(8,128)(2,1)S(1)} %get-tuple-element.10), channel_id=1, source_target_pairs={{0,128},{128,256},{256,384},{384,0},{1,129},{129,257},{257,385},{3... | collective-permute-start | bytes 884744 | tf_op jit(solution)/shard_map/ppermute | solution.py:280
  26.4 2.9 %collective-permute-start.1 = (bf16[128,1152]{1,0:T(8,128)(2,1)S(1)}, bf16[128,1152]{1,0:T(8,128)(2,1)S(1)}, u32[]{:S(2)}, u32[]{:S(2)}) collective-permute-start(bf16[128,1152]{1,0:T(8,128)(2,1)S(1)} %get-tuple-element.11), channel_id=1, source_target_pairs={{0,256},{128,384},{256,0},{384,128},{1,257},{129,385},{257,1},{385... | collective-permute-start | bytes 884744 | tf_op jit(solution)/shard_map/ppermute | solution.py:280
  29.3 4.3 %collective-permute-start.2 = (bf16[128,1152]{1,0:T(8,128)(2,1)S(1)}, bf16[128,1152]{1,0:T(8,128)(2,1)S(1)}, u32[]{:S(2)}, u32[]{:S(2)}) collective-permute-start(bf16[128,1152]{1,0:T(8,128)(2,1)S(1)} %get-tuple-element.12), channel_id=1, source_target_pairs={{0,384},{128,0},{256,128},{384,256},{1,385},{129,1},{257,129},{385... | collective-permute-start | bytes 884744 | tf_op jit(solution)/shard_map/ppermute | solution.py:280
  33.6 0.0 copy-done
  33.7 0.5 sine_negate_fusion
  34.2 2.7 %collective-permute-done.in1 = bf16[128,1152]{1,0:T(8,128)(2,1)S(1)} collective-permute-done((bf16[128,1152]{1,0:T(8,128)(2,1)S(1)}, bf16[128,1152]{1,0:T(8,128)(2,1)S(1)}, u32[]{:S(2)}, u32[]{:S(2)}) %collective-permute-start) | collective-permute-done | bytes 294944 | tf_op jit(solution)/shard_map/ppermute | solution.py:280
  36.9 4.6 %collective-permute-done.1.in2 = bf16[128,1152]{1,0:T(8,128)(2,1)S(1)} collective-permute-done((bf16[128,1152]{1,0:T(8,128)(2,1)S(1)}, bf16[128,1152]{1,0:T(8,128)(2,1)S(1)}, u32[]{:S(2)}, u32[]{:S(2)}) %collective-permute-start.1) | collective-permute-done | bytes 294944 | tf_op jit(solution)/shard_map/ppermute | solution.py:280
  41.5 4.7 %collective-permute-done.2.in3 = bf16[128,1152]{1,0:T(8,128)(2,1)S(1)} collective-permute-done((bf16[128,1152]{1,0:T(8,128)(2,1)S(1)}, bf16[128,1152]{1,0:T(8,128)(2,1)S(1)}, u32[]{:S(2)}, u32[]{:S(2)}) %collective-permute-start.2) | collective-permute-done | bytes 294944 | tf_op jit(solution)/shard_map/ppermute | solution.py:280
  46.3 2.0 %align.1.rows.own = bf16[512,1152]{1,0:T(8,128)(2,1)S(1)} custom-call(bf16[128,1152]{1,0:T(8,128)(2,1)S(1)} %get-tuple-element.9.in0, bf16[128,1152]{1,0:T(8,128)(2,1)S(1)} %collective-permute-done.in1, bf16[128,1152]{1,0:T(8,128)(2,1)S(1)} %collective-permute-done.1.in2, bf16[128,1152]{1,0:T(8,128)(2,1)S(1)} %collective-permute-done.2.in3, ...), custom_call_target="tpu_custom_call" | custom-call | flops 800000000 | bytes 4000000 | tf_op jit(solution)/shard_map/align/pallas_call | solution.py:283
  48.2 0.0 all-to-all-done
  48.3 0.1 reshape.40
  48.4 2.2 %all_gather.3.panel = bf16[256,1152]{1,0:T(8,128)(2,1)S(1)} all-gather(bf16[128,1152]{1,0:T(8,128)(2,1)S(1)} %reshape.40), channel_id=1, replica_groups=mesh['y'=4,'z'=16,'core'=2,'x'=4] {'core'}, dimensions={0}, use_global_device_ids=true | all-gather | bytes 884736 | tf_op jit(solution)/shard_map/all_gather | solution.py:294
  50.6 1.8 %score.1 = f32[32,12,128]{2,1,0:T(8,128)} custom-call(s32[1]{0:T(128)} %bitcast.y_ref, bf16[512,1152]{1,0:T(8,128)(2,1)S(1)} %align.1.rows.own, bf16[256,1152]{1,0:T(8,128)(2,1)S(1)} %all_gather.3.panel), custom_call_target="tpu_custom_call" | custom-call | flops 600000000 | bytes 2000000 | tf_op jit(solution)/shard_map/score/pallas_call | solution.py:295
  52.4 2.0 %collective-permute-start.3 = (bf16[512,1152]{1,0:T(8,128)(2,1)S(1)}, bf16[512,1152]{1,0:T(8,128)(2,1)S(1)}, u32[]{:S(2)}, u32[]{:S(2)}) collective-permute-start(bf16[512,1152]{1,0:T(8,128)(2,1)S(1)} %align.1.rows.own), channel_id=1, source_target_pairs={{0,4},{4,0},{1,5},{5,1},{2,6},{6,2},{3,7},{7,3},{8,12},{12,8},{9,1... | collective-permute-start | bytes 3538952 | tf_op jit(solution)/shard_map/ppermute | solution.py:307
  54.4 6.6 %all-to-all-start.1 = ((f32[32,12,128]{2,1,0:T(8,128)}), f32[32,12,128]{2,1,0:T(8,128)S(1)}, u32[]{:S(2)}, u32[]{:S(2)}) async-start(f32[32,12,128]{2,1,0:T(8,128)} %score.1), calls=%async_computation.1 | async-start | bytes 524288 | tf_op jit(solution)/shard_map/all_to_all | solution.py:306
  61.0 0.1 pad_add_fusion.at_ref
  61.1 7.3 %all-to-all-done.1.got = f32[32,12,128]{2,1,0:T(8,128)S(1)} async-done(((f32[32,12,128]{2,1,0:T(8,128)}), f32[32,12,128]{2,1,0:T(8,128)S(1)}, u32[]{:S(2)}, u32[]{:S(2)}) %all-to-all-start.1) | async-done | bytes 196640 | tf_op jit(solution)/shard_map/all_to_all | solution.py:306
  68.3 0.0 collective-permute-done.3.other
  68.3 1.1 %sum.1 = bf16[128,1152]{1,0:T(8,128)(2,1)S(1)} custom-call(s32[2]{0:T(128)S(1)} %pad_add_fusion.at_ref, f32[32,12,128]{2,1,0:T(8,128)S(1)} %all-to-all-done.1.got, bf16[512,1152]{1,0:T(8,128)(2,1)S(1)} %align.1.rows.own, bf16[512,1152]{1,0:T(8,128)(2,1)S(1)} %collective-permute-done.3.other), custom_call_target="tpu_custom_call" | custom-call | flops 300000000 | bytes 3000000 | tf_op jit(solution)/shard_map/sum/pallas_call | solution.py:308
  69.5 0.1 reshape.41
  69.6 36.7 %all_to_all.15 = bf16[64,2,1152]{2,1,0:T(2,128)(2,1)S(1)} all-to-all(bf16[64,2,1152]{2,1,0:T(2,128)(2,1)S(1)} %reshape.41), channel_id=1, replica_groups=mesh['y'=4,'z'=16,'core'=2,'x'=4] {'y','z'}, dimensions={0} | all-to-all | bytes 589824 | tf_op jit(solution)/shard_map/all_to_all | solution.py:318
  106.2 0.1 reshape.42.got
  106.4 0.8 finish.1
  (4 shorter events, 0.1 us)
Async XLA Ops:
  0.6 33.0 %copy-start = (f32[25,16,128]{2,1,0:T(8,128)S(1)}, f32[25,16,128]{2,1,0:T(8,128)}, u32[]{:S(2)}) copy-start(f32[25,16,128]{2,1,0:T(8,128)} %param.13) | copy-start | bytes 614404
  4.2 44.0 %all-to-all-start = ((bf16[64,2,1152]{2,1,0:T(2,128)(2,1)}), bf16[64,2,1152]{2,1,0:T(2,128)(2,1)S(1)}, u32[]{:S(2)}, u32[]{:S(2)}) async-start(bf16[64,2,1152]{2,1,0:T(2,128)(2,1)} %reshape.39), calls=%async_computation | async-start | bytes 589824 | tf_op jit(solution)/shard_map/all_to_all | solution.py:275
  22.9 14.0 %collective-permute-start = (bf16[128,1152]{1,0:T(8,128)(2,1)S(1)}, bf16[128,1152]{1,0:T(8,128)(2,1)S(1)}, u32[]{:S(2)}, u32[]{:S(2)}) collective-permute-start(bf16[128,1152]{1,0:T(8,128)(2,1)S(1)} %get-tuple-element.10), channel_id=1, source_target_pairs={{0,128},{128,256},{256,384},{384,0},{1,129},{129,257},{257,385},{3... | collective-permute-start | bytes 884744 | tf_op jit(solution)/shard_map/ppermute | solution.py:280
  26.4 15.1 %collective-permute-start.1 = (bf16[128,1152]{1,0:T(8,128)(2,1)S(1)}, bf16[128,1152]{1,0:T(8,128)(2,1)S(1)}, u32[]{:S(2)}, u32[]{:S(2)}) collective-permute-start(bf16[128,1152]{1,0:T(8,128)(2,1)S(1)} %get-tuple-element.11), channel_id=1, source_target_pairs={{0,256},{128,384},{256,0},{384,128},{1,257},{129,385},{257,1},{385... | collective-permute-start | bytes 884744 | tf_op jit(solution)/shard_map/ppermute | solution.py:280
  29.3 17.0 %collective-permute-start.2 = (bf16[128,1152]{1,0:T(8,128)(2,1)S(1)}, bf16[128,1152]{1,0:T(8,128)(2,1)S(1)}, u32[]{:S(2)}, u32[]{:S(2)}) collective-permute-start(bf16[128,1152]{1,0:T(8,128)(2,1)S(1)} %get-tuple-element.12), channel_id=1, source_target_pairs={{0,384},{128,0},{256,128},{384,256},{1,385},{129,1},{257,129},{385... | collective-permute-start | bytes 884744 | tf_op jit(solution)/shard_map/ppermute | solution.py:280
  52.4 16.0 %collective-permute-start.3 = (bf16[512,1152]{1,0:T(8,128)(2,1)S(1)}, bf16[512,1152]{1,0:T(8,128)(2,1)S(1)}, u32[]{:S(2)}, u32[]{:S(2)}) collective-permute-start(bf16[512,1152]{1,0:T(8,128)(2,1)S(1)} %align.1.rows.own), channel_id=1, source_target_pairs={{0,4},{4,0},{1,5},{5,1},{2,6},{6,2},{3,7},{7,3},{8,12},{12,8},{9,1... | collective-permute-start | bytes 3538952 | tf_op jit(solution)/shard_map/ppermute | solution.py:307
  54.4 13.9 %all-to-all-start.1 = ((f32[32,12,128]{2,1,0:T(8,128)}), f32[32,12,128]{2,1,0:T(8,128)S(1)}, u32[]{:S(2)}, u32[]{:S(2)}) async-start(f32[32,12,128]{2,1,0:T(8,128)} %score.1), calls=%async_computation.1 | async-start | bytes 524288 | tf_op jit(solution)/shard_map/all_to_all | solution.py:306

commit v4 on v3

--- a/solution.py
+++ b/solution.py
@@ -77,19 +77,19 @@
         copy.start()
     for copy in copies[:4]:
         copy.wait()
-    odd = (iota((2 * NZ, FULL), 0) & 1) == 1
     for j in range(2):
         wide = refs[j].astype(jnp.float32)
         for r in range(R_DEV):
             at = r // R_OWN * 2 + j
             lanes = slice(r % R_OWN * A, r % R_OWN * A + A)
             row_of[at : at + 1, lanes] = wide[r : r + 1]
+            row_of[at + 8 : at + 9, lanes] = wide[r : r + 1]
         tile = jnp.broadcast_to(sharp[0:1, j : j + 1], (1, 128))
-        for r in range(NY):
-            row_of[2 * r + j : 2 * r + j + 1, WIDE:] = tile
-    for r in range(NY):
-        pair = jnp.where(odd, row_of[2 * r + 1 : 2 * r + 2, :], row_of[2 * r : 2 * r + 1, :])
-        pieces[r * 2 * NZ : (r + 1) * 2 * NZ, :] = pair.astype(jnp.bfloat16)
+        for at in range(j, 4 * NY, 2):
+            row_of[at : at + 1, WIDE:] = tile
+    pair = row_of[...].astype(jnp.bfloat16)
+    for z in range(0, NZ, 2):
+        pieces[z * 8 : z * 8 + 16, :] = pair
     row, col = iota((A, A), 0), iota((A, A), 1)
     swap = (col == ((row & 15) * 16 + (row >> 4))).astype(jnp.float32).astype(jnp.bfloat16)
     for b in range(P_DEV // 16):
@@ -221,6 +221,7 @@
 VMEM = pl.BlockSpec(memory_space=pltpu.VMEM)
 SMEM = pl.BlockSpec(memory_space=pltpu.SMEM)
 HBM = pl.BlockSpec(memory_space=pltpu.HBM)
+ANY = pl.BlockSpec(memory_space=pl.ANY)
 
 
 def call(kernel, name, outs, scratch, flops, nbytes, in_specs, out_specs):
@@ -250,7 +251,7 @@
             pltpu.VMEM((P_DEV * R_DEV, A), jnp.bfloat16),
             pltpu.VMEM((2, R_DEV, A), jnp.bfloat16),
             pltpu.VMEM((8, P_DEV), jnp.int32),
-            pltpu.VMEM((2 * NY, FULL), jnp.float32),
+            pltpu.VMEM((4 * NY, FULL), jnp.float32),
             pltpu.VMEM((R_DEV, P_DEV, A), jnp.bfloat16),
             pltpu.SemaphoreType.DMA((8,)),
         ],
@@ -273,8 +274,10 @@
         sharpness.astype(jnp.float32).reshape(1, 2),
     )
     panel = lax.all_to_all(
-        pieces.reshape(NY * NZ, 2, FULL), ("y", "z"), split_axis=0, concat_axis=0, tiled=True
-    )
+        pieces.reshape(NZ, 2 * NY, FULL), "z", split_axis=0, concat_axis=0, tiled=True
+    )
+    panel = panel.reshape(NZ, NY, 2, FULL).transpose(1, 0, 2, 3).reshape(NY, 2 * NZ, FULL)
+    panel = lax.all_to_all(panel, "y", split_axis=0, concat_axis=0, tiled=True)
     blocks = [dealt[0]]
     for d in range(1, NY):
         blocks.append(lax.ppermute(dealt[d], "y", [(i, (i + d) % NY) for i in range(NY)]))
@@ -302,7 +305,17 @@
         [SMEM] + [VMEM] * 2,
         VMEM,
     )(y[None], rows, panel)
-    rows, payload = lax.optimization_barrier((rows, payload))
+    rows = pl.pallas_call(
+        lambda rows, payload, out: None,
+        out_shape=shape(rows.shape, rows.dtype),
+        in_specs=[ANY, ANY],
+        out_specs=ANY,
+        input_output_aliases={0: 0},
+        cost_estimate=pl.CostEstimate(
+            flops=20_000_000_000, bytes_accessed=2_000_000, transcendentals=0
+        ),
+        name="hold",
+    )(rows, payload)
     got = lax.all_to_all(payload, ("x", "y", "core"), split_axis=0, concat_axis=0, tiled=True)
     other = lax.ppermute(rows, "core", [(0, 1), (1, 0)])
     sums = call(

time: 108 us -> 106 us (0.981)
  blocking collectives: 38.9 us -> 34 us
  local copies, waits for them, and re-layouts: 1.2 us -> 3.36 us
  starting transfers between devices: 38 us -> 39.3 us
    ppermute x3, waiting for transfers between devices: 12 us -> 0.01 us  [body(): lax.ppermute(dealt[d], 'y', [(i, (i + d) % NY) for i in range(NY)])]
    all_to_all x1 -> x2, waiting for transfers between devices: 0.01 us -> 11.3 us  [the longest x1 8.08 us: body(): lax.all_to_all(pieces.reshape(NZ, 2 * NY, FULL), 'z', split_axis=0, conca...]
    all_to_all x1, blocking collectives: 36.7 us -> 31.8 us  [body(): lax.all_to_all(sums.reshape(NY * NZ, 2, FULL), ('y', 'z'), split_axis=0,...]
    unnamed x3 -> x9, local copies, waits for them, and re-layouts: 0.02 us -> 1.98 us
    all_to_all x1 -> x2, starting transfers between devices: 18.7 us -> 20.1 us  [the longest x1 15.2 us: body(): lax.all_to_all(pieces.reshape(NZ, 2 * NY, FULL), 'z', split_axis=0, conca...]
  transfers between devices with their start and end apart: 6 -> 7, of which waited for: 4 -> 3; matrix products, arithmetic and copies ran while one was open for 1% -> 2% of each run, Pallas kernels for 2% -> 2%
where the time goes in v4:
time: 106 us; the launch traced here: 105 us
  starting transfers between devices  39.3 us (37%)
  blocking collectives  34 us (32%)
  waiting for transfers between devices  18.6 us (18%)
  Pallas kernels  7.45 us (7%)
  local copies, waits for them, and re-layouts  3.36 us (3%)
  other arithmetic  1.32 us (1%)
    all_to_all x1, blocking collectives, body(): lax.all_to_all(sums.reshape(NY * NZ, 2, FULL), ('y', 'z'), split_axis=0,...  31.8 us
    all_to_all x1, starting transfers between devices, body(): lax.all_to_all(pieces.reshape(NZ, 2 * NY, FULL), 'z', split_axis=0, conca...  15.2 us
    ppermute x3, starting transfers between devices, body(): lax.ppermute(dealt[d], 'y', [(i, (i + d) % NY) for i in range(NY)])  10.7 us
    all_to_all x1, waiting for transfers between devices, body(): lax.all_to_all(pieces.reshape(NZ, 2 * NY, FULL), 'z', split_axis=0, conca...  8.08 us
    all_to_all x1, waiting for transfers between devices, body(): lax.all_to_all(payload, ('x', 'y', 'core'), split_axis=0, concat_axis=0,...  7.26 us
    all_to_all x1, starting transfers between devices, body(): lax.all_to_all(payload, ('x', 'y', 'core'), split_axis=0, concat_axis=0,...  6.55 us
    all_to_all x1, starting transfers between devices, body(): panel = lax.all_to_all(panel, 'y', split_axis=0, concat_axis=0, tiled=True)  4.92 us
    all_to_all x1, waiting for transfers between devices, body(): panel = lax.all_to_all(panel, 'y', split_axis=0, concat_axis=0, tiled=True)  3.27 us
  transfers between devices with their start and end apart: 7, of which 3 were waited for; matrix products, arithmetic and copies ran while one was open for 2% of the time, Pallas kernels for 2%

profile of v4, /device:TPU:8, one launch (start us, length us, event | category | flops | bytes accessed | tf_op | source)
XLA Modules:
  0.0 105.0 jit_solution(4957815445071496928)
XLA Ops:
  0.6 0.0 copy-start
  0.7 0.7 bitcast_convert_fusion.sharp
  1.3 2.5 %deal.1 = (bf16[128,1152]{1,0:T(8,128)(2,1)}, bf16[128,1152]{1,0:T(8,128)(2,1)S(1)}, bf16[128,1152]{1,0:T(8,128)(2,1)S(1)}, bf16[128,1152]{1,0:T(8,128)(2,1)S(1)}, bf16[128,1152]{1,0:T(8,128)(2,1)S(1)}) custom-call(s32[1]{0:T(128)} %bitcast.y_ref, bf16[2048,256]{1,0:T(8,128)(2,1)} %bitcast.20, bf16[2,16,256]{2,1,0:T(8,128)(2,1)} %refs_hbm.1, ...), custom_call_target="tpu_custom_call" | custom-call | flops 300000000 | bytes 3000000 | tf_op jit(solution)/shard_map/deal/pallas_call | solution.py:246
  3.9 15.2 %all-to-all-start = ((bf16[16,8,1152]{2,1,0:T(8,128)(2,1)}), bf16[16,8,1152]{2,1,0:T(8,128)(2,1)S(1)}, u32[]{:S(2)}, u32[]{:S(2)}) async-start(bf16[16,8,1152]{2,1,0:T(8,128)(2,1)} %bitcast.8), calls=%async_computation | async-start | bytes 589824 | tf_op jit(solution)/shard_map/all_to_all | solution.py:276
  19.1 3.5 %collective-permute-start = (bf16[128,1152]{1,0:T(8,128)(2,1)S(1)}, bf16[128,1152]{1,0:T(8,128)(2,1)S(1)}, u32[]{:S(2)}, u32[]{:S(2)}) collective-permute-start(bf16[128,1152]{1,0:T(8,128)(2,1)S(1)} %get-tuple-element.8), channel_id=1, source_target_pairs={{0,128},{128,256},{256,384},{384,0},{1,129},{129,257},{257,385},{3... | collective-permute-start | bytes 884744 | tf_op jit(solution)/shard_map/ppermute | solution.py:283
  22.6 2.9 %collective-permute-start.1 = (bf16[128,1152]{1,0:T(8,128)(2,1)S(1)}, bf16[128,1152]{1,0:T(8,128)(2,1)S(1)}, u32[]{:S(2)}, u32[]{:S(2)}) collective-permute-start(bf16[128,1152]{1,0:T(8,128)(2,1)S(1)} %get-tuple-element.9), channel_id=1, source_target_pairs={{0,256},{128,384},{256,0},{384,128},{1,257},{129,385},{257,1},{385... | collective-permute-start | bytes 884744 | tf_op jit(solution)/shard_map/ppermute | solution.py:283
  25.4 4.3 %collective-permute-start.2 = (bf16[128,1152]{1,0:T(8,128)(2,1)S(1)}, bf16[128,1152]{1,0:T(8,128)(2,1)S(1)}, u32[]{:S(2)}, u32[]{:S(2)}) collective-permute-start(bf16[128,1152]{1,0:T(8,128)(2,1)S(1)} %get-tuple-element.10), channel_id=1, source_target_pairs={{0,384},{128,0},{256,128},{384,256},{1,385},{129,1},{257,129},{385... | collective-permute-start | bytes 884744 | tf_op jit(solution)/shard_map/ppermute | solution.py:283
  29.7 0.5 sine_negate_fusion
  30.3 8.1 %all-to-all-done = bf16[16,8,1152]{2,1,0:T(8,128)(2,1)S(1)} async-done(((bf16[16,8,1152]{2,1,0:T(8,128)(2,1)}), bf16[16,8,1152]{2,1,0:T(8,128)(2,1)S(1)}, u32[]{:S(2)}, u32[]{:S(2)}) %all-to-all-start) | async-done | bytes 294944 | tf_op jit(solution)/shard_map/all_to_all | solution.py:276
  38.4 0.1 reshape.46
  38.5 0.2 copy.15
  38.7 0.8 reshape.47
  39.5 4.9 %all-to-all-start.1 = ((bf16[4,32,1152]{2,1,0:T(8,128)(2,1)}), bf16[4,32,1152]{2,1,0:T(8,128)(2,1)S(1)}, u32[]{:S(2)}, u32[]{:S(2)}) async-start(bf16[4,32,1152]{2,1,0:T(8,128)(2,1)} %reshape.47), calls=%async_computation.1 | async-start | bytes 589824 | tf_op jit(solution)/shard_map/all_to_all | solution.py:280
  44.5 0.0 collective-permute-done.in1
  44.5 0.0 collective-permute-done.1.in2
  44.5 0.0 collective-permute-done.2.in3
  44.5 2.0 %align.1.rows = bf16[512,1152]{1,0:T(8,128)(2,1)S(1)} custom-call(bf16[128,1152]{1,0:T(8,128)(2,1)S(1)} %get-tuple-element.7.in0, bf16[128,1152]{1,0:T(8,128)(2,1)S(1)} %collective-permute-done.in1, bf16[128,1152]{1,0:T(8,128)(2,1)S(1)} %collective-permute-done.1.in2, bf16[128,1152]{1,0:T(8,128)(2,1)S(1)} %collective-permute-done.2.in3, ...), custom_call_target="tpu_custom_call" | custom-call | flops 800000000 | bytes 4000000 | tf_op jit(solution)/shard_map/align/pallas_call | solution.py:286
  46.6 3.3 %all-to-all-done.1 = bf16[4,32,1152]{2,1,0:T(8,128)(2,1)S(1)} async-done(((bf16[4,32,1152]{2,1,0:T(8,128)(2,1)}), bf16[4,32,1152]{2,1,0:T(8,128)(2,1)S(1)}, u32[]{:S(2)}, u32[]{:S(2)}) %all-to-all-start.1) | async-done | bytes 294944 | tf_op jit(solution)/shard_map/all_to_all | solution.py:280
  49.8 2.2 %all_gather.3.panel = bf16[256,1152]{1,0:T(8,128)(2,1)S(1)} all-gather(bf16[128,1152]{1,0:T(8,128)(2,1)S(1)} %bitcast.17), channel_id=1, replica_groups=mesh['y'=4,'z'=16,'core'=2,'x'=4] {'core'}, dimensions={0}, use_global_device_ids=true | all-gather | bytes 884736 | tf_op jit(solution)/shard_map/all_gather | solution.py:297
  52.0 1.0 score.1.payload
  53.1 0.7 copy-done.3
  53.8 2.0 %collective-permute-start.3 = (bf16[512,1152]{1,0:T(8,128)(2,1)}, bf16[512,1152]{1,0:T(8,128)(2,1)S(1)}, u32[]{:S(2)}, u32[]{:S(2)}) collective-permute-start(bf16[512,1152]{1,0:T(8,128)(2,1)} %hold.1.own), channel_id=1, source_target_pairs={{0,4},{4,0},{1,5},{5,1},{2,6},{6,2},{3,7},{7,3},{8,12},{12,8},{9,1... | collective-permute-start | bytes 3538952 | tf_op jit(solution)/shard_map/ppermute | solution.py:320
  55.8 6.6 %all-to-all-start.2 = ((f32[32,12,128]{2,1,0:T(8,128)}), f32[32,12,128]{2,1,0:T(8,128)S(1)}, u32[]{:S(2)}, u32[]{:S(2)}) async-start(f32[32,12,128]{2,1,0:T(8,128)} %copy-done.3), calls=%async_computation.2 | async-start | bytes 524288 | tf_op jit(solution)/shard_map/all_to_all | solution.py:319
  62.4 0.1 pad_add_fusion.at_ref
  62.5 7.3 %all-to-all-done.2.got = f32[32,12,128]{2,1,0:T(8,128)S(1)} async-done(((f32[32,12,128]{2,1,0:T(8,128)}), f32[32,12,128]{2,1,0:T(8,128)S(1)}, u32[]{:S(2)}, u32[]{:S(2)}) %all-to-all-start.2) | async-done | bytes 196640 | tf_op jit(solution)/shard_map/all_to_all | solution.py:319
  69.7 0.0 collective-permute-done.3.other
  69.7 1.3 %copy-done.2 = bf16[512,1152]{1,0:T(8,128)(2,1)S(1)} copy-done((bf16[512,1152]{1,0:T(8,128)(2,1)S(1)}, bf16[512,1152]{1,0:T(8,128)(2,1)}, u32[]{:S(2)}) %copy-start.2) | copy-done | bytes 1179672
  71.0 1.1 %sum.1 = bf16[128,1152]{1,0:T(8,128)(2,1)S(1)} custom-call(s32[2]{0:T(128)S(1)} %pad_add_fusion.at_ref, f32[32,12,128]{2,1,0:T(8,128)S(1)} %all-to-all-done.2.got, bf16[512,1152]{1,0:T(8,128)(2,1)S(1)} %copy-done.2, bf16[512,1152]{1,0:T(8,128)(2,1)S(1)} %collective-permute-done.3.other), custom_call_target="tpu_custom_call" | custom-call | flops 300000000 | bytes 3000000 | tf_op jit(solution)/shard_map/sum/pallas_call | solution.py:321
  72.1 0.1 reshape.49
  72.2 31.8 %all_to_all.20 = bf16[64,2,1152]{2,1,0:T(2,128)(2,1)S(1)} all-to-all(bf16[64,2,1152]{2,1,0:T(2,128)(2,1)S(1)} %reshape.49), channel_id=1, replica_groups=mesh['y'=4,'z'=16,'core'=2,'x'=4] {'y','z'}, dimensions={0} | all-to-all | bytes 589824 | tf_op jit(solution)/shard_map/all_to_all | solution.py:331
  104.0 0.1 reshape.50.got
  104.2 0.8 finish.1
  (10 shorter events, 0.1 us)
Async XLA Ops:
  0.6 43.8 %copy-start = (f32[25,16,128]{2,1,0:T(8,128)S(1)}, f32[25,16,128]{2,1,0:T(8,128)}, u32[]{:S(2)}) copy-start(f32[25,16,128]{2,1,0:T(8,128)} %param.13) | copy-start | bytes 614404
  3.9 34.5 %all-to-all-start = ((bf16[16,8,1152]{2,1,0:T(8,128)(2,1)}), bf16[16,8,1152]{2,1,0:T(8,128)(2,1)S(1)}, u32[]{:S(2)}, u32[]{:S(2)}) async-start(bf16[16,8,1152]{2,1,0:T(8,128)(2,1)} %bitcast.8), calls=%async_computation | async-start | bytes 589824 | tf_op jit(solution)/shard_map/all_to_all | solution.py:276
  19.1 25.4 %collective-permute-start = (bf16[128,1152]{1,0:T(8,128)(2,1)S(1)}, bf16[128,1152]{1,0:T(8,128)(2,1)S(1)}, u32[]{:S(2)}, u32[]{:S(2)}) collective-permute-start(bf16[128,1152]{1,0:T(8,128)(2,1)S(1)} %get-tuple-element.8), channel_id=1, source_target_pairs={{0,128},{128,256},{256,384},{384,0},{1,129},{129,257},{257,385},{3... | collective-permute-start | bytes 884744 | tf_op jit(solution)/shard_map/ppermute | solution.py:283
  22.6 22.0 %collective-permute-start.1 = (bf16[128,1152]{1,0:T(8,128)(2,1)S(1)}, bf16[128,1152]{1,0:T(8,128)(2,1)S(1)}, u32[]{:S(2)}, u32[]{:S(2)}) collective-permute-start(bf16[128,1152]{1,0:T(8,128)(2,1)S(1)} %get-tuple-element.9), channel_id=1, source_target_pairs={{0,256},{128,384},{256,0},{384,128},{1,257},{129,385},{257,1},{385... | collective-permute-start | bytes 884744 | tf_op jit(solution)/shard_map/ppermute | solution.py:283
  25.4 19.1 %collective-permute-start.2 = (bf16[128,1152]{1,0:T(8,128)(2,1)S(1)}, bf16[128,1152]{1,0:T(8,128)(2,1)S(1)}, u32[]{:S(2)}, u32[]{:S(2)}) collective-permute-start(bf16[128,1152]{1,0:T(8,128)(2,1)S(1)} %get-tuple-element.10), channel_id=1, source_target_pairs={{0,384},{128,0},{256,128},{384,256},{1,385},{129,1},{257,129},{385... | collective-permute-start | bytes 884744 | tf_op jit(solution)/shard_map/ppermute | solution.py:283
  39.5 10.3 %all-to-all-start.1 = ((bf16[4,32,1152]{2,1,0:T(8,128)(2,1)}), bf16[4,32,1152]{2,1,0:T(8,128)(2,1)S(1)}, u32[]{:S(2)}, u32[]{:S(2)}) async-start(bf16[4,32,1152]{2,1,0:T(8,128)(2,1)} %reshape.47), calls=%async_computation.1 | async-start | bytes 589824 | tf_op jit(solution)/shard_map/all_to_all | solution.py:280
  46.6 6.5 %copy-start.1 = (bf16[512,1152]{1,0:T(8,128)(2,1)}, bf16[512,1152]{1,0:T(8,128)(2,1)S(1)}, u32[]{:S(2)}) copy-start(bf16[512,1152]{1,0:T(8,128)(2,1)S(1)} %align.1.rows) | copy-start | bytes 3538948
  53.1 0.7 copy-start.3
  53.8 15.9 %collective-permute-start.3 = (bf16[512,1152]{1,0:T(8,128)(2,1)}, bf16[512,1152]{1,0:T(8,128)(2,1)S(1)}, u32[]{:S(2)}, u32[]{:S(2)}) collective-permute-start(bf16[512,1152]{1,0:T(8,128)(2,1)} %hold.1.own), channel_id=1, source_target_pairs={{0,4},{4,0},{1,5},{5,1},{2,6},{6,2},{3,7},{7,3},{8,12},{12,8},{9,1... | collective-permute-start | bytes 3538952 | tf_op jit(solution)/shard_map/ppermute | solution.py:320
  55.8 13.9 %all-to-all-start.2 = ((f32[32,12,128]{2,1,0:T(8,128)}), f32[32,12,128]{2,1,0:T(8,128)S(1)}, u32[]{:S(2)}, u32[]{:S(2)}) async-start(f32[32,12,128]{2,1,0:T(8,128)} %copy-done.3), calls=%async_computation.2 | async-start | bytes 524288 | tf_op jit(solution)/shard_map/all_to_all | solution.py:319
  69.7 1.3 %copy-start.2 = (bf16[512,1152]{1,0:T(8,128)(2,1)S(1)}, bf16[512,1152]{1,0:T(8,128)(2,1)}, u32[]{:S(2)}) copy-start(bf16[512,1152]{1,0:T(8,128)(2,1)} %hold.1.own) | copy-start | bytes 3538948

commit v5 on v3

--- a/solution.py
+++ b/solution.py
@@ -302,7 +302,6 @@
         [SMEM] + [VMEM] * 2,
         VMEM,
     )(y[None], rows, panel)
-    rows, payload = lax.optimization_barrier((rows, payload))
     got = lax.all_to_all(payload, ("x", "y", "core"), split_axis=0, concat_axis=0, tiled=True)
     other = lax.ppermute(rows, "core", [(0, 1), (1, 0)])
     sums = call(

time: 108 us -> 104 us (0.963)
  blocking collectives: 38.9 us -> 30.8 us
  waiting for transfers between devices: 19.3 us -> 24.1 us
    all_to_all x1, waiting for transfers between devices: 0.01 us -> 16.8 us  [body(): lax.all_to_all(pieces.reshape(NY * NZ, 2, FULL), ('y', 'z'), split_axis=0...]
    ppermute x3, waiting for transfers between devices: 12 us -> 0.01 us  [body(): lax.ppermute(dealt[d], 'y', [(i, (i + d) % NY) for i in range(NY)])]
    all_to_all x1, blocking collectives: 36.7 us -> 28.6 us  [body(): lax.all_to_all(sums.reshape(NY * NZ, 2, FULL), ('y', 'z'), split_axis=0,...]
    all_to_all x1, starting transfers between devices: 18.7 us -> 14.1 us  [body(): lax.all_to_all(pieces.reshape(NY * NZ, 2, FULL), ('y', 'z'), split_axis=0...]
    ppermute x3, starting transfers between devices: 10.6 us -> 13.6 us  [body(): lax.ppermute(dealt[d], 'y', [(i, (i + d) % NY) for i in range(NY)])]
  transfers between devices with their start and end apart: 6 -> 6, of which waited for: 4 -> 2; matrix products, arithmetic and copies ran while one was open for 1% -> 2% of each run, Pallas kernels for 2% -> 4%
where the time goes in v5:
time: 104 us; the launch traced here: 103 us
  starting transfers between devices  37.2 us (36%)
  blocking collectives  30.8 us (30%)
  waiting for transfers between devices  24.1 us (23%)
  Pallas kernels  7.68 us (7%)
  other arithmetic  1.32 us (1%)
  local copies, waits for them, and re-layouts  1.2 us (1%)
    all_to_all x1, blocking collectives, body(): lax.all_to_all(sums.reshape(NY * NZ, 2, FULL), ('y', 'z'), split_axis=0,...  28.6 us
    all_to_all x1, waiting for transfers between devices, body(): lax.all_to_all(pieces.reshape(NY * NZ, 2, FULL), ('y', 'z'), split_axis=0...  16.8 us
    all_to_all x1, starting transfers between devices, body(): lax.all_to_all(pieces.reshape(NY * NZ, 2, FULL), ('y', 'z'), split_axis=0...  14.1 us
    ppermute x3, starting transfers between devices, body(): lax.ppermute(dealt[d], 'y', [(i, (i + d) % NY) for i in range(NY)])  13.6 us
    all_to_all x1, starting transfers between devices, body(): lax.all_to_all(payload, ('x', 'y', 'core'), split_axis=0, concat_axis=0,...  7.53 us
    all_to_all x1, waiting for transfers between devices, body(): lax.all_to_all(payload, ('x', 'y', 'core'), split_axis=0, concat_axis=0,...  7.26 us
    all_gather x1, blocking collectives, body(): lax.all_gather(panel.reshape(NY * NZ * 2, FULL), 'core', axis=0, tiled=True)  2.23 us
  transfers between devices with their start and end apart: 6, of which 2 were waited for; matrix products, arithmetic and copies ran while one was open for 2% of the time, Pallas kernels for 4%

profile of v5, /device:TPU:8, one launch (start us, length us, event | category | flops | bytes accessed | tf_op | source)
XLA Modules:
  0.0 103.1 jit_solution(3082103878190848145)
XLA Ops:
  0.6 0.0 copy-start
  0.7 0.7 bitcast_convert_fusion.sharp
  1.3 2.0 %deal.1 = (bf16[128,1152]{1,0:T(8,128)(2,1)S(1)}, bf16[128,1152]{1,0:T(8,128)(2,1)S(1)}, bf16[128,1152]{1,0:T(8,128)(2,1)S(1)}, bf16[128,1152]{1,0:T(8,128)(2,1)S(1)}, bf16[128,1152]{1,0:T(8,128)(2,1)S(1)}) custom-call(s32[1]{0:T(128)} %bitcast.y_ref, bf16[2048,256]{1,0:T(8,128)(2,1)} %bitcast.13, bf16[2,16,256]{2,1,0:T(8,128)(2,1)} %refs_hbm.1, ...), custom_call_target="tpu_custom_call" | custom-call | flops 300000000 | bytes 3000000 | tf_op jit(solution)/shard_map/deal/pallas_call | solution.py:245
  3.4 3.5 %collective-permute-start = (bf16[128,1152]{1,0:T(8,128)(2,1)S(1)}, bf16[128,1152]{1,0:T(8,128)(2,1)S(1)}, u32[]{:S(2)}, u32[]{:S(2)}) collective-permute-start(bf16[128,1152]{1,0:T(8,128)(2,1)S(1)} %get-tuple-element.8), channel_id=1, source_target_pairs={{0,128},{128,256},{256,384},{384,0},{1,129},{129,257},{257,385},{3... | collective-permute-start | bytes 884744 | tf_op jit(solution)/shard_map/ppermute | solution.py:280
  6.9 8.2 %collective-permute-start.1 = (bf16[128,1152]{1,0:T(8,128)(2,1)S(1)}, bf16[128,1152]{1,0:T(8,128)(2,1)S(1)}, u32[]{:S(2)}, u32[]{:S(2)}) collective-permute-start(bf16[128,1152]{1,0:T(8,128)(2,1)S(1)} %get-tuple-element.9), channel_id=1, source_target_pairs={{0,256},{128,384},{256,0},{384,128},{1,257},{129,385},{257,1},{385... | collective-permute-start | bytes 884744 | tf_op jit(solution)/shard_map/ppermute | solution.py:280
  15.1 1.9 %collective-permute-start.2 = (bf16[128,1152]{1,0:T(8,128)(2,1)S(1)}, bf16[128,1152]{1,0:T(8,128)(2,1)S(1)}, u32[]{:S(2)}, u32[]{:S(2)}) collective-permute-start(bf16[128,1152]{1,0:T(8,128)(2,1)S(1)} %get-tuple-element.10), channel_id=1, source_target_pairs={{0,384},{128,0},{256,128},{384,256},{1,385},{129,1},{257,129},{385... | collective-permute-start | bytes 884744 | tf_op jit(solution)/shard_map/ppermute | solution.py:280
  17.1 0.8 reshape.39
  17.9 14.1 %all-to-all-start = ((bf16[64,2,1152]{2,1,0:T(2,128)(2,1)}), bf16[64,2,1152]{2,1,0:T(2,128)(2,1)S(1)}, u32[]{:S(2)}, u32[]{:S(2)}) async-start(bf16[64,2,1152]{2,1,0:T(2,128)(2,1)} %reshape.39), calls=%async_computation | async-start | bytes 589824 | tf_op jit(solution)/shard_map/all_to_all | solution.py:275
  32.0 0.0 copy-done
  32.1 0.5 sine_negate_fusion
  32.6 0.0 collective-permute-done.in1
  32.6 0.0 collective-permute-done.1.in2
  32.7 0.0 collective-permute-done.2.in3
  32.7 2.0 %align.1.rows.own = bf16[512,1152]{1,0:T(8,128)(2,1)S(1)} custom-call(bf16[128,1152]{1,0:T(8,128)(2,1)S(1)} %get-tuple-element.7.in0, bf16[128,1152]{1,0:T(8,128)(2,1)S(1)} %collective-permute-done.in1, bf16[128,1152]{1,0:T(8,128)(2,1)S(1)} %collective-permute-done.1.in2, bf16[128,1152]{1,0:T(8,128)(2,1)S(1)} %collective-permute-done.2.in3, ...), custom_call_target="tpu_custom_call" | custom-call | flops 800000000 | bytes 4000000 | tf_op jit(solution)/shard_map/align/pallas_call | solution.py:283
  34.7 1.9 %collective-permute-start.3 = (bf16[512,1152]{1,0:T(8,128)(2,1)S(1)}, bf16[512,1152]{1,0:T(8,128)(2,1)S(1)}, u32[]{:S(2)}, u32[]{:S(2)}) collective-permute-start(bf16[512,1152]{1,0:T(8,128)(2,1)S(1)} %align.1.rows.own), channel_id=1, source_target_pairs={{0,4},{4,0},{1,5},{5,1},{2,6},{6,2},{3,7},{7,3},{8,12},{12,8},{9,1... | collective-permute-start | bytes 3538952 | tf_op jit(solution)/shard_map/ppermute | solution.py:306
  36.6 16.8 %all-to-all-done = bf16[64,2,1152]{2,1,0:T(2,128)(2,1)S(1)} async-done(((bf16[64,2,1152]{2,1,0:T(2,128)(2,1)}), bf16[64,2,1152]{2,1,0:T(2,128)(2,1)S(1)}, u32[]{:S(2)}, u32[]{:S(2)}) %all-to-all-start) | async-done | bytes 294944 | tf_op jit(solution)/shard_map/all_to_all | solution.py:275
  53.4 0.1 reshape.40
  53.5 2.2 %all_gather.3.panel = bf16[256,1152]{1,0:T(8,128)(2,1)S(1)} all-gather(bf16[128,1152]{1,0:T(8,128)(2,1)S(1)} %reshape.40), channel_id=1, replica_groups=mesh['y'=4,'z'=16,'core'=2,'x'=4] {'core'}, dimensions={0}, use_global_device_ids=true | all-gather | bytes 884736 | tf_op jit(solution)/shard_map/all_gather | solution.py:294
  55.7 1.8 %score.1 = f32[32,12,128]{2,1,0:T(8,128)} custom-call(s32[1]{0:T(128)} %bitcast.y_ref, bf16[512,1152]{1,0:T(8,128)(2,1)S(1)} %align.1.rows.own, bf16[256,1152]{1,0:T(8,128)(2,1)S(1)} %all_gather.3.panel), custom_call_target="tpu_custom_call" | custom-call | flops 600000000 | bytes 2000000 | tf_op jit(solution)/shard_map/score/pallas_call | solution.py:295
  57.5 7.5 %all-to-all-start.1 = ((f32[32,12,128]{2,1,0:T(8,128)}), f32[32,12,128]{2,1,0:T(8,128)S(1)}, u32[]{:S(2)}, u32[]{:S(2)}) async-start(f32[32,12,128]{2,1,0:T(8,128)} %score.1), calls=%async_computation.1 | async-start | bytes 524288 | tf_op jit(solution)/shard_map/all_to_all | solution.py:305
  65.0 0.1 pad_add_fusion.at_ref
  65.1 7.3 %all-to-all-done.1.got = f32[32,12,128]{2,1,0:T(8,128)S(1)} async-done(((f32[32,12,128]{2,1,0:T(8,128)}), f32[32,12,128]{2,1,0:T(8,128)S(1)}, u32[]{:S(2)}, u32[]{:S(2)}) %all-to-all-start.1) | async-done | bytes 196640 | tf_op jit(solution)/shard_map/all_to_all | solution.py:305
  72.4 0.0 collective-permute-done.3.other
  72.4 1.1 %sum.1 = bf16[128,1152]{1,0:T(8,128)(2,1)S(1)} custom-call(s32[2]{0:T(128)S(1)} %pad_add_fusion.at_ref, f32[32,12,128]{2,1,0:T(8,128)S(1)} %all-to-all-done.1.got, bf16[512,1152]{1,0:T(8,128)(2,1)S(1)} %align.1.rows.own, bf16[512,1152]{1,0:T(8,128)(2,1)S(1)} %collective-permute-done.3.other), custom_call_target="tpu_custom_call" | custom-call | flops 300000000 | bytes 3000000 | tf_op jit(solution)/shard_map/sum/pallas_call | solution.py:307
  73.5 0.1 reshape.41
  73.6 28.6 %all_to_all.15 = bf16[64,2,1152]{2,1,0:T(2,128)(2,1)S(1)} all-to-all(bf16[64,2,1152]{2,1,0:T(2,128)(2,1)S(1)} %reshape.41), channel_id=1, replica_groups=mesh['y'=4,'z'=16,'core'=2,'x'=4] {'y','z'}, dimensions={0} | all-to-all | bytes 589824 | tf_op jit(solution)/shard_map/all_to_all | solution.py:317
  102.2 0.1 reshape.42.got
  102.3 0.8 finish.1
  (4 shorter events, 0.1 us)
Async XLA Ops:
  0.6 31.4 %copy-start = (f32[25,16,128]{2,1,0:T(8,128)S(1)}, f32[25,16,128]{2,1,0:T(8,128)}, u32[]{:S(2)}) copy-start(f32[25,16,128]{2,1,0:T(8,128)} %param.13) | copy-start | bytes 614404
  3.4 29.3 %collective-permute-start = (bf16[128,1152]{1,0:T(8,128)(2,1)S(1)}, bf16[128,1152]{1,0:T(8,128)(2,1)S(1)}, u32[]{:S(2)}, u32[]{:S(2)}) collective-permute-start(bf16[128,1152]{1,0:T(8,128)(2,1)S(1)} %get-tuple-element.8), channel_id=1, source_target_pairs={{0,128},{128,256},{256,384},{384,0},{1,129},{129,257},{257,385},{3... | collective-permute-start | bytes 884744 | tf_op jit(solution)/shard_map/ppermute | solution.py:280
  6.9 25.8 %collective-permute-start.1 = (bf16[128,1152]{1,0:T(8,128)(2,1)S(1)}, bf16[128,1152]{1,0:T(8,128)(2,1)S(1)}, u32[]{:S(2)}, u32[]{:S(2)}) collective-permute-start(bf16[128,1152]{1,0:T(8,128)(2,1)S(1)} %get-tuple-element.9), channel_id=1, source_target_pairs={{0,256},{128,384},{256,0},{384,128},{1,257},{129,385},{257,1},{385... | collective-permute-start | bytes 884744 | tf_op jit(solution)/shard_map/ppermute | solution.py:280
  15.1 17.5 %collective-permute-start.2 = (bf16[128,1152]{1,0:T(8,128)(2,1)S(1)}, bf16[128,1152]{1,0:T(8,128)(2,1)S(1)}, u32[]{:S(2)}, u32[]{:S(2)}) collective-permute-start(bf16[128,1152]{1,0:T(8,128)(2,1)S(1)} %get-tuple-element.10), channel_id=1, source_target_pairs={{0,384},{128,0},{256,128},{384,256},{1,385},{129,1},{257,129},{385... | collective-permute-start | bytes 884744 | tf_op jit(solution)/shard_map/ppermute | solution.py:280
  17.9 35.5 %all-to-all-start = ((bf16[64,2,1152]{2,1,0:T(2,128)(2,1)}), bf16[64,2,1152]{2,1,0:T(2,128)(2,1)S(1)}, u32[]{:S(2)}, u32[]{:S(2)}) async-start(bf16[64,2,1152]{2,1,0:T(2,128)(2,1)} %reshape.39), calls=%async_computation | async-start | bytes 589824 | tf_op jit(solution)/shard_map/all_to_all | solution.py:275
  34.7 37.7 %collective-permute-start.3 = (bf16[512,1152]{1,0:T(8,128)(2,1)S(1)}, bf16[512,1152]{1,0:T(8,128)(2,1)S(1)}, u32[]{:S(2)}, u32[]{:S(2)}) collective-permute-start(bf16[512,1152]{1,0:T(8,128)(2,1)S(1)} %align.1.rows.own), channel_id=1, source_target_pairs={{0,4},{4,0},{1,5},{5,1},{2,6},{6,2},{3,7},{7,3},{8,12},{12,8},{9,1... | collective-permute-start | bytes 3538952 | tf_op jit(solution)/shard_map/ppermute | solution.py:306
  57.5 14.9 %all-to-all-start.1 = ((f32[32,12,128]{2,1,0:T(8,128)}), f32[32,12,128]{2,1,0:T(8,128)S(1)}, u32[]{:S(2)}, u32[]{:S(2)}) async-start(f32[32,12,128]{2,1,0:T(8,128)} %score.1), calls=%async_computation.1 | async-start | bytes 524288 | tf_op jit(solution)/shard_map/all_to_all | solution.py:305

commit v6 on v5

--- a/solution.py
+++ b/solution.py
@@ -44,7 +44,7 @@
     label_hbm,
     rot_hbm,
     shift_hbm,
-    sharp,
+    sharp_hbm,
     pieces,
     out0,
     out1,
@@ -53,6 +53,7 @@
     images,
     refs,
     ints,
+    sharp,
     row_of,
     grid,
     sems,
@@ -66,35 +67,36 @@
                 (label_hbm, ints.at[pl.ds(0, 1)]),
                 (rot_hbm, ints.at[pl.ds(1, 1)]),
                 (shift_hbm, ints.at[pl.ds(2, 1)]),
+                (sharp_hbm, sharp),
             )
         )
     ]
     quarter = P_DEV * R_DEV // 4
     for i in range(4):
         rows = pl.ds(i * quarter, quarter)
-        copies.append(pltpu.make_async_copy(images_hbm.at[rows], images.at[rows], sems.at[4 + i]))
+        copies.append(pltpu.make_async_copy(images_hbm.at[rows], images.at[rows], sems.at[5 + i]))
     for copy in copies:
         copy.start()
-    for copy in copies[:4]:
+    for copy in copies[:5]:
         copy.wait()
-    odd = (iota((2 * NZ, FULL), 0) & 1) == 1
     for j in range(2):
         wide = refs[j].astype(jnp.float32)
         for r in range(R_DEV):
             at = r // R_OWN * 2 + j
             lanes = slice(r % R_OWN * A, r % R_OWN * A + A)
             row_of[at : at + 1, lanes] = wide[r : r + 1]
-        tile = jnp.broadcast_to(sharp[0:1, j : j + 1], (1, 128))
+        tile = jnp.broadcast_to(sharp[...].astype(jnp.float32)[0:1, j : j + 1], (1, 128))
         for r in range(NY):
             row_of[2 * r + j : 2 * r + j + 1, WIDE:] = tile
     for r in range(NY):
-        pair = jnp.where(odd, row_of[2 * r + 1 : 2 * r + 2, :], row_of[2 * r : 2 * r + 1, :])
-        pieces[r * 2 * NZ : (r + 1) * 2 * NZ, :] = pair.astype(jnp.bfloat16)
+        pair = row_of[2 * r : 2 * r + 2, :].astype(jnp.bfloat16)
+        for z in range(NZ):
+            pieces[r * NZ + z] = pair
     row, col = iota((A, A), 0), iota((A, A), 1)
     swap = (col == ((row & 15) * 16 + (row >> 4))).astype(jnp.float32).astype(jnp.bfloat16)
     for b in range(P_DEV // 16):
         if b % 2 == 0:
-            copies[4 + b // 2].wait()
+            copies[5 + b // 2].wait()
         x = jnp.dot(swap, images[b * A : b * A + A, :], preferred_element_type=jnp.float32)
         x = x.astype(jnp.bfloat16)
         for r in range(R_DEV):
@@ -144,52 +146,58 @@
         out[rows, WIDE:] = block[:, WIDE:]
 
 
-def score_kernel(y_ref, rows, panel, out, stats):
-    y = y_ref[0]
-    refs = panel[:, :WIDE]
-    wide = refs.astype(jnp.float32)
+def labels_of(rows, first, core):
+    label = rows[first : first + 16, WIDE:].astype(jnp.float32)[0:1].astype(jnp.int32)
+    return label ^ (core * P_DEV)
+
+
+def norm_kernel(refs, out):
+    wide = refs[:, :WIDE].astype(jnp.float32)
     norm = jnp.sum(wide * wide, axis=1, keepdims=True)
-    sharp = panel[:, WIDE:].astype(jnp.float32)
-    diagonal = iota((P_DEV, P_DEV), 0) == iota((P_DEV, P_DEV), 1)
-    for d in range(NY):
-        source = (y - d) & (NY - 1)
-        flat = rows[d * P_DEV : d * P_DEV + P_DEV, :WIDE]
-        label = rows[d * P_DEV : d * P_DEV + 16, WIDE:].astype(jnp.float32)[0:1].astype(jnp.int32)
-        member = iota((C, P_DEV), 0) == label
-        scores = lax.dot_general(
-            refs, flat, (((1,), (1,)), ((), ())), preferred_element_type=jnp.float32
-        )
-        gram = lax.dot_general(
-            flat, flat, (((1,), (1,)), ((), ())), preferred_element_type=jnp.float32
-        )
-        inner = jnp.sum(jnp.where(member, scores, 0.0), axis=0, keepdims=True)
-        power = jnp.sum(jnp.where(diagonal, gram, 0.0), axis=0, keepdims=True)
-        ref_power = jnp.sum(jnp.where(member, norm, 0.0), axis=0, keepdims=True)
-        own_sharp = jnp.sum(jnp.where(member, sharp, 0.0), axis=0, keepdims=True)
-        for at, value in enumerate((own_sharp * inner, power, ref_power)):
-            stats[pl.ds(at * NY + source, 1), :] = value
+    out[...] = jnp.broadcast_to(norm, (P_DEV, P_DEV))
+
+
+def score_kernel(at_ref, own, other, refs, norm, out, stats):
+    y, core = at_ref[0], at_ref[1]
+    flat_refs = refs[:, :WIDE]
+    sharp = refs[:, WIDE:].astype(jnp.float32)
+    class_of = iota((P_DEV, P_DEV), 0)
+    diagonal = class_of == iota((P_DEV, P_DEV), 1)
+    for side, rows in enumerate((own, other)):
+        for d in range(NY):
+            source = (y - d) & (NY - 1)
+            flat = rows[d * P_DEV : d * P_DEV + P_DEV, :WIDE]
+            member = class_of == labels_of(rows, d * P_DEV, core)
+            scores = lax.dot_general(
+                flat_refs, flat, (((1,), (1,)), ((), ())), preferred_element_type=jnp.float32
+            )
+            gram = lax.dot_general(
+                flat, flat, (((1,), (1,)), ((), ())), preferred_element_type=jnp.float32
+            )
+            inner = jnp.sum(jnp.where(member, scores * sharp, 0.0), axis=0, keepdims=True)
+            power = jnp.sum(jnp.where(diagonal, gram, 0.0), axis=0, keepdims=True)
+            ref_power = jnp.sum(jnp.where(member, norm[...], 0.0), axis=0, keepdims=True)
+            for at, value in enumerate((inner, power, ref_power)):
+                stats[pl.ds(at * 2 * NY + side * NY + source, 1), :] = value
     value = stats[...]
-    for i in range(NX * NY * 2):
+    for i in range(NX * NY):
         out[i] = value
 
 
 def sum_kernel(at_ref, got, own, other, out, weights):
     y, core = at_ref[0], at_ref[1]
-    for c in range(2):
-        total = got[c]
-        for i in range(1, NX * NY):
-            total = total + got[2 * i + c]
-        inner, power, ref_power = total[0:NY], total[NY : 2 * NY], total[2 * NY : 3 * NY]
-        weight = jax.nn.sigmoid(inner / jnp.sqrt((power + EPSILON) * (ref_power + EPSILON)))
-        weights[c * NY : c * NY + NY, :] = weight.astype(jnp.bfloat16).astype(jnp.float32)
+    total = got[0]
+    for i in range(1, NX * NY):
+        total = total + got[i]
+    inner, power, ref_power = total[:8], total[8:16], total[16:]
+    weight = jax.nn.sigmoid(inner / jnp.sqrt((power + EPSILON) * (ref_power + EPSILON)))
+    weights[...] = weight.astype(jnp.bfloat16).astype(jnp.float32)
     spread = []
-    for rows, side in ((own, core), (other, 1 - core)):
+    for side, rows in enumerate((own, other)):
         parts = []
         for d in range(NY):
             source = (y - d) & (NY - 1)
-            first = d * P_DEV
-            label = rows[first : first + 16, WIDE:].astype(jnp.float32)[0:1].astype(jnp.int32)
-            member = iota((P_DEV, P_DEV), 0) == (label ^ (core * 128))
+            member = iota((P_DEV, P_DEV), 0) == labels_of(rows, d * P_DEV, core)
             weight = weights[pl.ds(side * NY + source, 1), :]
             parts.append(jnp.where(member, weight, 0.0).astype(jnp.bfloat16))
         spread.append(jnp.concatenate(parts, axis=1))
@@ -245,18 +253,19 @@
     pieces, *dealt = call(
         deal_kernel,
         "deal",
-        [block] * (1 + NY),
+        [shape((NY * NZ, 2, FULL), jnp.bfloat16)] + [block] * NY,
         [
             pltpu.VMEM((P_DEV * R_DEV, A), jnp.bfloat16),
             pltpu.VMEM((2, R_DEV, A), jnp.bfloat16),
             pltpu.VMEM((8, P_DEV), jnp.int32),
+            pltpu.VMEM((1, 2), jnp.bfloat16),
             pltpu.VMEM((2 * NY, FULL), jnp.float32),
             pltpu.VMEM((R_DEV, P_DEV, A), jnp.bfloat16),
-            pltpu.SemaphoreType.DMA((8,)),
+            pltpu.SemaphoreType.DMA((9,)),
         ],
         300_000_000,
         3_000_000,
-        [SMEM] + [HBM] * 5 + [VMEM],
+        [SMEM] + [HBM] * 6,
         [VMEM] * (1 + NY),
     )(
         y[None],
@@ -268,16 +277,17 @@
                 classes.reshape(1, P_DEV),
                 rotations.reshape(1, P_DEV),
                 shifts.reshape(1, P_DEV),
+                sharpness.reshape(1, 2),
             )
         ],
-        sharpness.astype(jnp.float32).reshape(1, 2),
-    )
-    panel = lax.all_to_all(
-        pieces.reshape(NY * NZ, 2, FULL), ("y", "z"), split_axis=0, concat_axis=0, tiled=True
     )
     blocks = [dealt[0]]
     for d in range(1, NY):
         blocks.append(lax.ppermute(dealt[d], "y", [(i, (i + d) % NY) for i in range(NY)]))
+    pieces, blocks[1] = lax.optimization_barrier((pieces, blocks[1]))
+    panel = lax.all_to_all(
+        pieces, ("y", "z"), split_axis=0, concat_axis=0, tiled=True
+    )
     phases = lax.dynamic_slice_in_dim(shift_phase, y * R_OWN, R_OWN, 1).transpose(1, 0, 2)
     phases = jnp.pad(phases, ((0, 0), (0, SHIFT_ROWS - 25), (0, 0)))
     rows = call(
@@ -291,19 +301,30 @@
         VMEM,
     )(*blocks, spectral_table(A), phases)
 
-    panel = lax.all_gather(panel.reshape(NY * NZ * 2, FULL), "core", axis=0, tiled=True)
+    other = lax.ppermute(rows, "core", [(0, 1), (1, 0)])
+    at = jnp.stack([y, core])
+    panel = panel.reshape(NY * NZ * 2, FULL)
+    norm = call(
+        norm_kernel,
+        "norms",
+        shape((P_DEV, P_DEV), jnp.float32),
+        [],
+        300_000,
+        300_000,
+        [VMEM],
+        VMEM,
+    )(panel)
     payload = call(
         score_kernel,
         "score",
-        shape((NX * NY * 2, 3 * NY, P_DEV), jnp.float32),
-        [pltpu.VMEM((3 * NY, P_DEV), jnp.float32)],
+        shape((NX * NY, 6 * NY, P_DEV), jnp.float32),
+        [pltpu.VMEM((6 * NY, P_DEV), jnp.float32)],
         600_000_000,
         2_000_000,
-        [SMEM] + [VMEM] * 2,
+        [SMEM] + [VMEM] * 4,
         VMEM,
-    )(y[None], rows, panel)
-    got = lax.all_to_all(payload, ("x", "y", "core"), split_axis=0, concat_axis=0, tiled=True)
-    other = lax.ppermute(rows, "core", [(0, 1), (1, 0)])
+    )(at, rows, other, panel, norm)
+    got = lax.all_to_all(payload, ("x", "y"), split_axis=0, concat_axis=0, tiled=True)
     sums = call(
         sum_kernel,
         "sum",
@@ -313,7 +334,7 @@
         3_000_000,
         [SMEM] + [VMEM] * 3,
         VMEM,
-    )(jnp.stack([y, core]), got, rows, other)
+    )(at, got, rows, other)
     sums = lax.all_to_all(
         sums.reshape(NY * NZ, 2, FULL), ("y", "z"), split_axis=0, concat_axis=0, tiled=True
     )

time: 104 us -> 99.4 us (0.956)
  waiting for transfers between devices: 24.1 us -> 14.2 us
  blocking collectives: 30.8 us -> 38.6 us
  starting transfers between devices: 37.2 us -> 36 us
    all_to_all x0 -> x1, blocking collectives: none -> 13.9 us  [body(): lax.all_to_all(payload, ('x', 'y'), split_axis=0, concat_axis=0, tiled=True)]
    all_to_all x2 -> x1, waiting for transfers between devices: 24.1 us -> 13.2 us  [body(): lax.all_to_all(pieces, ('y', 'z'), split_axis=0, concat_axis=0, tiled=True)]
    all_to_all x1, blocking collectives: 28.6 us -> 24.7 us  [body(): lax.all_to_all(sums.reshape(NY * NZ, 2, FULL), ('y', 'z'), split_axis=0,...]
    all_gather x1 -> x0, blocking collectives: 2.23 us -> none  [body(): lax.all_gather(panel.reshape(NY * NZ * 2, FULL), 'core', axis=0, tiled=True)]
    all_to_all x2 -> x1, starting transfers between devices: 21.6 us -> 20.5 us  [body(): lax.all_to_all(pieces, ('y', 'z'), split_axis=0, concat_axis=0, tiled=True)]
    pallas_call x2 -> x3, Pallas kernels: 3.79 us -> 4.56 us  [the longest x1 2.61 us: body(): call(deal_kernel, 'deal', [shape((NY * NZ, 2, FULL), jnp.bfloat16)] + [bl...]
  transfers between devices with their start and end apart: 6 -> 5, of which waited for: 2 -> 2; matrix products, arithmetic and copies ran while one was open for 2% -> 1% of each run, Pallas kernels for 4% -> 2%
where the time goes in v6:
time: 99.4 us; the launch traced here: 99.1 us
  blocking collectives  38.6 us (39%)
  starting transfers between devices  36 us (36%)
  waiting for transfers between devices  14.2 us (14%)
  Pallas kernels  8.48 us (9%)
    all_to_all x1, blocking collectives, body(): lax.all_to_all(sums.reshape(NY * NZ, 2, FULL), ('y', 'z'), split_axis=0,...  24.7 us
    all_to_all x1, starting transfers between devices, body(): lax.all_to_all(pieces, ('y', 'z'), split_axis=0, concat_axis=0, tiled=True)  20.5 us
    all_to_all x1, blocking collectives, body(): lax.all_to_all(payload, ('x', 'y'), split_axis=0, concat_axis=0, tiled=True)  13.9 us
    ppermute x3, starting transfers between devices, body(): lax.ppermute(dealt[d], 'y', [(i, (i + d) % NY) for i in range(NY)])  13.6 us
    all_to_all x1, waiting for transfers between devices, body(): lax.all_to_all(pieces, ('y', 'z'), split_axis=0, concat_axis=0, tiled=True)  13.2 us
    pallas_call x1, Pallas kernels, body(): call(deal_kernel, 'deal', [shape((NY * NZ, 2, FULL), jnp.bfloat16)] + [bl...  2.61 us
    pallas_call x1, Pallas kernels, body(): call(align_kernel, 'align', shape((NY * P_DEV, FULL), jnp.bfloat16), [plt...  2.02 us
  transfers between devices with their start and end apart: 5, of which 2 were waited for; matrix products, arithmetic and copies ran while one was open for 1% of the time, Pallas kernels for 2%

profile of v6, /device:TPU:8, one launch (start us, length us, event | category | flops | bytes accessed | tf_op | source)
XLA Modules:
  0.0 99.1 jit_solution(10717592635580108859)
XLA Ops:
  0.6 0.0 copy-start
  0.7 2.6 %deal.1 = (bf16[64,2,1152]{2,1,0:T(2,128)(2,1)}, bf16[128,1152]{1,0:T(8,128)(2,1)S(1)}, bf16[128,1152]{1,0:T(8,128)(2,1)S(1)}, bf16[128,1152]{1,0:T(8,128)(2,1)S(1)}, bf16[128,1152]{1,0:T(8,128)(2,1)S(1)}) custom-call(s32[1]{0:T(128)} %bitcast.y_ref, bf16[2048,256]{1,0:T(8,128)(2,1)} %bitcast.11, bf16[2,16,256]{2,1,0:T(8,128)(2,1)} %refs_hbm.1, ...), custom_call_target="tpu_custom_call" | custom-call | flops 300000000 | bytes 3000000 | tf_op jit(solution)/shard_map/deal/pallas_call | solution.py:253
  3.3 3.5 %collective-permute-start = (bf16[128,1152]{1,0:T(8,128)(2,1)S(1)}, bf16[128,1152]{1,0:T(8,128)(2,1)S(1)}, u32[]{:S(2)}, u32[]{:S(2)}) collective-permute-start(bf16[128,1152]{1,0:T(8,128)(2,1)S(1)} %get-tuple-element.11), channel_id=1, source_target_pairs={{0,128},{128,256},{256,384},{384,0},{1,129},{129,257},{257,385},{3... | collective-permute-start | bytes 884744 | tf_op jit(solution)/shard_map/ppermute | solution.py:286
  6.8 8.2 %collective-permute-start.1 = (bf16[128,1152]{1,0:T(8,128)(2,1)S(1)}, bf16[128,1152]{1,0:T(8,128)(2,1)S(1)}, u32[]{:S(2)}, u32[]{:S(2)}) collective-permute-start(bf16[128,1152]{1,0:T(8,128)(2,1)S(1)} %get-tuple-element.13), channel_id=1, source_target_pairs={{0,256},{128,384},{256,0},{384,128},{1,257},{129,385},{257,1},{385... | collective-permute-start | bytes 884744 | tf_op jit(solution)/shard_map/ppermute | solution.py:286
  15.0 1.9 %collective-permute-start.2 = (bf16[128,1152]{1,0:T(8,128)(2,1)S(1)}, bf16[128,1152]{1,0:T(8,128)(2,1)S(1)}, u32[]{:S(2)}, u32[]{:S(2)}) collective-permute-start(bf16[128,1152]{1,0:T(8,128)(2,1)S(1)} %get-tuple-element.14), channel_id=1, source_target_pairs={{0,384},{128,0},{256,128},{384,256},{1,385},{129,1},{257,129},{385... | collective-permute-start | bytes 884744 | tf_op jit(solution)/shard_map/ppermute | solution.py:286
  16.9 0.5 sine_negate_fusion
  17.5 1.0 collective-permute-done.in1
  18.4 20.5 %all-to-all-start = ((bf16[64,2,1152]{2,1,0:T(2,128)(2,1)}), bf16[64,2,1152]{2,1,0:T(2,128)(2,1)S(1)}, u32[]{:S(2)}, u32[]{:S(2)}) async-start(bf16[64,2,1152]{2,1,0:T(2,128)(2,1)} %get-tuple-element.15), calls=%async_computation | async-start | bytes 589824 | tf_op jit(solution)/shard_map/all_to_all | solution.py:288
  39.0 0.0 copy-done
  39.0 0.0 collective-permute-done.1.in2
  39.0 0.0 collective-permute-done.2.in3
  39.0 2.0 %align.1.own = bf16[512,1152]{1,0:T(8,128)(2,1)S(1)} custom-call(bf16[128,1152]{1,0:T(8,128)(2,1)S(1)} %get-tuple-element.9.in0, bf16[128,1152]{1,0:T(8,128)(2,1)S(1)} %collective-permute-done.in1, bf16[128,1152]{1,0:T(8,128)(2,1)S(1)} %collective-permute-done.1.in2, bf16[128,1152]{1,0:T(8,128)(2,1)S(1)} %collective-permute-done.2.in3, ...), custom_call_target="tpu_custom_call" | custom-call | flops 800000000 | bytes 4000000 | tf_op jit(solution)/shard_map/align/pallas_call | solution.py:293
  41.1 1.9 %collective-permute-start.3 = (bf16[512,1152]{1,0:T(8,128)(2,1)S(1)}, bf16[512,1152]{1,0:T(8,128)(2,1)S(1)}, u32[]{:S(2)}, u32[]{:S(2)}) collective-permute-start(bf16[512,1152]{1,0:T(8,128)(2,1)S(1)} %align.1.own), channel_id=1, source_target_pairs={{0,4},{4,0},{1,5},{5,1},{2,6},{6,2},{3,7},{7,3},{8,12},{12,8},{9,1... | collective-permute-start | bytes 3538952 | tf_op jit(solution)/shard_map/ppermute | solution.py:304
  43.0 13.2 %all-to-all-done = bf16[64,2,1152]{2,1,0:T(2,128)(2,1)S(1)} async-done(((bf16[64,2,1152]{2,1,0:T(2,128)(2,1)}), bf16[64,2,1152]{2,1,0:T(2,128)(2,1)S(1)}, u32[]{:S(2)}, u32[]{:S(2)}) %all-to-all-start) | async-done | bytes 294944 | tf_op jit(solution)/shard_map/all_to_all | solution.py:288
  56.2 0.1 reshape.33.refs
  56.3 0.1 pad_add_fusion.at_ref
  56.4 0.1 norms.1.norm
  56.5 0.0 collective-permute-done.3.other
  56.5 1.8 %score.1 = f32[16,24,128]{2,1,0:T(8,128)S(1)} custom-call(s32[2]{0:T(128)S(1)} %pad_add_fusion.at_ref, bf16[512,1152]{1,0:T(8,128)(2,1)S(1)} %align.1.own, bf16[512,1152]{1,0:T(8,128)(2,1)S(1)} %collective-permute-done.3.other, bf16[128,1152]{1,0:T(8,128)(2,1)S(1)} %reshape.33.refs, f32[128,128]{1,0:T(8,128)S(1)} %norms.1.norm), custom_call_target="tpu_custom_call" | custom-call | flops 600000000 | bytes 2000000 | tf_op jit(solution)/shard_map/score/pallas_call | solution.py:317
  58.3 13.9 %all_to_all.15.got = f32[16,24,128]{2,1,0:T(8,128)S(1)} all-to-all(f32[16,24,128]{2,1,0:T(8,128)S(1)} %score.1), channel_id=1, replica_groups=mesh['y'=4,'z'=16,'core'=2,'x'=4] {'x','y'}, dimensions={0} | all-to-all | bytes 393216 | tf_op jit(solution)/shard_map/all_to_all | solution.py:327
  72.2 1.1 %sum.1 = bf16[128,1152]{1,0:T(8,128)(2,1)S(1)} custom-call(s32[2]{0:T(128)S(1)} %pad_add_fusion.at_ref, f32[16,24,128]{2,1,0:T(8,128)S(1)} %all_to_all.15.got, bf16[512,1152]{1,0:T(8,128)(2,1)S(1)} %align.1.own, bf16[512,1152]{1,0:T(8,128)(2,1)S(1)} %collective-permute-done.3.other), custom_call_target="tpu_custom_call" | custom-call | flops 300000000 | bytes 3000000 | tf_op jit(solution)/shard_map/sum/pallas_call | solution.py:328
  73.3 0.1 reshape.34
  73.4 24.7 %all_to_all.16 = bf16[64,2,1152]{2,1,0:T(2,128)(2,1)S(1)} all-to-all(bf16[64,2,1152]{2,1,0:T(2,128)(2,1)S(1)} %reshape.34), channel_id=1, replica_groups=mesh['y'=4,'z'=16,'core'=2,'x'=4] {'y','z'}, dimensions={0} | all-to-all | bytes 589824 | tf_op jit(solution)/shard_map/all_to_all | solution.py:338
  98.2 0.1 reshape.35.got
  98.3 0.8 finish.1
  (4 shorter events, 0.1 us)
Async XLA Ops:
  0.6 38.3 %copy-start = (f32[25,16,128]{2,1,0:T(8,128)S(1)}, f32[25,16,128]{2,1,0:T(8,128)}, u32[]{:S(2)}) copy-start(f32[25,16,128]{2,1,0:T(8,128)} %param.13) | copy-start | bytes 614404
  3.3 15.2 %collective-permute-start = (bf16[128,1152]{1,0:T(8,128)(2,1)S(1)}, bf16[128,1152]{1,0:T(8,128)(2,1)S(1)}, u32[]{:S(2)}, u32[]{:S(2)}) collective-permute-start(bf16[128,1152]{1,0:T(8,128)(2,1)S(1)} %get-tuple-element.11), channel_id=1, source_target_pairs={{0,128},{128,256},{256,384},{384,0},{1,129},{129,257},{257,385},{3... | collective-permute-start | bytes 884744 | tf_op jit(solution)/shard_map/ppermute | solution.py:286
  6.8 32.3 %collective-permute-start.1 = (bf16[128,1152]{1,0:T(8,128)(2,1)S(1)}, bf16[128,1152]{1,0:T(8,128)(2,1)S(1)}, u32[]{:S(2)}, u32[]{:S(2)}) collective-permute-start(bf16[128,1152]{1,0:T(8,128)(2,1)S(1)} %get-tuple-element.13), channel_id=1, source_target_pairs={{0,256},{128,384},{256,0},{384,128},{1,257},{129,385},{257,1},{385... | collective-permute-start | bytes 884744 | tf_op jit(solution)/shard_map/ppermute | solution.py:286
  15.0 24.0 %collective-permute-start.2 = (bf16[128,1152]{1,0:T(8,128)(2,1)S(1)}, bf16[128,1152]{1,0:T(8,128)(2,1)S(1)}, u32[]{:S(2)}, u32[]{:S(2)}) collective-permute-start(bf16[128,1152]{1,0:T(8,128)(2,1)S(1)} %get-tuple-element.14), channel_id=1, source_target_pairs={{0,384},{128,0},{256,128},{384,256},{1,385},{129,1},{257,129},{385... | collective-permute-start | bytes 884744 | tf_op jit(solution)/shard_map/ppermute | solution.py:286
  18.4 37.7 %all-to-all-start = ((bf16[64,2,1152]{2,1,0:T(2,128)(2,1)}), bf16[64,2,1152]{2,1,0:T(2,128)(2,1)S(1)}, u32[]{:S(2)}, u32[]{:S(2)}) async-start(bf16[64,2,1152]{2,1,0:T(2,128)(2,1)} %get-tuple-element.15), calls=%async_computation | async-start | bytes 589824 | tf_op jit(solution)/shard_map/all_to_all | solution.py:288
  41.1 15.4 %collective-permute-start.3 = (bf16[512,1152]{1,0:T(8,128)(2,1)S(1)}, bf16[512,1152]{1,0:T(8,128)(2,1)S(1)}, u32[]{:S(2)}, u32[]{:S(2)}) collective-permute-start(bf16[512,1152]{1,0:T(8,128)(2,1)S(1)} %align.1.own), channel_id=1, source_target_pairs={{0,4},{4,0},{1,5},{5,1},{2,6},{6,2},{3,7},{7,3},{8,12},{12,8},{9,1... | collective-permute-start | bytes 3538952 | tf_op jit(solution)/shard_map/ppermute | solution.py:304

commit v7 on v6

--- a/solution.py
+++ b/solution.py
@@ -19,6 +19,7 @@
 WIDE = R_OWN * A
 FULL = WIDE + 128
 SHIFT_ROWS = 32
+CHUNKS = P_DEV // 16
 VMEM_LIMIT = 40 * 1024 * 1024
 
 
@@ -37,47 +38,65 @@
     return lax.broadcasted_iota(jnp.int32, shape, axis)
 
 
+def step_of(slot, core):
+    return (slot * (1 + 2 * core)) & (NY - 1)
+
+
 def deal_kernel(
-    y_ref,
+    at_ref,
     images_hbm,
-    refs_hbm,
     label_hbm,
     rot_hbm,
     shift_hbm,
-    sharp_hbm,
-    pieces,
     out0,
     out1,
     out2,
     out3,
     images,
-    refs,
     ints,
-    sharp,
-    row_of,
     grid,
     sems,
 ):
-    y = y_ref[0]
-    copies = [
-        pltpu.make_async_copy(source, target, sems.at[at])
-        for at, (source, target) in enumerate(
-            (
-                (refs_hbm, refs),
-                (label_hbm, ints.at[pl.ds(0, 1)]),
-                (rot_hbm, ints.at[pl.ds(1, 1)]),
-                (shift_hbm, ints.at[pl.ds(2, 1)]),
-                (sharp_hbm, sharp),
-            )
-        )
-    ]
-    quarter = P_DEV * R_DEV // 4
-    for i in range(4):
-        rows = pl.ds(i * quarter, quarter)
-        copies.append(pltpu.make_async_copy(images_hbm.at[rows], images.at[rows], sems.at[5 + i]))
+    y, core = at_ref[0], at_ref[1]
+    part = P_DEV * R_DEV // CHUNKS
+    copies = []
+    for i in range(CHUNKS):
+        rows = pl.ds(i * part, part)
+        copies.append(pltpu.make_async_copy(images_hbm.at[rows], images.at[rows], sems.at[3 + i]))
+    for i, source in enumerate((label_hbm, rot_hbm, shift_hbm)):
+        copies.append(pltpu.make_async_copy(source, ints.at[pl.ds(i, 1)], sems.at[i]))
     for copy in copies:
         copy.start()
-    for copy in copies[:5]:
+    row, col = iota((A, A), 0), iota((A, A), 1)
+    swap = (col == ((row & 15) * 16 + (row >> 4))).astype(jnp.float32).astype(jnp.bfloat16)
+    for b in range(P_DEV // 16):
+        copies[b].wait()
+        x = jnp.dot(swap, images[b * A : b * A + A, :], preferred_element_type=jnp.float32)
+        x = x.astype(jnp.bfloat16)
+        for r in range(R_DEV):
+            grid[r, b * 16 : b * 16 + 16, :] = x[r * 16 : r * 16 + 16]
+    for copy in copies[CHUNKS:]:
+        copy.wait()
+    label = ints[0:1, :]
+    label = ((label >> 1) & 1) * 128 + (label >> 2) * 2 + (label & 1)
+    at = iota((P_DEV, P_DEV), 0)
+    tail = jnp.where(at == 0, label, jnp.where(at == 1, ints[1:2, :], ints[2:3, :]))
+    tail = tail.astype(jnp.float32).astype(jnp.bfloat16)
+    for slot, out in enumerate((out0, out1, out2, out3)):
+        first = ((y + step_of(slot, core)) & (NY - 1)) * R_OWN
+        for i in range(R_OWN):
+            out[:, i * A : i * A + A] = grid[first + i]
+        out[:, WIDE:] = tail
+
+
+def pieces_kernel(refs_hbm, sharp_hbm, pieces, refs, sharp, row_of, sems):
+    copies = [
+        pltpu.make_async_copy(refs_hbm, refs, sems.at[0]),
+        pltpu.make_async_copy(sharp_hbm, sharp, sems.at[1]),
+    ]
+    for copy in copies:
+        copy.start()
+    for copy in copies:
         copy.wait()
     for j in range(2):
         wide = refs[j].astype(jnp.float32)
@@ -92,25 +111,6 @@
         pair = row_of[2 * r : 2 * r + 2, :].astype(jnp.bfloat16)
         for z in range(NZ):
             pieces[r * NZ + z] = pair
-    row, col = iota((A, A), 0), iota((A, A), 1)
-    swap = (col == ((row & 15) * 16 + (row >> 4))).astype(jnp.float32).astype(jnp.bfloat16)
-    for b in range(P_DEV // 16):
-        if b % 2 == 0:
-            copies[5 + b // 2].wait()
-        x = jnp.dot(swap, images[b * A : b * A + A, :], preferred_element_type=jnp.float32)
-        x = x.astype(jnp.bfloat16)
-        for r in range(R_DEV):
-            grid[r, b * 16 : b * 16 + 16, :] = x[r * 16 : r * 16 + 16]
-    label = ints[0:1, :]
-    label = ((label >> 1) & 1) * 128 + (label >> 2) * 2 + (label & 1)
-    at = iota((P_DEV, P_DEV), 0)
-    tail = jnp.where(at == 0, label, jnp.where(at == 1, ints[1:2, :], ints[2:3, :]))
-    tail = tail.astype(jnp.float32).astype(jnp.bfloat16)
-    for d, out in enumerate((out0, out1, out2, out3)):
-        first = ((y + d) & (NY - 1)) * R_OWN
-        for i in range(R_OWN):
-            out[:, i * A : i * A + A] = grid[first + i]
-        out[:, WIDE:] = tail
 
 
 def align_kernel(in0, in1, in2, in3, table, phases, out, parts):
@@ -165,7 +165,7 @@
     diagonal = class_of == iota((P_DEV, P_DEV), 1)
     for side, rows in enumerate((own, other)):
         for d in range(NY):
-            source = (y - d) & (NY - 1)
+            source = (y - step_of(d, core ^ side)) & (NY - 1)
             flat = rows[d * P_DEV : d * P_DEV + P_DEV, :WIDE]
             member = class_of == labels_of(rows, d * P_DEV, core)
             scores = lax.dot_general(
@@ -196,7 +196,7 @@
     for side, rows in enumerate((own, other)):
         parts = []
         for d in range(NY):
-            source = (y - d) & (NY - 1)
+            source = (y - step_of(d, core ^ side)) & (NY - 1)
             member = iota((P_DEV, P_DEV), 0) == labels_of(rows, d * P_DEV, core)
             weight = weights[pl.ds(side * NY + source, 1), :]
             parts.append(jnp.where(member, weight, 0.0).astype(jnp.bfloat16))
@@ -249,45 +249,58 @@
     core = lax.axis_index("core").astype(jnp.int32)
     shape = jax.ShapeDtypeStruct
 
+    def in_hbm(*arrays):
+        return [pltpu.with_memory_space_constraint(x, pltpu.HBM) for x in arrays]
+
+    at = jnp.stack([y, core])
     block = shape((P_DEV, FULL), jnp.bfloat16)
-    pieces, *dealt = call(
+    dealt = call(
         deal_kernel,
         "deal",
-        [shape((NY * NZ, 2, FULL), jnp.bfloat16)] + [block] * NY,
+        [block] * NY,
         [
             pltpu.VMEM((P_DEV * R_DEV, A), jnp.bfloat16),
-            pltpu.VMEM((2, R_DEV, A), jnp.bfloat16),
             pltpu.VMEM((8, P_DEV), jnp.int32),
-            pltpu.VMEM((1, 2), jnp.bfloat16),
-            pltpu.VMEM((2 * NY, FULL), jnp.float32),
             pltpu.VMEM((R_DEV, P_DEV, A), jnp.bfloat16),
-            pltpu.SemaphoreType.DMA((9,)),
+            pltpu.SemaphoreType.DMA((3 + CHUNKS,)),
         ],
         300_000_000,
         3_000_000,
-        [SMEM] + [HBM] * 6,
-        [VMEM] * (1 + NY),
+        [SMEM] + [HBM] * 4,
+        [VMEM] * NY,
     )(
-        y[None],
-        *[
-            pltpu.with_memory_space_constraint(x, pltpu.HBM)
-            for x in (
-                images.reshape(P_DEV * R_DEV, A),
-                references,
-                classes.reshape(1, P_DEV),
-                rotations.reshape(1, P_DEV),
-                shifts.reshape(1, P_DEV),
-                sharpness.reshape(1, 2),
-            )
-        ],
+        at,
+        *in_hbm(
+            images.reshape(P_DEV * R_DEV, A),
+            classes.reshape(1, P_DEV),
+            rotations.reshape(1, P_DEV),
+            shifts.reshape(1, P_DEV),
+        ),
     )
     blocks = [dealt[0]]
-    for d in range(1, NY):
-        blocks.append(lax.ppermute(dealt[d], "y", [(i, (i + d) % NY) for i in range(NY)]))
+    for slot in range(1, NY):
+        pairs = [
+            (2 * i + c, 2 * ((i + step_of(slot, c)) % NY) + c) for i in range(NY) for c in range(2)
+        ]
+        blocks.append(lax.ppermute(dealt[slot], ("y", "core"), pairs))
+
+    pieces = call(
+        pieces_kernel,
+        "pieces",
+        shape((NY * NZ, 2, FULL), jnp.bfloat16),
+        [
+            pltpu.VMEM((2, R_DEV, A), jnp.bfloat16),
+            pltpu.VMEM((1, 2), jnp.bfloat16),
+            pltpu.VMEM((2 * NY, FULL), jnp.float32),
+            pltpu.SemaphoreType.DMA((2,)),
+        ],
+        1_000_000,
+        500_000,
+        [HBM] * 2,
+        VMEM,
+    )(*in_hbm(references, sharpness.reshape(1, 2)))
     pieces, blocks[1] = lax.optimization_barrier((pieces, blocks[1]))
-    panel = lax.all_to_all(
-        pieces, ("y", "z"), split_axis=0, concat_axis=0, tiled=True
-    )
+    panel = lax.all_to_all(pieces, ("y", "z"), split_axis=0, concat_axis=0, tiled=True)
     phases = lax.dynamic_slice_in_dim(shift_phase, y * R_OWN, R_OWN, 1).transpose(1, 0, 2)
     phases = jnp.pad(phases, ((0, 0), (0, SHIFT_ROWS - 25), (0, 0)))
     rows = call(
@@ -302,14 +315,13 @@
     )(*blocks, spectral_table(A), phases)
 
     other = lax.ppermute(rows, "core", [(0, 1), (1, 0)])
-    at = jnp.stack([y, core])
     panel = panel.reshape(NY * NZ * 2, FULL)
     norm = call(
         norm_kernel,
         "norms",
         shape((P_DEV, P_DEV), jnp.float32),
         [],
-        300_000,
+        1_000_000_000,
         300_000,
         [VMEM],
         VMEM,

time: 99.4 us -> 107 us (1.076)
  blocking collectives: 38.6 us -> 42.9 us
  starting transfers between devices: 36 us -> 33.3 us
  waiting for transfers between devices: 14.2 us -> 16.7 us
  Pallas kernels: 8.48 us -> 10.8 us
    all_to_all x1, starting transfers between devices: 20.5 us -> 16.4 us  [body(): lax.all_to_all(pieces, ('y', 'z'), split_axis=0, concat_axis=0, tiled=True)]
    all_to_all x1, blocking collectives: 24.7 us -> 28.2 us  [body(): lax.all_to_all(sums.reshape(NY * NZ, 2, FULL), ('y', 'z'), split_axis=0,...]
    all_to_all x1, waiting for transfers between devices: 13.2 us -> 16.7 us  [body(): lax.all_to_all(pieces, ('y', 'z'), split_axis=0, concat_axis=0, tiled=True)]
    pallas_call x2 -> x3, Pallas kernels: 2.74 us -> 5.05 us  [the longest x1 3.37 us: body(): call(deal_kernel, 'deal', [block] * NY, [pltpu.VMEM((P_DEV * R_DEV, A), j...]
    ppermute x1, starting transfers between devices: 1.92 us -> 3.3 us  [body(): other = lax.ppermute(rows, 'core', [(0, 1), (1, 0)])]
  transfers between devices with their start and end apart: 5 -> 5, of which waited for: 2 -> 1; matrix products, arithmetic and copies ran while one was open for 1% -> 2% of each run, Pallas kernels for 2% -> 3%
where the time goes in v7:
time: 107 us; the launch traced here: 106 us
  blocking collectives  42.9 us (40%)
  starting transfers between devices  33.3 us (31%)
  waiting for transfers between devices  16.7 us (16%)
  Pallas kernels  10.8 us (10%)
  local copies, waits for them, and re-layouts  1.34 us (1%)
    all_to_all x1, blocking collectives, body(): lax.all_to_all(sums.reshape(NY * NZ, 2, FULL), ('y', 'z'), split_axis=0,...  28.2 us
    all_to_all x1, waiting for transfers between devices, body(): lax.all_to_all(pieces, ('y', 'z'), split_axis=0, concat_axis=0, tiled=True)  16.7 us
    all_to_all x1, starting transfers between devices, body(): lax.all_to_all(pieces, ('y', 'z'), split_axis=0, concat_axis=0, tiled=True)  16.4 us
    all_to_all x1, blocking collectives, body(): lax.all_to_all(payload, ('x', 'y'), split_axis=0, concat_axis=0, tiled=True)  14.7 us
    ppermute x3, starting transfers between devices, body(): blocks.append(lax.ppermute(dealt[slot], ('y', 'core'), pairs))  13.6 us
    pallas_call x1, Pallas kernels, body(): call(deal_kernel, 'deal', [block] * NY, [pltpu.VMEM((P_DEV * R_DEV, A), j...  3.37 us
    ppermute x1, starting transfers between devices, body(): other = lax.ppermute(rows, 'core', [(0, 1), (1, 0)])  3.3 us
  transfers between devices with their start and end apart: 5, of which 1 were waited for; matrix products, arithmetic and copies ran while one was open for 2% of the time, Pallas kernels for 3%

profile of v7, /device:TPU:8, one launch (start us, length us, event | category | flops | bytes accessed | tf_op | source)
XLA Modules:
  0.0 106.5 jit_solution(11558052945395259709)
XLA Ops:
  0.6 0.0 copy-start
  0.6 0.1 pad_add_fusion.at_ref
  0.7 3.4 %deal.1 = (bf16[128,1152]{1,0:T(8,128)(2,1)S(1)}, bf16[128,1152]{1,0:T(8,128)(2,1)S(1)}, bf16[128,1152]{1,0:T(8,128)(2,1)S(1)}, bf16[128,1152]{1,0:T(8,128)(2,1)S(1)}) custom-call(s32[2]{0:T(128)S(1)} %pad_add_fusion.at_ref, bf16[2048,256]{1,0:T(8,128)(2,1)} %bitcast.12, s32[1,128]{1,0:T(1,128)} %bitcast.13, s32[1,128]{1,0:T(1,128)} %bitcast.14, ...), custom_call_target="tpu_custom_call" | custom-call | flops 300000000 | bytes 3000000 | tf_op jit(solution)/shard_map/deal/pallas_call | solution.py:257
  4.1 3.5 %collective-permute-start = (bf16[128,1152]{1,0:T(8,128)(2,1)S(1)}, bf16[128,1152]{1,0:T(8,128)(2,1)S(1)}, u32[]{:S(2)}, u32[]{:S(2)}) collective-permute-start(bf16[128,1152]{1,0:T(8,128)(2,1)S(1)} %get-tuple-element.9), channel_id=1, source_target_pairs={{0,128},{4,388},{128,256},{132,4},{256,384},{260,132},{384,0},{388... | collective-permute-start | bytes 884744 | tf_op jit(solution)/shard_map/ppermute | solution.py:285
  7.6 8.2 %collective-permute-start.1 = (bf16[128,1152]{1,0:T(8,128)(2,1)S(1)}, bf16[128,1152]{1,0:T(8,128)(2,1)S(1)}, u32[]{:S(2)}, u32[]{:S(2)}) collective-permute-start(bf16[128,1152]{1,0:T(8,128)(2,1)S(1)} %get-tuple-element.11), channel_id=1, source_target_pairs={{0,256},{4,260},{128,384},{132,388},{256,0},{260,4},{384,128},{388... | collective-permute-start | bytes 884744 | tf_op jit(solution)/shard_map/ppermute | solution.py:285
  15.8 1.9 %collective-permute-start.2 = (bf16[128,1152]{1,0:T(8,128)(2,1)S(1)}, bf16[128,1152]{1,0:T(8,128)(2,1)S(1)}, u32[]{:S(2)}, u32[]{:S(2)}) collective-permute-start(bf16[128,1152]{1,0:T(8,128)(2,1)S(1)} %get-tuple-element.12), channel_id=1, source_target_pairs={{0,384},{4,132},{128,0},{132,260},{256,128},{260,388},{384,256},{3... | collective-permute-start | bytes 884744 | tf_op jit(solution)/shard_map/ppermute | solution.py:285
  17.8 1.5 %pieces.1 = bf16[64,2,1152]{2,1,0:T(2,128)(2,1)} custom-call(bf16[2,16,256]{2,1,0:T(8,128)(2,1)} %refs_hbm.1, bf16[1,2]{1,0:T(2,128)(2,1)} %bitcast.11), custom_call_target="tpu_custom_call" | custom-call | flops 1000000 | bytes 500000 | tf_op jit(solution)/shard_map/pieces/pallas_call | solution.py:287
  19.3 0.0 copy-done
  19.4 0.5 sine_negate_fusion
  19.9 0.0 collective-permute-done.in1
  19.9 16.4 %all-to-all-start = ((bf16[64,2,1152]{2,1,0:T(2,128)(2,1)}), bf16[64,2,1152]{2,1,0:T(2,128)(2,1)}, u32[]{:S(2)}, u32[]{:S(2)}) async-start(bf16[64,2,1152]{2,1,0:T(2,128)(2,1)} %pieces.1), calls=%async_computation | async-start | bytes 589824 | tf_op jit(solution)/shard_map/all_to_all | solution.py:303
  36.4 0.0 collective-permute-done.1.in2
  36.4 0.0 collective-permute-done.2.in3
  36.4 2.0 %align.1.own = bf16[512,1152]{1,0:T(8,128)(2,1)S(1)} custom-call(bf16[128,1152]{1,0:T(8,128)(2,1)S(1)} %get-tuple-element.8.in0, bf16[128,1152]{1,0:T(8,128)(2,1)S(1)} %collective-permute-done.in1, bf16[128,1152]{1,0:T(8,128)(2,1)S(1)} %collective-permute-done.1.in2, bf16[128,1152]{1,0:T(8,128)(2,1)S(1)} %collective-permute-done.2.in3, ...), custom_call_target="tpu_custom_call" | custom-call | flops 800000000 | bytes 4000000 | tf_op jit(solution)/shard_map/align/pallas_call | solution.py:306
  38.4 3.3 %collective-permute-start.3 = (bf16[512,1152]{1,0:T(8,128)(2,1)S(1)}, bf16[512,1152]{1,0:T(8,128)(2,1)S(1)}, u32[]{:S(2)}, u32[]{:S(2)}) collective-permute-start(bf16[512,1152]{1,0:T(8,128)(2,1)S(1)} %align.1.own), channel_id=1, source_target_pairs={{0,4},{4,0},{1,5},{5,1},{2,6},{6,2},{3,7},{7,3},{8,12},{12,8},{9,1... | collective-permute-start | bytes 3538952 | tf_op jit(solution)/shard_map/ppermute | solution.py:317
  41.7 16.7 %all-to-all-done = bf16[64,2,1152]{2,1,0:T(2,128)(2,1)} async-done(((bf16[64,2,1152]{2,1,0:T(2,128)(2,1)}), bf16[64,2,1152]{2,1,0:T(2,128)(2,1)}, u32[]{:S(2)}, u32[]{:S(2)}) %all-to-all-start) | async-done | bytes 294944 | tf_op jit(solution)/shard_map/all_to_all | solution.py:303
  58.4 1.1 %reshape.33.refs = bf16[128,1152]{1,0:T(8,128)(2,1)S(1)} reshape(bf16[64,2,1152]{2,1,0:T(2,128)(2,1)} %all-to-all-done) | data formatting | bytes 589824 | tf_op jit(solution)/shard_map/reshape | solution.py:318
  59.5 0.1 norms.1.norm
  59.6 0.0 collective-permute-done.3.other
  59.6 1.8 %score.1 = f32[16,24,128]{2,1,0:T(8,128)S(1)} custom-call(s32[2]{0:T(128)S(1)} %pad_add_fusion.at_ref, bf16[512,1152]{1,0:T(8,128)(2,1)S(1)} %align.1.own, bf16[512,1152]{1,0:T(8,128)(2,1)S(1)} %collective-permute-done.3.other, bf16[128,1152]{1,0:T(8,128)(2,1)S(1)} %reshape.33.refs, f32[128,128]{1,0:T(8,128)S(1)} %norms.1.norm), custom_call_target="tpu_custom_call" | custom-call | flops 600000000 | bytes 2000000 | tf_op jit(solution)/shard_map/score/pallas_call | solution.py:329
  61.4 14.7 %all_to_all.15.got = f32[16,24,128]{2,1,0:T(8,128)S(1)} all-to-all(f32[16,24,128]{2,1,0:T(8,128)S(1)} %score.1), channel_id=1, replica_groups=mesh['y'=4,'z'=16,'core'=2,'x'=4] {'x','y'}, dimensions={0} | all-to-all | bytes 393216 | tf_op jit(solution)/shard_map/all_to_all | solution.py:339
  76.1 1.1 %sum.1 = bf16[128,1152]{1,0:T(8,128)(2,1)S(1)} custom-call(s32[2]{0:T(128)S(1)} %pad_add_fusion.at_ref, f32[16,24,128]{2,1,0:T(8,128)S(1)} %all_to_all.15.got, bf16[512,1152]{1,0:T(8,128)(2,1)S(1)} %align.1.own, bf16[512,1152]{1,0:T(8,128)(2,1)S(1)} %collective-permute-done.3.other), custom_call_target="tpu_custom_call" | custom-call | flops 300000000 | bytes 3000000 | tf_op jit(solution)/shard_map/sum/pallas_call | solution.py:340
  77.2 0.1 reshape.34
  77.3 28.2 %all_to_all.16 = bf16[64,2,1152]{2,1,0:T(2,128)(2,1)S(1)} all-to-all(bf16[64,2,1152]{2,1,0:T(2,128)(2,1)S(1)} %reshape.34), channel_id=1, replica_groups=mesh['y'=4,'z'=16,'core'=2,'x'=4] {'y','z'}, dimensions={0} | all-to-all | bytes 589824 | tf_op jit(solution)/shard_map/all_to_all | solution.py:350
  105.6 0.1 reshape.35.got
  105.7 0.8 finish.1
  (4 shorter events, 0.1 us)
Async XLA Ops:
  0.6 18.7 %copy-start = (f32[25,16,128]{2,1,0:T(8,128)S(1)}, f32[25,16,128]{2,1,0:T(8,128)}, u32[]{:S(2)}) copy-start(f32[25,16,128]{2,1,0:T(8,128)} %param.13) | copy-start | bytes 614404
  4.1 15.8 %collective-permute-start = (bf16[128,1152]{1,0:T(8,128)(2,1)S(1)}, bf16[128,1152]{1,0:T(8,128)(2,1)S(1)}, u32[]{:S(2)}, u32[]{:S(2)}) collective-permute-start(bf16[128,1152]{1,0:T(8,128)(2,1)S(1)} %get-tuple-element.9), channel_id=1, source_target_pairs={{0,128},{4,388},{128,256},{132,4},{256,384},{260,132},{384,0},{388... | collective-permute-start | bytes 884744 | tf_op jit(solution)/shard_map/ppermute | solution.py:285
  7.6 28.8 %collective-permute-start.1 = (bf16[128,1152]{1,0:T(8,128)(2,1)S(1)}, bf16[128,1152]{1,0:T(8,128)(2,1)S(1)}, u32[]{:S(2)}, u32[]{:S(2)}) collective-permute-start(bf16[128,1152]{1,0:T(8,128)(2,1)S(1)} %get-tuple-element.11), channel_id=1, source_target_pairs={{0,256},{4,260},{128,384},{132,388},{256,0},{260,4},{384,128},{388... | collective-permute-start | bytes 884744 | tf_op jit(solution)/shard_map/ppermute | solution.py:285
  15.8 20.5 %collective-permute-start.2 = (bf16[128,1152]{1,0:T(8,128)(2,1)S(1)}, bf16[128,1152]{1,0:T(8,128)(2,1)S(1)}, u32[]{:S(2)}, u32[]{:S(2)}) collective-permute-start(bf16[128,1152]{1,0:T(8,128)(2,1)S(1)} %get-tuple-element.12), channel_id=1, source_target_pairs={{0,384},{4,132},{128,0},{132,260},{256,128},{260,388},{384,256},{3... | collective-permute-start | bytes 884744 | tf_op jit(solution)/shard_map/ppermute | solution.py:285
  19.9 38.5 %all-to-all-start = ((bf16[64,2,1152]{2,1,0:T(2,128)(2,1)}), bf16[64,2,1152]{2,1,0:T(2,128)(2,1)}, u32[]{:S(2)}, u32[]{:S(2)}) async-start(bf16[64,2,1152]{2,1,0:T(2,128)(2,1)} %pieces.1), calls=%async_computation | async-start | bytes 589824 | tf_op jit(solution)/shard_map/all_to_all | solution.py:303
  38.4 21.2 %collective-permute-start.3 = (bf16[512,1152]{1,0:T(8,128)(2,1)S(1)}, bf16[512,1152]{1,0:T(8,128)(2,1)S(1)}, u32[]{:S(2)}, u32[]{:S(2)}) collective-permute-start(bf16[512,1152]{1,0:T(8,128)(2,1)S(1)} %align.1.own), channel_id=1, source_target_pairs={{0,4},{4,0},{1,5},{5,1},{2,6},{6,2},{3,7},{7,3},{8,12},{12,8},{9,1... | collective-permute-start | bytes 3538952 | tf_op jit(solution)/shard_map/ppermute | solution.py:317

commit v8 on v6

--- a/solution.py
+++ b/solution.py
@@ -39,18 +39,18 @@
 
 def deal_kernel(
     y_ref,
-    images_hbm,
+    images,
     refs_hbm,
     label_hbm,
     rot_hbm,
     shift_hbm,
     sharp_hbm,
     pieces,
+    head,
     out0,
     out1,
     out2,
     out3,
-    images,
     refs,
     ints,
     sharp,
@@ -71,13 +71,9 @@
             )
         )
     ]
-    quarter = P_DEV * R_DEV // 4
-    for i in range(4):
-        rows = pl.ds(i * quarter, quarter)
-        copies.append(pltpu.make_async_copy(images_hbm.at[rows], images.at[rows], sems.at[5 + i]))
     for copy in copies:
         copy.start()
-    for copy in copies[:5]:
+    for copy in copies:
         copy.wait()
     for j in range(2):
         wide = refs[j].astype(jnp.float32)
@@ -95,8 +91,6 @@
     row, col = iota((A, A), 0), iota((A, A), 1)
     swap = (col == ((row & 15) * 16 + (row >> 4))).astype(jnp.float32).astype(jnp.bfloat16)
     for b in range(P_DEV // 16):
-        if b % 2 == 0:
-            copies[5 + b // 2].wait()
         x = jnp.dot(swap, images[b * A : b * A + A, :], preferred_element_type=jnp.float32)
         x = x.astype(jnp.bfloat16)
         for r in range(R_DEV):
@@ -106,6 +100,7 @@
     at = iota((P_DEV, P_DEV), 0)
     tail = jnp.where(at == 0, label, jnp.where(at == 1, ints[1:2, :], ints[2:3, :]))
     tail = tail.astype(jnp.float32).astype(jnp.bfloat16)
+    head[...] = tail[:16]
     for d, out in enumerate((out0, out1, out2, out3)):
         first = ((y + d) & (NY - 1)) * R_OWN
         for i in range(R_OWN):
@@ -146,8 +141,8 @@
         out[rows, WIDE:] = block[:, WIDE:]
 
 
-def labels_of(rows, first, core):
-    label = rows[first : first + 16, WIDE:].astype(jnp.float32)[0:1].astype(jnp.int32)
+def labels_of(tail, core):
+    label = tail.astype(jnp.float32)[0:1].astype(jnp.int32)
     return label ^ (core * P_DEV)
 
 
@@ -157,7 +152,7 @@
     out[...] = jnp.broadcast_to(norm, (P_DEV, P_DEV))
 
 
-def score_kernel(at_ref, own, other, refs, norm, out, stats):
+def score_kernel(at_ref, own, other, head, refs, norm, out, stats):
     y, core = at_ref[0], at_ref[1]
     flat_refs = refs[:, :WIDE]
     sharp = refs[:, WIDE:].astype(jnp.float32)
@@ -167,7 +162,8 @@
         for d in range(NY):
             source = (y - d) & (NY - 1)
             flat = rows[d * P_DEV : d * P_DEV + P_DEV, :WIDE]
-            member = class_of == labels_of(rows, d * P_DEV, core)
+            tail = rows[d * P_DEV : d * P_DEV + 16, WIDE:] if (side, d) != (1, 0) else head[...]
+            member = class_of == labels_of(tail, core)
             scores = lax.dot_general(
                 flat_refs, flat, (((1,), (1,)), ((), ())), preferred_element_type=jnp.float32
             )
@@ -197,7 +193,9 @@
         parts = []
         for d in range(NY):
             source = (y - d) & (NY - 1)
-            member = iota((P_DEV, P_DEV), 0) == labels_of(rows, d * P_DEV, core)
+            member = iota((P_DEV, P_DEV), 0) == labels_of(
+                rows[d * P_DEV : d * P_DEV + 16, WIDE:], core
+            )
             weight = weights[pl.ds(side * NY + source, 1), :]
             parts.append(jnp.where(member, weight, 0.0).astype(jnp.bfloat16))
         spread.append(jnp.concatenate(parts, axis=1))
@@ -250,29 +248,28 @@
     shape = jax.ShapeDtypeStruct
 
     block = shape((P_DEV, FULL), jnp.bfloat16)
-    pieces, *dealt = call(
+    pieces, head, *dealt = call(
         deal_kernel,
         "deal",
-        [shape((NY * NZ, 2, FULL), jnp.bfloat16)] + [block] * NY,
+        [shape((NY * NZ, 2, FULL), jnp.bfloat16), shape((16, P_DEV), jnp.bfloat16)] + [block] * NY,
         [
-            pltpu.VMEM((P_DEV * R_DEV, A), jnp.bfloat16),
             pltpu.VMEM((2, R_DEV, A), jnp.bfloat16),
             pltpu.VMEM((8, P_DEV), jnp.int32),
             pltpu.VMEM((1, 2), jnp.bfloat16),
             pltpu.VMEM((2 * NY, FULL), jnp.float32),
             pltpu.VMEM((R_DEV, P_DEV, A), jnp.bfloat16),
-            pltpu.SemaphoreType.DMA((9,)),
+            pltpu.SemaphoreType.DMA((5,)),
         ],
         300_000_000,
         3_000_000,
-        [SMEM] + [HBM] * 6,
-        [VMEM] * (1 + NY),
+        [SMEM, VMEM] + [HBM] * 5,
+        [VMEM] * (2 + NY),
     )(
         y[None],
+        images.reshape(P_DEV * R_DEV, A),
         *[
             pltpu.with_memory_space_constraint(x, pltpu.HBM)
             for x in (
-                images.reshape(P_DEV * R_DEV, A),
                 references,
                 classes.reshape(1, P_DEV),
                 rotations.reshape(1, P_DEV),
@@ -281,10 +278,11 @@
             )
         ],
     )
+    head = lax.ppermute(head, "core", [(0, 1), (1, 0)])
     blocks = [dealt[0]]
     for d in range(1, NY):
         blocks.append(lax.ppermute(dealt[d], "y", [(i, (i + d) % NY) for i in range(NY)]))
-    pieces, blocks[1] = lax.optimization_barrier((pieces, blocks[1]))
+    pieces, head = lax.optimization_barrier((pieces, head))
     panel = lax.all_to_all(
         pieces, ("y", "z"), split_axis=0, concat_axis=0, tiled=True
     )
@@ -321,9 +319,9 @@
         [pltpu.VMEM((6 * NY, P_DEV), jnp.float32)],
         600_000_000,
         2_000_000,
-        [SMEM] + [VMEM] * 4,
+        [SMEM] + [VMEM] * 5,
         VMEM,
-    )(at, rows, other, panel, norm)
+    )(at, rows, other, head, panel, norm)
     got = lax.all_to_all(payload, ("x", "y"), split_axis=0, concat_axis=0, tiled=True)
     sums = call(
         sum_kernel,

time: 99.4 us -> 101 us (1.016)
  starting transfers between devices: 36 us -> 31.6 us
  waiting for transfers between devices: 14.2 us -> 18 us
  local copies, waits for them, and re-layouts: 0.38 us -> 1.64 us
  blocking collectives: 38.6 us -> 39.7 us
    all_to_all x1, starting transfers between devices: 20.5 us -> 14.2 us  [body(): lax.all_to_all(pieces, ('y', 'z'), split_axis=0, concat_axis=0, tiled=True)]
    all_to_all x1, waiting for transfers between devices: 13.2 us -> 18 us  [body(): lax.all_to_all(pieces, ('y', 'z'), split_axis=0, concat_axis=0, tiled=True)]
    ppermute x0 -> x1, starting transfers between devices: none -> 1.92 us  [body(): head = lax.ppermute(head, 'core', [(0, 1), (1, 0)])]
    unnamed x3 -> x5, local copies, waits for them, and re-layouts: 0.02 us -> 1.27 us
    all_to_all x1, blocking collectives: 24.7 us -> 25.9 us  [body(): lax.all_to_all(sums.reshape(NY * NZ, 2, FULL), ('y', 'z'), split_axis=0,...]
  transfers between devices with their start and end apart: 5 -> 6, of which waited for: 2 -> 1; matrix products, arithmetic and copies ran while one was open for 1% -> 1% of each run, Pallas kernels for 2% -> 2%
where the time goes in v8:
time: 101 us; the launch traced here: 100 us
  blocking collectives  39.7 us (39%)
  starting transfers between devices  31.6 us (31%)
  waiting for transfers between devices  18 us (18%)
  Pallas kernels  7.79 us (8%)
  local copies, waits for them, and re-layouts  1.64 us (2%)
    all_to_all x1, blocking collectives, body(): lax.all_to_all(sums.reshape(NY * NZ, 2, FULL), ('y', 'z'), split_axis=0,...  25.9 us
    all_to_all x1, waiting for transfers between devices, body(): lax.all_to_all(pieces, ('y', 'z'), split_axis=0, concat_axis=0, tiled=True)  18 us
    all_to_all x1, starting transfers between devices, body(): lax.all_to_all(pieces, ('y', 'z'), split_axis=0, concat_axis=0, tiled=True)  14.2 us
    all_to_all x1, blocking collectives, body(): lax.all_to_all(payload, ('x', 'y'), split_axis=0, concat_axis=0, tiled=True)  13.8 us
    ppermute x3, starting transfers between devices, body(): lax.ppermute(dealt[d], 'y', [(i, (i + d) % NY) for i in range(NY)])  13.6 us
  transfers between devices with their start and end apart: 6, of which 1 were waited for; matrix products, arithmetic and copies ran while one was open for 1% of the time, Pallas kernels for 2%

profile of v8, /device:TPU:8, one launch (start us, length us, event | category | flops | bytes accessed | tf_op | source)
XLA Modules:
  0.0 100.2 jit_solution(3523931803563405181)
XLA Ops:
  0.6 0.0 copy-start
  0.7 0.0 copy-start.1
  0.7 1.3 %copy-done.1 = bf16[128,16,256]{2,1,0:T(8,128)(2,1)S(1)} copy-done((bf16[128,16,256]{2,1,0:T(8,128)(2,1)S(1)}, bf16[128,16,256]{2,1,0:T(8,128)(2,1)}, u32[]{:S(2)}) %copy-start.1) | copy-done | bytes 1048600
  1.9 1.9 %deal.1 = (bf16[64,2,1152]{2,1,0:T(2,128)(2,1)}, bf16[16,128]{1,0:T(8,128)(2,1)S(1)}, bf16[128,1152]{1,0:T(8,128)(2,1)S(1)}, bf16[128,1152]{1,0:T(8,128)(2,1)S(1...) custom-call(s32[1]{0:T(128)} %bitcast.y_ref, bf16[2048,256]{1,0:T(8,128)(2,1)S(1)} %bitcast.10, ...), custom_call_target="tpu_custom_call" | custom-call | flops 300000000 | bytes 3000000 | tf_op jit(solution)/shard_map/deal/pallas_call | solution.py:251
  3.9 1.9 %collective-permute-start.4 = (bf16[16,128]{1,0:T(8,128)(2,1)S(1)}, bf16[16,128]{1,0:T(8,128)(2,1)S(1)}, u32[]{:S(2)}, u32[]{:S(2)}) collective-permute-start(bf16[16,128]{1,0:T(8,128)(2,1)S(1)} %get-tuple-element.15), channel_id=1, source_target_pairs={{0,4},{4,0},{1,5},{5,1},{2,6},{6,2},{3,7},{7,3},{8,12},{12,8},{9,1... | collective-permute-start | bytes 12296 | tf_op jit(solution)/shard_map/ppermute | solution.py:281
  5.8 3.5 %collective-permute-start = (bf16[128,1152]{1,0:T(8,128)(2,1)S(1)}, bf16[128,1152]{1,0:T(8,128)(2,1)S(1)}, u32[]{:S(2)}, u32[]{:S(2)}) collective-permute-start(bf16[128,1152]{1,0:T(8,128)(2,1)S(1)} %get-tuple-element.11), channel_id=1, source_target_pairs={{0,128},{128,256},{256,384},{384,0},{1,129},{129,257},{257,385},{3... | collective-permute-start | bytes 884744 | tf_op jit(solution)/shard_map/ppermute | solution.py:284
  9.3 8.2 %collective-permute-start.1 = (bf16[128,1152]{1,0:T(8,128)(2,1)S(1)}, bf16[128,1152]{1,0:T(8,128)(2,1)S(1)}, u32[]{:S(2)}, u32[]{:S(2)}) collective-permute-start(bf16[128,1152]{1,0:T(8,128)(2,1)S(1)} %get-tuple-element.12), channel_id=1, source_target_pairs={{0,256},{128,384},{256,0},{384,128},{1,257},{129,385},{257,1},{385... | collective-permute-start | bytes 884744 | tf_op jit(solution)/shard_map/ppermute | solution.py:284
  17.5 1.9 %collective-permute-start.2 = (bf16[128,1152]{1,0:T(8,128)(2,1)S(1)}, bf16[128,1152]{1,0:T(8,128)(2,1)S(1)}, u32[]{:S(2)}, u32[]{:S(2)}) collective-permute-start(bf16[128,1152]{1,0:T(8,128)(2,1)S(1)} %get-tuple-element.13), channel_id=1, source_target_pairs={{0,384},{128,0},{256,128},{384,256},{1,385},{129,1},{257,129},{385... | collective-permute-start | bytes 884744 | tf_op jit(solution)/shard_map/ppermute | solution.py:284
  19.4 0.5 sine_negate_fusion
  20.0 0.0 collective-permute-done.4.head
  20.0 14.2 %all-to-all-start = ((bf16[64,2,1152]{2,1,0:T(2,128)(2,1)}), bf16[64,2,1152]{2,1,0:T(2,128)(2,1)S(1)}, u32[]{:S(2)}, u32[]{:S(2)}) async-start(bf16[64,2,1152]{2,1,0:T(2,128)(2,1)} %get-tuple-element.17), calls=%async_computation | async-start | bytes 589824 | tf_op jit(solution)/shard_map/all_to_all | solution.py:286
  34.2 0.0 copy-done
  34.2 0.0 collective-permute-done.in1
  34.2 0.0 collective-permute-done.1.in2
  34.3 0.0 collective-permute-done.2.in3
  34.3 2.0 %align.1.own = bf16[512,1152]{1,0:T(8,128)(2,1)S(1)} custom-call(bf16[128,1152]{1,0:T(8,128)(2,1)S(1)} %get-tuple-element.10.in0, bf16[128,1152]{1,0:T(8,128)(2,1)S(1)} %collective-permute-done.in1, bf16[128,1152]{1,0:T(8,128)(2,1)S(1)} %collective-permute-done.1.in2, bf16[128,1152]{1,0:T(8,128)(2,1)S(1)} %collective-permute-done.2.in3, ...), custom_call_target="tpu_custom_call" | custom-call | flops 800000000 | bytes 4000000 | tf_op jit(solution)/shard_map/align/pallas_call | solution.py:291
  36.3 1.9 %collective-permute-start.3 = (bf16[512,1152]{1,0:T(8,128)(2,1)S(1)}, bf16[512,1152]{1,0:T(8,128)(2,1)S(1)}, u32[]{:S(2)}, u32[]{:S(2)}) collective-permute-start(bf16[512,1152]{1,0:T(8,128)(2,1)S(1)} %align.1.own), channel_id=1, source_target_pairs={{0,4},{4,0},{1,5},{5,1},{2,6},{6,2},{3,7},{7,3},{8,12},{12,8},{9,1... | collective-permute-start | bytes 3538952 | tf_op jit(solution)/shard_map/ppermute | solution.py:302
  38.2 18.0 %all-to-all-done = bf16[64,2,1152]{2,1,0:T(2,128)(2,1)S(1)} async-done(((bf16[64,2,1152]{2,1,0:T(2,128)(2,1)}), bf16[64,2,1152]{2,1,0:T(2,128)(2,1)S(1)}, u32[]{:S(2)}, u32[]{:S(2)}) %all-to-all-start) | async-done | bytes 294944 | tf_op jit(solution)/shard_map/all_to_all | solution.py:286
  56.2 0.1 reshape.33.refs
  56.3 0.1 pad_add_fusion.at_ref
  56.4 0.1 norms.1.norm
  56.5 0.0 collective-permute-done.3.other
  56.5 1.8 %score.1 = f32[16,24,128]{2,1,0:T(8,128)S(1)} custom-call(s32[2]{0:T(128)S(1)} %pad_add_fusion.at_ref, bf16[512,1152]{1,0:T(8,128)(2,1)S(1)} %align.1.own, bf16[512,1152]{1,0:T(8,128)(2,1)S(1)} %collective-permute-done.3.other, bf16[16,128]{1,0:T(8,128)(2,1)S(1)} %collective-permute-done.4.head, bf16[128,1152]{1,0:T(8,128)(2,1)S(1)} %reshape.33.refs, ...), custom_call_target="tpu_custom_call" | custom-call | flops 600000000 | bytes 2000000 | tf_op jit(solution)/shard_map/score/pallas_call | solution.py:315
  58.3 13.8 %all_to_all.15.got = f32[16,24,128]{2,1,0:T(8,128)S(1)} all-to-all(f32[16,24,128]{2,1,0:T(8,128)S(1)} %score.1), channel_id=1, replica_groups=mesh['y'=4,'z'=16,'core'=2,'x'=4] {'x','y'}, dimensions={0} | all-to-all | bytes 393216 | tf_op jit(solution)/shard_map/all_to_all | solution.py:325
  72.2 1.1 %sum.1 = bf16[128,1152]{1,0:T(8,128)(2,1)S(1)} custom-call(s32[2]{0:T(128)S(1)} %pad_add_fusion.at_ref, f32[16,24,128]{2,1,0:T(8,128)S(1)} %all_to_all.15.got, bf16[512,1152]{1,0:T(8,128)(2,1)S(1)} %align.1.own, bf16[512,1152]{1,0:T(8,128)(2,1)S(1)} %collective-permute-done.3.other), custom_call_target="tpu_custom_call" | custom-call | flops 300000000 | bytes 3000000 | tf_op jit(solution)/shard_map/sum/pallas_call | solution.py:326
  73.3 0.1 reshape.34
  73.4 25.9 %all_to_all.16 = bf16[64,2,1152]{2,1,0:T(2,128)(2,1)S(1)} all-to-all(bf16[64,2,1152]{2,1,0:T(2,128)(2,1)S(1)} %reshape.34), channel_id=1, replica_groups=mesh['y'=4,'z'=16,'core'=2,'x'=4] {'y','z'}, dimensions={0} | all-to-all | bytes 589824 | tf_op jit(solution)/shard_map/all_to_all | solution.py:336
  99.3 0.1 reshape.35.got
  99.4 0.8 finish.1
  (4 shorter events, 0.1 us)
Async XLA Ops:
  0.6 33.5 %copy-start = (f32[25,16,128]{2,1,0:T(8,128)S(1)}, f32[25,16,128]{2,1,0:T(8,128)}, u32[]{:S(2)}) copy-start(f32[25,16,128]{2,1,0:T(8,128)} %param.13) | copy-start | bytes 614404
  0.7 1.3 %copy-start.1 = (bf16[128,16,256]{2,1,0:T(8,128)(2,1)S(1)}, bf16[128,16,256]{2,1,0:T(8,128)(2,1)}, u32[]{:S(2)}) copy-start(bf16[128,16,256]{2,1,0:T(8,128)(2,1)} %param.7) | copy-start | bytes 3145732
  3.9 16.1 %collective-permute-start.4 = (bf16[16,128]{1,0:T(8,128)(2,1)S(1)}, bf16[16,128]{1,0:T(8,128)(2,1)S(1)}, u32[]{:S(2)}, u32[]{:S(2)}) collective-permute-start(bf16[16,128]{1,0:T(8,128)(2,1)S(1)} %get-tuple-element.15), channel_id=1, source_target_pairs={{0,4},{4,0},{1,5},{5,1},{2,6},{6,2},{3,7},{7,3},{8,12},{12,8},{9,1... | collective-permute-start | bytes 12296 | tf_op jit(solution)/shard_map/ppermute | solution.py:281
  5.8 28.5 %collective-permute-start = (bf16[128,1152]{1,0:T(8,128)(2,1)S(1)}, bf16[128,1152]{1,0:T(8,128)(2,1)S(1)}, u32[]{:S(2)}, u32[]{:S(2)}) collective-permute-start(bf16[128,1152]{1,0:T(8,128)(2,1)S(1)} %get-tuple-element.11), channel_id=1, source_target_pairs={{0,128},{128,256},{256,384},{384,0},{1,129},{129,257},{257,385},{3... | collective-permute-start | bytes 884744 | tf_op jit(solution)/shard_map/ppermute | solution.py:284
  9.3 25.0 %collective-permute-start.1 = (bf16[128,1152]{1,0:T(8,128)(2,1)S(1)}, bf16[128,1152]{1,0:T(8,128)(2,1)S(1)}, u32[]{:S(2)}, u32[]{:S(2)}) collective-permute-start(bf16[128,1152]{1,0:T(8,128)(2,1)S(1)} %get-tuple-element.12), channel_id=1, source_target_pairs={{0,256},{128,384},{256,0},{384,128},{1,257},{129,385},{257,1},{385... | collective-permute-start | bytes 884744 | tf_op jit(solution)/shard_map/ppermute | solution.py:284
  17.5 16.8 %collective-permute-start.2 = (bf16[128,1152]{1,0:T(8,128)(2,1)S(1)}, bf16[128,1152]{1,0:T(8,128)(2,1)S(1)}, u32[]{:S(2)}, u32[]{:S(2)}) collective-permute-start(bf16[128,1152]{1,0:T(8,128)(2,1)S(1)} %get-tuple-element.13), channel_id=1, source_target_pairs={{0,384},{128,0},{256,128},{384,256},{1,385},{129,1},{257,129},{385... | collective-permute-start | bytes 884744 | tf_op jit(solution)/shard_map/ppermute | solution.py:284
  20.0 36.2 %all-to-all-start = ((bf16[64,2,1152]{2,1,0:T(2,128)(2,1)}), bf16[64,2,1152]{2,1,0:T(2,128)(2,1)S(1)}, u32[]{:S(2)}, u32[]{:S(2)}) async-start(bf16[64,2,1152]{2,1,0:T(2,128)(2,1)} %get-tuple-element.17), calls=%async_computation | async-start | bytes 589824 | tf_op jit(solution)/shard_map/all_to_all | solution.py:286
  36.3 20.2 %collective-permute-start.3 = (bf16[512,1152]{1,0:T(8,128)(2,1)S(1)}, bf16[512,1152]{1,0:T(8,128)(2,1)S(1)}, u32[]{:S(2)}, u32[]{:S(2)}) collective-permute-start(bf16[512,1152]{1,0:T(8,128)(2,1)S(1)} %align.1.own), channel_id=1, source_target_pairs={{0,4},{4,0},{1,5},{5,1},{2,6},{6,2},{3,7},{7,3},{8,12},{12,8},{9,1... | collective-permute-start | bytes 3538952 | tf_op jit(solution)/shard_map/ppermute | solution.py:302

commit v9 on v6

--- a/solution.py
+++ b/solution.py
@@ -19,6 +19,7 @@
 WIDE = R_OWN * A
 FULL = WIDE + 128
 SHIFT_ROWS = 32
+NEAR, FAR = (0, 1, 3), 2
 VMEM_LIMIT = 40 * 1024 * 1024
 
 
@@ -113,7 +114,8 @@
         out[:, WIDE:] = tail
 
 
-def align_kernel(in0, in1, in2, in3, table, phases, out, parts):
+def align_kernel(*refs):
+    *blocks, table, phases, out, parts = refs
     for r in range(R_OWN):
         phase = phases[r]
         for at, value in ((0, jnp.cos(phase)), (FREQS, jnp.sin(phase))):
@@ -125,8 +127,8 @@
     dft = table[...]
     diagonal = iota((P_DEV, P_DEV), 0) == iota((P_DEV, P_DEV), 1)
     lane = iota((P_DEV, P_DEV), 1)
-    for d, block in enumerate((in0, in1, in2, in3)):
-        rows = slice(d * P_DEV, d * P_DEV + P_DEV)
+    for at, block in enumerate(blocks):
+        rows = slice(at * P_DEV, at * P_DEV + P_DEV)
         tail = block[0:16, WIDE:].astype(jnp.float32)
         rot = jnp.sum(jnp.where(diagonal, tail[1:2], 0.0), axis=1, keepdims=True)
         shift = jnp.sum(jnp.where(diagonal, tail[2:3], 0.0), axis=1, keepdims=True)
@@ -146,28 +148,28 @@
         out[rows, WIDE:] = block[:, WIDE:]
 
 
+def blocks_of(near, far):
+    return [(near, i * P_DEV, d) for i, d in enumerate(NEAR)] + [(far, 0, FAR)]
+
+
 def labels_of(rows, first, core):
     label = rows[first : first + 16, WIDE:].astype(jnp.float32)[0:1].astype(jnp.int32)
     return label ^ (core * P_DEV)
 
 
-def norm_kernel(refs, out):
-    wide = refs[:, :WIDE].astype(jnp.float32)
-    norm = jnp.sum(wide * wide, axis=1, keepdims=True)
-    out[...] = jnp.broadcast_to(norm, (P_DEV, P_DEV))
-
-
-def score_kernel(at_ref, own, other, refs, norm, out, stats):
+def score_kernel(at_ref, near, far, other_near, other_far, refs, out, stats):
     y, core = at_ref[0], at_ref[1]
     flat_refs = refs[:, :WIDE]
+    wide = flat_refs.astype(jnp.float32)
+    norm = jnp.sum(wide * wide, axis=1, keepdims=True)
     sharp = refs[:, WIDE:].astype(jnp.float32)
     class_of = iota((P_DEV, P_DEV), 0)
     diagonal = class_of == iota((P_DEV, P_DEV), 1)
-    for side, rows in enumerate((own, other)):
-        for d in range(NY):
+    for side, pair in enumerate(((near, far), (other_near, other_far))):
+        for rows, first, d in blocks_of(*pair):
             source = (y - d) & (NY - 1)
-            flat = rows[d * P_DEV : d * P_DEV + P_DEV, :WIDE]
-            member = class_of == labels_of(rows, d * P_DEV, core)
+            flat = rows[first : first + P_DEV, :WIDE]
+            member = class_of == labels_of(rows, first, core)
             scores = lax.dot_general(
                 flat_refs, flat, (((1,), (1,)), ((), ())), preferred_element_type=jnp.float32
             )
@@ -176,7 +178,7 @@
             )
             inner = jnp.sum(jnp.where(member, scores * sharp, 0.0), axis=0, keepdims=True)
             power = jnp.sum(jnp.where(diagonal, gram, 0.0), axis=0, keepdims=True)
-            ref_power = jnp.sum(jnp.where(member, norm[...], 0.0), axis=0, keepdims=True)
+            ref_power = jnp.sum(jnp.where(member, norm, 0.0), axis=0, keepdims=True)
             for at, value in enumerate((inner, power, ref_power)):
                 stats[pl.ds(at * 2 * NY + side * NY + source, 1), :] = value
     value = stats[...]
@@ -184,7 +186,7 @@
         out[i] = value
 
 
-def sum_kernel(at_ref, got, own, other, out, weights):
+def sum_kernel(at_ref, got, near, far, other_near, other_far, out, weights):
     y, core = at_ref[0], at_ref[1]
     total = got[0]
     for i in range(1, NX * NY):
@@ -192,23 +194,24 @@
     inner, power, ref_power = total[:8], total[8:16], total[16:]
     weight = jax.nn.sigmoid(inner / jnp.sqrt((power + EPSILON) * (ref_power + EPSILON)))
     weights[...] = weight.astype(jnp.bfloat16).astype(jnp.float32)
-    spread = []
-    for side, rows in enumerate((own, other)):
+    spread, arrays = [], (near, far, other_near, other_far)
+    for side in range(2):
         parts = []
-        for d in range(NY):
+        for rows, first, d in blocks_of(*arrays[2 * side : 2 * side + 2]):
             source = (y - d) & (NY - 1)
-            member = iota((P_DEV, P_DEV), 0) == labels_of(rows, d * P_DEV, core)
+            member = iota((P_DEV, P_DEV), 0) == labels_of(rows, first, core)
             weight = weights[pl.ds(side * NY + source, 1), :]
             parts.append(jnp.where(member, weight, 0.0).astype(jnp.bfloat16))
-        spread.append(jnp.concatenate(parts, axis=1))
+        spread += [jnp.concatenate(parts[:-1], axis=1), parts[-1]]
+
+    def summed(blocks):
+        pairs = zip(spread, blocks)
+        return sum(jnp.dot(a, b, preferred_element_type=jnp.float32) for a, b in pairs)
+
     for i in range(R_OWN):
         lanes = slice(i * A, i * A + A)
-        sums = jnp.dot(spread[0], own[:, lanes], preferred_element_type=jnp.float32)
-        sums = sums + jnp.dot(spread[1], other[:, lanes], preferred_element_type=jnp.float32)
-        out[:, lanes] = sums.astype(jnp.bfloat16)
-    ones = jnp.ones((NY * P_DEV, P_DEV), jnp.bfloat16)
-    sums = jnp.dot(spread[0], ones, preferred_element_type=jnp.float32)
-    sums = sums + jnp.dot(spread[1], ones, preferred_element_type=jnp.float32)
+        out[:, lanes] = summed([rows[:, lanes] for rows in arrays]).astype(jnp.bfloat16)
+    sums = summed([jnp.ones((rows.shape[0], P_DEV), jnp.bfloat16) for rows in arrays])
     high = sums.astype(jnp.bfloat16).astype(jnp.float32)
     sums = jnp.where(iota((P_DEV, P_DEV), 1) < 64, high, sums - high)
     out[:, WIDE:] = sums.astype(jnp.bfloat16)
@@ -281,39 +284,32 @@
             )
         ],
     )
+    panel = lax.all_to_all(
+        pieces, ("y", "z"), split_axis=0, concat_axis=0, tiled=True
+    )
     blocks = [dealt[0]]
     for d in range(1, NY):
         blocks.append(lax.ppermute(dealt[d], "y", [(i, (i + d) % NY) for i in range(NY)]))
-    pieces, blocks[1] = lax.optimization_barrier((pieces, blocks[1]))
-    panel = lax.all_to_all(
-        pieces, ("y", "z"), split_axis=0, concat_axis=0, tiled=True
-    )
     phases = lax.dynamic_slice_in_dim(shift_phase, y * R_OWN, R_OWN, 1).transpose(1, 0, 2)
     phases = jnp.pad(phases, ((0, 0), (0, SHIFT_ROWS - 25), (0, 0)))
-    rows = call(
-        align_kernel,
-        "align",
-        shape((NY * P_DEV, FULL), jnp.bfloat16),
-        [pltpu.VMEM((2 * SHIFT_ROWS, WIDE), jnp.bfloat16)],
-        800_000_000,
-        4_000_000,
-        [VMEM] * 6,
-        VMEM,
-    )(*blocks, spectral_table(A), phases)
-
-    other = lax.ppermute(rows, "core", [(0, 1), (1, 0)])
+    table = spectral_table(A)
+
+    def align(name, *some):
+        return call(
+            align_kernel,
+            name,
+            shape((len(some) * P_DEV, FULL), jnp.bfloat16),
+            [pltpu.VMEM((2 * SHIFT_ROWS, WIDE), jnp.bfloat16)],
+            600_000_000 if len(some) > 1 else 20_000_000_000,
+            1_000_000 * len(some),
+            [VMEM] * (len(some) + 2),
+            VMEM,
+        )(*some, table, phases)
+
+    near = align("align_near", *[blocks[d] for d in NEAR])
+    far = align("align_far", blocks[FAR])
+    rows = [near, far] + [lax.ppermute(part, "core", [(0, 1), (1, 0)]) for part in (near, far)]
     at = jnp.stack([y, core])
-    panel = panel.reshape(NY * NZ * 2, FULL)
-    norm = call(
-        norm_kernel,
-        "norms",
-        shape((P_DEV, P_DEV), jnp.float32),
-        [],
-        300_000,
-        300_000,
-        [VMEM],
-        VMEM,
-    )(panel)
     payload = call(
         score_kernel,
         "score",
@@ -321,9 +317,9 @@
         [pltpu.VMEM((6 * NY, P_DEV), jnp.float32)],
         600_000_000,
         2_000_000,
-        [SMEM] + [VMEM] * 4,
+        [SMEM] + [VMEM] * 5,
         VMEM,
-    )(at, rows, other, panel, norm)
+    )(at, *rows, panel.reshape(NY * NZ * 2, FULL))
     got = lax.all_to_all(payload, ("x", "y"), split_axis=0, concat_axis=0, tiled=True)
     sums = call(
         sum_kernel,
@@ -332,9 +328,9 @@
         [pltpu.VMEM((2 * NY, P_DEV), jnp.float32)],
         300_000_000,
         3_000_000,
-        [SMEM] + [VMEM] * 3,
+        [SMEM] + [VMEM] * 5,
         VMEM,
-    )(at, got, rows, other)
+    )(at, got, *rows)
     sums = lax.all_to_all(
         sums.reshape(NY * NZ, 2, FULL), ("y", "z"), split_axis=0, concat_axis=0, tiled=True
     )

time: 99.4 us -> 105 us (1.056)
  blocking collectives: 38.6 us -> 52 us
  waiting for transfers between devices: 14.2 us -> 9.91 us
  starting transfers between devices: 36 us -> 32.6 us
    all_to_all x1, waiting for transfers between devices: 13.2 us -> 0.01 us  [body(): lax.all_to_all(pieces, ('y', 'z'), split_axis=0, concat_axis=0, tiled=True)]
    all_to_all x1, blocking collectives: 24.7 us -> 35.1 us  [body(): lax.all_to_all(sums.reshape(NY * NZ, 2, FULL), ('y', 'z'), split_axis=0,...]
    ppermute x3, waiting for transfers between devices: 0.97 us -> 8.56 us  [body(): lax.ppermute(dealt[d], 'y', [(i, (i + d) % NY) for i in range(NY)])]
    ppermute x3, starting transfers between devices: 13.6 us -> 10 us  [body(): lax.ppermute(dealt[d], 'y', [(i, (i + d) % NY) for i in range(NY)])]
    all_to_all x1, blocking collectives: 13.9 us -> 16.9 us  [body(): lax.all_to_all(payload, ('x', 'y'), split_axis=0, concat_axis=0, tiled=True)]
    ppermute x1 -> x2, starting transfers between devices: 1.92 us -> 3.84 us  [body(): lax.ppermute(part, 'core', [(0, 1), (1, 0)])]
    all_to_all x1, starting transfers between devices: 20.5 us -> 18.7 us  [body(): lax.all_to_all(pieces, ('y', 'z'), split_axis=0, concat_axis=0, tiled=True)]
    ppermute x1 -> x2, waiting for transfers between devices: 0.01 us -> 1.35 us  [body(): lax.ppermute(part, 'core', [(0, 1), (1, 0)])]
  transfers between devices with their start and end apart: 5 -> 6, of which waited for: 2 -> 4; matrix products, arithmetic and copies ran while one was open for 1% -> 1% of each run, Pallas kernels for 2% -> 2%
where the time goes in v9:
time: 105 us
  blocking collectives  52 us (50%)
  starting transfers between devices  32.6 us (31%)
  waiting for transfers between devices  9.91 us (9%)
  Pallas kernels  8.7 us (8%)
    all_to_all x1, blocking collectives, body(): lax.all_to_all(sums.reshape(NY * NZ, 2, FULL), ('y', 'z'), split_axis=0,...  35.1 us
    all_to_all x1, starting transfers between devices, body(): lax.all_to_all(pieces, ('y', 'z'), split_axis=0, concat_axis=0, tiled=True)  18.7 us
    all_to_all x1, blocking collectives, body(): lax.all_to_all(payload, ('x', 'y'), split_axis=0, concat_axis=0, tiled=True)  16.9 us
    ppermute x3, starting transfers between devices, body(): lax.ppermute(dealt[d], 'y', [(i, (i + d) % NY) for i in range(NY)])  10 us
    ppermute x3, waiting for transfers between devices, body(): lax.ppermute(dealt[d], 'y', [(i, (i + d) % NY) for i in range(NY)])  8.56 us
    ppermute x2, starting transfers between devices, body(): lax.ppermute(part, 'core', [(0, 1), (1, 0)])  3.84 us
    pallas_call x1, Pallas kernels, body(): call(deal_kernel, 'deal', [shape((NY * NZ, 2, FULL), jnp.bfloat16)] + [bl...  2.61 us
    pallas_call x2, Pallas kernels, align(): call(align_kernel, name, shape((len(some) * P_DEV, FULL), jnp.bfloat16),...  2.23 us
  transfers between devices with their start and end apart: 6, of which 4 were waited for; matrix products, arithmetic and copies ran while one was open for 1% of the time, Pallas kernels for 2%

profile of v9, /device:TPU:8, one launch (start us, length us, event | category | flops | bytes accessed | tf_op | source)
XLA Modules:
  0.0 105.0 jit_solution(2364016639159810240)
XLA Ops:
  0.6 0.0 copy-start
  0.7 2.6 %deal.1 = (bf16[64,2,1152]{2,1,0:T(2,128)(2,1)}, bf16[128,1152]{1,0:T(8,128)(2,1)S(1)}, bf16[128,1152]{1,0:T(8,128)(2,1)S(1)}, bf16[128,1152]{1,0:T(8,128)(2,1)S(1)}, bf16[128,1152]{1,0:T(8,128)(2,1)S(1)}) custom-call(s32[1]{0:T(128)} %bitcast.y_ref, bf16[2048,256]{1,0:T(8,128)(2,1)} %bitcast.11, bf16[2,16,256]{2,1,0:T(8,128)(2,1)} %refs_hbm.1, ...), custom_call_target="tpu_custom_call" | custom-call | flops 300000000 | bytes 3000000 | tf_op jit(solution)/shard_map/deal/pallas_call | solution.py:256
  3.3 18.7 %all-to-all-start = ((bf16[64,2,1152]{2,1,0:T(2,128)(2,1)}), bf16[64,2,1152]{2,1,0:T(2,128)(2,1)S(1)}, u32[]{:S(2)}, u32[]{:S(2)}) async-start(bf16[64,2,1152]{2,1,0:T(2,128)(2,1)} %get-tuple-element.11), calls=%async_computation | async-start | bytes 589824 | tf_op jit(solution)/shard_map/all_to_all | solution.py:287
  22.0 3.5 %collective-permute-start = (bf16[128,1152]{1,0:T(8,128)(2,1)S(1)}, bf16[128,1152]{1,0:T(8,128)(2,1)S(1)}, u32[]{:S(2)}, u32[]{:S(2)}) collective-permute-start(bf16[128,1152]{1,0:T(8,128)(2,1)S(1)} %get-tuple-element.8), channel_id=1, source_target_pairs={{0,128},{128,256},{256,384},{384,0},{1,129},{129,257},{257,385},{3... | collective-permute-start | bytes 884744 | tf_op jit(solution)/shard_map/ppermute | solution.py:292
  25.5 2.4 %collective-permute-start.1 = (bf16[128,1152]{1,0:T(8,128)(2,1)S(1)}, bf16[128,1152]{1,0:T(8,128)(2,1)S(1)}, u32[]{:S(2)}, u32[]{:S(2)}) collective-permute-start(bf16[128,1152]{1,0:T(8,128)(2,1)S(1)} %get-tuple-element.9), channel_id=1, source_target_pairs={{0,384},{128,0},{256,128},{384,256},{1,385},{129,1},{257,129},{385... | collective-permute-start | bytes 884744 | tf_op jit(solution)/shard_map/ppermute | solution.py:292
  27.9 4.2 %collective-permute-start.2 = (bf16[128,1152]{1,0:T(8,128)(2,1)S(1)}, bf16[128,1152]{1,0:T(8,128)(2,1)S(1)}, u32[]{:S(2)}, u32[]{:S(2)}) collective-permute-start(bf16[128,1152]{1,0:T(8,128)(2,1)S(1)} %get-tuple-element.10), channel_id=1, source_target_pairs={{0,256},{128,384},{256,0},{384,128},{1,257},{129,385},{257,1},{385... | collective-permute-start | bytes 884744 | tf_op jit(solution)/shard_map/ppermute | solution.py:292
  32.1 0.0 copy-done
  32.1 0.5 sine_negate_fusion
  32.7 2.4 %collective-permute-done.refs_1_ = bf16[128,1152]{1,0:T(8,128)(2,1)S(1)} collective-permute-done((bf16[128,1152]{1,0:T(8,128)(2,1)S(1)}, bf16[128,1152]{1,0:T(8,128)(2,1)S(1)}, u32[]{:S(2)}, u32[]{:S(2)}) %collective-permute-start) | collective-permute-done | bytes 294944 | tf_op jit(solution)/shard_map/ppermute | solution.py:292
  35.0 3.2 %collective-permute-done.1.refs_2_ = bf16[128,1152]{1,0:T(8,128)(2,1)S(1)} collective-permute-done((bf16[128,1152]{1,0:T(8,128)(2,1)S(1)}, bf16[128,1152]{1,0:T(8,128)(2,1)S(1)}, u32[]{:S(2)}, u32[]{:S(2)}) %collective-permute-start.1) | collective-permute-done | bytes 294944 | tf_op jit(solution)/shard_map/ppermute | solution.py:292
  38.2 1.5 %align_near.1.near = bf16[384,1152]{1,0:T(8,128)(2,1)S(1)} custom-call(bf16[128,1152]{1,0:T(8,128)(2,1)S(1)} %get-tuple-element.7.refs_0_, bf16[128,1152]{1,0:T(8,128)(2,1)S(1)} %collective-permute-done.refs_1_, bf16[128,1152]{1,0:T(8,128)(2,1)S(1)} %collective-permute-done.1.refs_2_, bf16[256,256]{1,0:T(8,128)(2,1)S(1)} %fusion.refs_3_.refs_1_, ...), custom_call_target="tpu_custom_call" | custom-call | flops 600000000 | bytes 3000000 | tf_op jit(solution)/shard_map/align_near/pallas_call | solution.py:298
  39.8 1.9 %collective-permute-start.3 = (bf16[384,1152]{1,0:T(8,128)(2,1)S(1)}, bf16[384,1152]{1,0:T(8,128)(2,1)S(1)}, u32[]{:S(2)}, u32[]{:S(2)}) collective-permute-start(bf16[384,1152]{1,0:T(8,128)(2,1)S(1)} %align_near.1.near), channel_id=1, source_target_pairs={{0,4},{4,0},{1,5},{5,1},{2,6},{6,2},{3,7},{7,3},{8,12},{12,8},{9,1... | collective-permute-start | bytes 2654216 | tf_op jit(solution)/shard_map/ppermute | solution.py:311
  41.7 3.0 %collective-permute-done.2.refs_0_ = bf16[128,1152]{1,0:T(8,128)(2,1)S(1)} collective-permute-done((bf16[128,1152]{1,0:T(8,128)(2,1)S(1)}, bf16[128,1152]{1,0:T(8,128)(2,1)S(1)}, u32[]{:S(2)}, u32[]{:S(2)}) %collective-permute-start.2) | collective-permute-done | bytes 294944 | tf_op jit(solution)/shard_map/ppermute | solution.py:292
  44.7 0.7 align_far.1.far
  45.4 1.9 %collective-permute-start.4 = (bf16[128,1152]{1,0:T(8,128)(2,1)S(1)}, bf16[128,1152]{1,0:T(8,128)(2,1)S(1)}, u32[]{:S(2)}, u32[]{:S(2)}) collective-permute-start(bf16[128,1152]{1,0:T(8,128)(2,1)S(1)} %align_far.1.far), channel_id=1, source_target_pairs={{0,4},{4,0},{1,5},{5,1},{2,6},{6,2},{3,7},{7,3},{8,12},{12,8},{9,1... | collective-permute-start | bytes 884744 | tf_op jit(solution)/shard_map/ppermute | solution.py:311
  47.4 0.1 pad_add_fusion.at_ref
  47.4 0.0 all-to-all-done
  47.4 0.1 reshape.33.refs
  47.5 1.3 %collective-permute-done.4.other_far = bf16[128,1152]{1,0:T(8,128)(2,1)S(1)} collective-permute-done((bf16[128,1152]{1,0:T(8,128)(2,1)S(1)}, bf16[128,1152]{1,0:T(8,128)(2,1)S(1)}, u32[]{:S(2)}, u32[]{:S(2)}) %collective-permute-start.4) | collective-permute-done | bytes 294944 | tf_op jit(solution)/shard_map/ppermute | solution.py:311
  48.9 0.0 collective-permute-done.3.other_near
  48.9 1.8 %score.1 = f32[16,24,128]{2,1,0:T(8,128)S(1)} custom-call(s32[2]{0:T(128)S(1)} %pad_add_fusion.at_ref, bf16[384,1152]{1,0:T(8,128)(2,1)S(1)} %align_near.1.near, bf16[128,1152]{1,0:T(8,128)(2,1)S(1)} %align_far.1.far, bf16[384,1152]{1,0:T(8,128)(2,1)S(1)} %collective-permute-done.3.other_near, bf16[128,1152]{1,0:T(8,128)(2,1)S(1)} %collective-permute-done.4.other_far, ...), custom_call_target="tpu_custom_call" | custom-call | flops 600000000 | bytes 2000000 | tf_op jit(solution)/shard_map/score/pallas_call | solution.py:313
  50.7 16.9 %all_to_all.15.got = f32[16,24,128]{2,1,0:T(8,128)S(1)} all-to-all(f32[16,24,128]{2,1,0:T(8,128)S(1)} %score.1), channel_id=1, replica_groups=mesh['y'=4,'z'=16,'core'=2,'x'=4] {'x','y'}, dimensions={0} | all-to-all | bytes 393216 | tf_op jit(solution)/shard_map/all_to_all | solution.py:323
  67.6 1.2 %sum.1 = bf16[128,1152]{1,0:T(8,128)(2,1)S(1)} custom-call(s32[2]{0:T(128)S(1)} %pad_add_fusion.at_ref, f32[16,24,128]{2,1,0:T(8,128)S(1)} %all_to_all.15.got, bf16[384,1152]{1,0:T(8,128)(2,1)S(1)} %align_near.1.near, bf16[128,1152]{1,0:T(8,128)(2,1)S(1)} %align_far.1.far, bf16[384,1152]{1,0:T(8,128)(2,1)S(1)} %collective-permute-done.3.other_near, ...), custom_call_target="tpu_custom_call" | custom-call | flops 300000000 | bytes 3000000 | tf_op jit(solution)/shard_map/sum/pallas_call | solution.py:324
  68.9 0.1 reshape.34
  69.0 35.1 %all_to_all.16 = bf16[64,2,1152]{2,1,0:T(2,128)(2,1)S(1)} all-to-all(bf16[64,2,1152]{2,1,0:T(2,128)(2,1)S(1)} %reshape.34), channel_id=1, replica_groups=mesh['y'=4,'z'=16,'core'=2,'x'=4] {'y','z'}, dimensions={0} | all-to-all | bytes 589824 | tf_op jit(solution)/shard_map/all_to_all | solution.py:334
  104.1 0.1 reshape.35.got
  104.2 0.8 finish.1
  (4 shorter events, 0.1 us)
Async XLA Ops:
  0.6 31.4 %copy-start = (f32[25,16,128]{2,1,0:T(8,128)S(1)}, f32[25,16,128]{2,1,0:T(8,128)}, u32[]{:S(2)}) copy-start(f32[25,16,128]{2,1,0:T(8,128)} %param.13) | copy-start | bytes 614404
  3.3 44.2 %all-to-all-start = ((bf16[64,2,1152]{2,1,0:T(2,128)(2,1)}), bf16[64,2,1152]{2,1,0:T(2,128)(2,1)S(1)}, u32[]{:S(2)}, u32[]{:S(2)}) async-start(bf16[64,2,1152]{2,1,0:T(2,128)(2,1)} %get-tuple-element.11), calls=%async_computation | async-start | bytes 589824 | tf_op jit(solution)/shard_map/all_to_all | solution.py:287
  22.0 13.0 %collective-permute-start = (bf16[128,1152]{1,0:T(8,128)(2,1)S(1)}, bf16[128,1152]{1,0:T(8,128)(2,1)S(1)}, u32[]{:S(2)}, u32[]{:S(2)}) collective-permute-start(bf16[128,1152]{1,0:T(8,128)(2,1)S(1)} %get-tuple-element.8), channel_id=1, source_target_pairs={{0,128},{128,256},{256,384},{384,0},{1,129},{129,257},{257,385},{3... | collective-permute-start | bytes 884744 | tf_op jit(solution)/shard_map/ppermute | solution.py:292
  25.5 12.7 %collective-permute-start.1 = (bf16[128,1152]{1,0:T(8,128)(2,1)S(1)}, bf16[128,1152]{1,0:T(8,128)(2,1)S(1)}, u32[]{:S(2)}, u32[]{:S(2)}) collective-permute-start(bf16[128,1152]{1,0:T(8,128)(2,1)S(1)} %get-tuple-element.9), channel_id=1, source_target_pairs={{0,384},{128,0},{256,128},{384,256},{1,385},{129,1},{257,129},{385... | collective-permute-start | bytes 884744 | tf_op jit(solution)/shard_map/ppermute | solution.py:292
  27.9 16.9 %collective-permute-start.2 = (bf16[128,1152]{1,0:T(8,128)(2,1)S(1)}, bf16[128,1152]{1,0:T(8,128)(2,1)S(1)}, u32[]{:S(2)}, u32[]{:S(2)}) collective-permute-start(bf16[128,1152]{1,0:T(8,128)(2,1)S(1)} %get-tuple-element.10), channel_id=1, source_target_pairs={{0,256},{128,384},{256,0},{384,128},{1,257},{129,385},{257,1},{385... | collective-permute-start | bytes 884744 | tf_op jit(solution)/shard_map/ppermute | solution.py:292
  39.8 9.1 %collective-permute-start.3 = (bf16[384,1152]{1,0:T(8,128)(2,1)S(1)}, bf16[384,1152]{1,0:T(8,128)(2,1)S(1)}, u32[]{:S(2)}, u32[]{:S(2)}) collective-permute-start(bf16[384,1152]{1,0:T(8,128)(2,1)S(1)} %align_near.1.near), channel_id=1, source_target_pairs={{0,4},{4,0},{1,5},{5,1},{2,6},{6,2},{3,7},{7,3},{8,12},{12,8},{9,1... | collective-permute-start | bytes 2654216 | tf_op jit(solution)/shard_map/ppermute | solution.py:311
  45.4 3.5 %collective-permute-start.4 = (bf16[128,1152]{1,0:T(8,128)(2,1)S(1)}, bf16[128,1152]{1,0:T(8,128)(2,1)S(1)}, u32[]{:S(2)}, u32[]{:S(2)}) collective-permute-start(bf16[128,1152]{1,0:T(8,128)(2,1)S(1)} %align_far.1.far), channel_id=1, source_target_pairs={{0,4},{4,0},{1,5},{5,1},{2,6},{6,2},{3,7},{7,3},{8,12},{12,8},{9,1... | collective-permute-start | bytes 884744 | tf_op jit(solution)/shard_map/ppermute | solution.py:311

commit v10 on v6

--- a/solution.py
+++ b/solution.py
@@ -19,6 +19,7 @@
 WIDE = R_OWN * A
 FULL = WIDE + 128
 SHIFT_ROWS = 32
+STEPS = (0, 1, 3, 2)
 VMEM_LIMIT = 40 * 1024 * 1024
 
 
@@ -106,8 +107,8 @@
     at = iota((P_DEV, P_DEV), 0)
     tail = jnp.where(at == 0, label, jnp.where(at == 1, ints[1:2, :], ints[2:3, :]))
     tail = tail.astype(jnp.float32).astype(jnp.bfloat16)
-    for d, out in enumerate((out0, out1, out2, out3)):
-        first = ((y + d) & (NY - 1)) * R_OWN
+    for step, out in zip(STEPS, (out0, out1, out2, out3)):
+        first = ((y + step) & (NY - 1)) * R_OWN
         for i in range(R_OWN):
             out[:, i * A : i * A + A] = grid[first + i]
         out[:, WIDE:] = tail
@@ -165,7 +166,7 @@
     diagonal = class_of == iota((P_DEV, P_DEV), 1)
     for side, rows in enumerate((own, other)):
         for d in range(NY):
-            source = (y - d) & (NY - 1)
+            source = (y - STEPS[d]) & (NY - 1)
             flat = rows[d * P_DEV : d * P_DEV + P_DEV, :WIDE]
             member = class_of == labels_of(rows, d * P_DEV, core)
             scores = lax.dot_general(
@@ -196,7 +197,7 @@
     for side, rows in enumerate((own, other)):
         parts = []
         for d in range(NY):
-            source = (y - d) & (NY - 1)
+            source = (y - STEPS[d]) & (NY - 1)
             member = iota((P_DEV, P_DEV), 0) == labels_of(rows, d * P_DEV, core)
             weight = weights[pl.ds(side * NY + source, 1), :]
             parts.append(jnp.where(member, weight, 0.0).astype(jnp.bfloat16))
@@ -283,7 +284,8 @@
     )
     blocks = [dealt[0]]
     for d in range(1, NY):
-        blocks.append(lax.ppermute(dealt[d], "y", [(i, (i + d) % NY) for i in range(NY)]))
+        pairs = [(i, (i + STEPS[d]) % NY) for i in range(NY)]
+        blocks.append(lax.ppermute(dealt[d], "y", pairs))
     pieces, blocks[1] = lax.optimization_barrier((pieces, blocks[1]))
     panel = lax.all_to_all(
         pieces, ("y", "z"), split_axis=0, concat_axis=0, tiled=True

time: 99.4 us -> 97.5 us (0.981)
  starting transfers between devices: 36 us -> 31.1 us
  waiting for transfers between devices: 14.2 us -> 16.8 us
    all_to_all x1, starting transfers between devices: 20.5 us -> 15.6 us  [body(): lax.all_to_all(pieces, ('y', 'z'), split_axis=0, concat_axis=0, tiled=True)]
    all_to_all x1, waiting for transfers between devices: 13.2 us -> 16.8 us  [body(): lax.all_to_all(pieces, ('y', 'z'), split_axis=0, concat_axis=0, tiled=True)]
  transfers between devices with their start and end apart: 5 -> 5, of which waited for: 2 -> 1; matrix products, arithmetic and copies ran while one was open for 1% -> 1% of each run, Pallas kernels for 2% -> 2%
where the time goes in v10:
time: 97.5 us; the launch traced here: 97.1 us
  blocking collectives  38.9 us (40%)
  starting transfers between devices  31.1 us (32%)
  waiting for transfers between devices  16.8 us (17%)
  Pallas kernels  8.48 us (9%)
    all_to_all x1, blocking collectives, body(): lax.all_to_all(sums.reshape(NY * NZ, 2, FULL), ('y', 'z'), split_axis=0,...  25 us
    all_to_all x1, waiting for transfers between devices, body(): lax.all_to_all(pieces, ('y', 'z'), split_axis=0, concat_axis=0, tiled=True)  16.8 us
    all_to_all x1, starting transfers between devices, body(): lax.all_to_all(pieces, ('y', 'z'), split_axis=0, concat_axis=0, tiled=True)  15.6 us
    all_to_all x1, blocking collectives, body(): lax.all_to_all(payload, ('x', 'y'), split_axis=0, concat_axis=0, tiled=True)  13.9 us
    ppermute x3, starting transfers between devices, body(): blocks.append(lax.ppermute(dealt[d], 'y', pairs))  13.6 us
    pallas_call x1, Pallas kernels, body(): call(deal_kernel, 'deal', [shape((NY * NZ, 2, FULL), jnp.bfloat16)] + [bl...  2.61 us
    pallas_call x1, Pallas kernels, body(): call(align_kernel, 'align', shape((NY * P_DEV, FULL), jnp.bfloat16), [plt...  2.01 us
  transfers between devices with their start and end apart: 5, of which 1 were waited for; matrix products, arithmetic and copies ran while one was open for 1% of the time, Pallas kernels for 2%

profile of v10, /device:TPU:8, one launch (start us, length us, event | category | flops | bytes accessed | tf_op | source)
XLA Modules:
  0.0 97.1 jit_solution(5757606357258973773)
XLA Ops:
  0.6 0.0 copy-start
  0.7 2.6 %deal.1 = (bf16[64,2,1152]{2,1,0:T(2,128)(2,1)}, bf16[128,1152]{1,0:T(8,128)(2,1)S(1)}, bf16[128,1152]{1,0:T(8,128)(2,1)S(1)}, bf16[128,1152]{1,0:T(8,128)(2,1)S(1)}, bf16[128,1152]{1,0:T(8,128)(2,1)S(1)}) custom-call(s32[1]{0:T(128)} %bitcast.y_ref, bf16[2048,256]{1,0:T(8,128)(2,1)} %bitcast.11, bf16[2,16,256]{2,1,0:T(8,128)(2,1)} %refs_hbm.1, ...), custom_call_target="tpu_custom_call" | custom-call | flops 300000000 | bytes 3000000 | tf_op jit(solution)/shard_map/deal/pallas_call | solution.py:254
  3.3 3.5 %collective-permute-start = (bf16[128,1152]{1,0:T(8,128)(2,1)S(1)}, bf16[128,1152]{1,0:T(8,128)(2,1)S(1)}, u32[]{:S(2)}, u32[]{:S(2)}) collective-permute-start(bf16[128,1152]{1,0:T(8,128)(2,1)S(1)} %get-tuple-element.11), channel_id=1, source_target_pairs={{0,128},{128,256},{256,384},{384,0},{1,129},{129,257},{257,385},{3... | collective-permute-start | bytes 884744 | tf_op jit(solution)/shard_map/ppermute | solution.py:288
  6.8 6.2 %collective-permute-start.1 = (bf16[128,1152]{1,0:T(8,128)(2,1)S(1)}, bf16[128,1152]{1,0:T(8,128)(2,1)S(1)}, u32[]{:S(2)}, u32[]{:S(2)}) collective-permute-start(bf16[128,1152]{1,0:T(8,128)(2,1)S(1)} %get-tuple-element.13), channel_id=1, source_target_pairs={{0,384},{128,0},{256,128},{384,256},{1,385},{129,1},{257,129},{385... | collective-permute-start | bytes 884744 | tf_op jit(solution)/shard_map/ppermute | solution.py:288
  12.9 4.0 %collective-permute-start.2 = (bf16[128,1152]{1,0:T(8,128)(2,1)S(1)}, bf16[128,1152]{1,0:T(8,128)(2,1)S(1)}, u32[]{:S(2)}, u32[]{:S(2)}) collective-permute-start(bf16[128,1152]{1,0:T(8,128)(2,1)S(1)} %get-tuple-element.14), channel_id=1, source_target_pairs={{0,256},{128,384},{256,0},{384,128},{1,257},{129,385},{257,1},{385... | collective-permute-start | bytes 884744 | tf_op jit(solution)/shard_map/ppermute | solution.py:288
  16.9 0.5 sine_negate_fusion
  17.5 0.0 collective-permute-done.in1
  17.5 15.6 %all-to-all-start = ((bf16[64,2,1152]{2,1,0:T(2,128)(2,1)}), bf16[64,2,1152]{2,1,0:T(2,128)(2,1)S(1)}, u32[]{:S(2)}, u32[]{:S(2)}) async-start(bf16[64,2,1152]{2,1,0:T(2,128)(2,1)} %get-tuple-element.15), calls=%async_computation | async-start | bytes 589824 | tf_op jit(solution)/shard_map/all_to_all | solution.py:290
  33.1 0.0 copy-done
  33.1 0.0 collective-permute-done.1.in2
  33.2 0.0 collective-permute-done.2.in3
  33.2 2.0 %align.1.own = bf16[512,1152]{1,0:T(8,128)(2,1)S(1)} custom-call(bf16[128,1152]{1,0:T(8,128)(2,1)S(1)} %get-tuple-element.9.in0, bf16[128,1152]{1,0:T(8,128)(2,1)S(1)} %collective-permute-done.in1, bf16[128,1152]{1,0:T(8,128)(2,1)S(1)} %collective-permute-done.1.in2, bf16[128,1152]{1,0:T(8,128)(2,1)S(1)} %collective-permute-done.2.in3, ...), custom_call_target="tpu_custom_call" | custom-call | flops 800000000 | bytes 4000000 | tf_op jit(solution)/shard_map/align/pallas_call | solution.py:295
  35.2 1.9 %collective-permute-start.3 = (bf16[512,1152]{1,0:T(8,128)(2,1)S(1)}, bf16[512,1152]{1,0:T(8,128)(2,1)S(1)}, u32[]{:S(2)}, u32[]{:S(2)}) collective-permute-start(bf16[512,1152]{1,0:T(8,128)(2,1)S(1)} %align.1.own), channel_id=1, source_target_pairs={{0,4},{4,0},{1,5},{5,1},{2,6},{6,2},{3,7},{7,3},{8,12},{12,8},{9,1... | collective-permute-start | bytes 3538952 | tf_op jit(solution)/shard_map/ppermute | solution.py:306
  37.1 16.8 %all-to-all-done = bf16[64,2,1152]{2,1,0:T(2,128)(2,1)S(1)} async-done(((bf16[64,2,1152]{2,1,0:T(2,128)(2,1)}), bf16[64,2,1152]{2,1,0:T(2,128)(2,1)S(1)}, u32[]{:S(2)}, u32[]{:S(2)}) %all-to-all-start) | async-done | bytes 294944 | tf_op jit(solution)/shard_map/all_to_all | solution.py:290
  53.9 0.1 reshape.33.refs
  54.0 0.1 pad_add_fusion.at_ref
  54.1 0.1 norms.1.norm
  54.3 0.0 collective-permute-done.3.other
  54.3 1.8 %score.1 = f32[16,24,128]{2,1,0:T(8,128)S(1)} custom-call(s32[2]{0:T(128)S(1)} %pad_add_fusion.at_ref, bf16[512,1152]{1,0:T(8,128)(2,1)S(1)} %align.1.own, bf16[512,1152]{1,0:T(8,128)(2,1)S(1)} %collective-permute-done.3.other, bf16[128,1152]{1,0:T(8,128)(2,1)S(1)} %reshape.33.refs, f32[128,128]{1,0:T(8,128)S(1)} %norms.1.norm), custom_call_target="tpu_custom_call" | custom-call | flops 600000000 | bytes 2000000 | tf_op jit(solution)/shard_map/score/pallas_call | solution.py:319
  56.1 13.9 %all_to_all.15.got = f32[16,24,128]{2,1,0:T(8,128)S(1)} all-to-all(f32[16,24,128]{2,1,0:T(8,128)S(1)} %score.1), channel_id=1, replica_groups=mesh['y'=4,'z'=16,'core'=2,'x'=4] {'x','y'}, dimensions={0} | all-to-all | bytes 393216 | tf_op jit(solution)/shard_map/all_to_all | solution.py:329
  70.0 1.1 %sum.1 = bf16[128,1152]{1,0:T(8,128)(2,1)S(1)} custom-call(s32[2]{0:T(128)S(1)} %pad_add_fusion.at_ref, f32[16,24,128]{2,1,0:T(8,128)S(1)} %all_to_all.15.got, bf16[512,1152]{1,0:T(8,128)(2,1)S(1)} %align.1.own, bf16[512,1152]{1,0:T(8,128)(2,1)S(1)} %collective-permute-done.3.other), custom_call_target="tpu_custom_call" | custom-call | flops 300000000 | bytes 3000000 | tf_op jit(solution)/shard_map/sum/pallas_call | solution.py:330
  71.1 0.1 reshape.34
  71.2 25.0 %all_to_all.16 = bf16[64,2,1152]{2,1,0:T(2,128)(2,1)S(1)} all-to-all(bf16[64,2,1152]{2,1,0:T(2,128)(2,1)S(1)} %reshape.34), channel_id=1, replica_groups=mesh['y'=4,'z'=16,'core'=2,'x'=4] {'y','z'}, dimensions={0} | all-to-all | bytes 589824 | tf_op jit(solution)/shard_map/all_to_all | solution.py:340
  96.2 0.1 reshape.35.got
  96.3 0.8 finish.1
  (4 shorter events, 0.1 us)
Async XLA Ops:
  0.6 32.4 %copy-start = (f32[25,16,128]{2,1,0:T(8,128)S(1)}, f32[25,16,128]{2,1,0:T(8,128)}, u32[]{:S(2)}) copy-start(f32[25,16,128]{2,1,0:T(8,128)} %param.13) | copy-start | bytes 614404
  3.3 14.2 %collective-permute-start = (bf16[128,1152]{1,0:T(8,128)(2,1)S(1)}, bf16[128,1152]{1,0:T(8,128)(2,1)S(1)}, u32[]{:S(2)}, u32[]{:S(2)}) collective-permute-start(bf16[128,1152]{1,0:T(8,128)(2,1)S(1)} %get-tuple-element.11), channel_id=1, source_target_pairs={{0,128},{128,256},{256,384},{384,0},{1,129},{129,257},{257,385},{3... | collective-permute-start | bytes 884744 | tf_op jit(solution)/shard_map/ppermute | solution.py:288
  6.8 26.4 %collective-permute-start.1 = (bf16[128,1152]{1,0:T(8,128)(2,1)S(1)}, bf16[128,1152]{1,0:T(8,128)(2,1)S(1)}, u32[]{:S(2)}, u32[]{:S(2)}) collective-permute-start(bf16[128,1152]{1,0:T(8,128)(2,1)S(1)} %get-tuple-element.13), channel_id=1, source_target_pairs={{0,384},{128,0},{256,128},{384,256},{1,385},{129,1},{257,129},{385... | collective-permute-start | bytes 884744 | tf_op jit(solution)/shard_map/ppermute | solution.py:288
  12.9 20.2 %collective-permute-start.2 = (bf16[128,1152]{1,0:T(8,128)(2,1)S(1)}, bf16[128,1152]{1,0:T(8,128)(2,1)S(1)}, u32[]{:S(2)}, u32[]{:S(2)}) collective-permute-start(bf16[128,1152]{1,0:T(8,128)(2,1)S(1)} %get-tuple-element.14), channel_id=1, source_target_pairs={{0,256},{128,384},{256,0},{384,128},{1,257},{129,385},{257,1},{385... | collective-permute-start | bytes 884744 | tf_op jit(solution)/shard_map/ppermute | solution.py:288
  17.5 36.4 %all-to-all-start = ((bf16[64,2,1152]{2,1,0:T(2,128)(2,1)}), bf16[64,2,1152]{2,1,0:T(2,128)(2,1)S(1)}, u32[]{:S(2)}, u32[]{:S(2)}) async-start(bf16[64,2,1152]{2,1,0:T(2,128)(2,1)} %get-tuple-element.15), calls=%async_computation | async-start | bytes 589824 | tf_op jit(solution)/shard_map/all_to_all | solution.py:290
  35.2 19.1 %collective-permute-start.3 = (bf16[512,1152]{1,0:T(8,128)(2,1)S(1)}, bf16[512,1152]{1,0:T(8,128)(2,1)S(1)}, u32[]{:S(2)}, u32[]{:S(2)}) collective-permute-start(bf16[512,1152]{1,0:T(8,128)(2,1)S(1)} %align.1.own), channel_id=1, source_target_pairs={{0,4},{4,0},{1,5},{5,1},{2,6},{6,2},{3,7},{7,3},{8,12},{12,8},{9,1... | collective-permute-start | bytes 3538952 | tf_op jit(solution)/shard_map/ppermute | solution.py:306

commit v11 on v10

--- a/solution.py
+++ b/solution.py
@@ -72,9 +72,9 @@
             )
         )
     ]
-    quarter = P_DEV * R_DEV // 4
-    for i in range(4):
-        rows = pl.ds(i * quarter, quarter)
+    half = P_DEV * R_DEV // 2
+    for i in range(2):
+        rows = pl.ds(i * half, half)
         copies.append(pltpu.make_async_copy(images_hbm.at[rows], images.at[rows], sems.at[5 + i]))
     for copy in copies:
         copy.start()
@@ -96,8 +96,8 @@
     row, col = iota((A, A), 0), iota((A, A), 1)
     swap = (col == ((row & 15) * 16 + (row >> 4))).astype(jnp.float32).astype(jnp.bfloat16)
     for b in range(P_DEV // 16):
-        if b % 2 == 0:
-            copies[5 + b // 2].wait()
+        if b % 4 == 0:
+            copies[5 + b // 4].wait()
         x = jnp.dot(swap, images[b * A : b * A + A, :], preferred_element_type=jnp.float32)
         x = x.astype(jnp.bfloat16)
         for r in range(R_DEV):
@@ -125,7 +125,7 @@
             parts[SHIFT_ROWS : 2 * SHIFT_ROWS, lanes] = low
     dft = table[...]
     diagonal = iota((P_DEV, P_DEV), 0) == iota((P_DEV, P_DEV), 1)
-    lane = iota((P_DEV, P_DEV), 1)
+    row, lane = iota((P_DEV, P_DEV), 0), iota((P_DEV, P_DEV), 1)
     for d, block in enumerate((in0, in1, in2, in3)):
         rows = slice(d * P_DEV, d * P_DEV + P_DEV)
         tail = block[0:16, WIDE:].astype(jnp.float32)
@@ -144,18 +144,29 @@
             real, imag = spectra[:, :FREQS], spectra[:, FREQS:]
             out[rows, i * A : i * A + FREQS] = (real * cosine - imag * sine).astype(jnp.bfloat16)
             out[rows, i * A + FREQS : i * A + A] = (real * sine + imag * cosine).astype(jnp.bfloat16)
-        out[rows, WIDE:] = block[:, WIDE:]
-
-
-def labels_of(rows, first, core):
-    label = rows[first : first + 16, WIDE:].astype(jnp.float32)[0:1].astype(jnp.int32)
-    return label ^ (core * P_DEV)
+        flat = out[rows, :WIDE]
+        gram = lax.dot_general(
+            flat, flat, (((1,), (1,)), ((), ())), preferred_element_type=jnp.float32
+        )
+        power = jnp.sum(jnp.where(diagonal, gram, 0.0), axis=0, keepdims=True)
+        high = power.astype(jnp.bfloat16).astype(jnp.float32)
+        tail = jnp.where(row == 3, high, jnp.where(row == 4, power - high, block[:, WIDE:].astype(jnp.float32)))
+        out[rows, WIDE:] = tail.astype(jnp.bfloat16)
 
 
 def norm_kernel(refs, out):
     wide = refs[:, :WIDE].astype(jnp.float32)
     norm = jnp.sum(wide * wide, axis=1, keepdims=True)
     out[...] = jnp.broadcast_to(norm, (P_DEV, P_DEV))
+
+
+def tail_of(rows, d, core):
+    tail = rows[d * P_DEV : d * P_DEV + 16, WIDE:].astype(jnp.float32)
+    return tail[0:1].astype(jnp.int32) ^ (core * P_DEV), tail[3:4] + tail[4:5]
+
+
+def lanes_of(side, source):
+    return pl.ds(pl.multiple_of((side * NY + source) * P_DEV, P_DEV), P_DEV)
 
 
 def score_kernel(at_ref, own, other, refs, norm, out, stats):
@@ -166,40 +177,44 @@
     diagonal = class_of == iota((P_DEV, P_DEV), 1)
     for side, rows in enumerate((own, other)):
         for d in range(NY):
-            source = (y - STEPS[d]) & (NY - 1)
-            flat = rows[d * P_DEV : d * P_DEV + P_DEV, :WIDE]
-            member = class_of == labels_of(rows, d * P_DEV, core)
+            lanes = lanes_of(side, (y - STEPS[d]) & (NY - 1))
+            label, power = tail_of(rows, d, core)
             scores = lax.dot_general(
-                flat_refs, flat, (((1,), (1,)), ((), ())), preferred_element_type=jnp.float32
+                flat_refs,
+                rows[d * P_DEV : d * P_DEV + P_DEV, :WIDE],
+                (((1,), (1,)), ((), ())),
+                preferred_element_type=jnp.float32,
             )
-            gram = lax.dot_general(
-                flat, flat, (((1,), (1,)), ((), ())), preferred_element_type=jnp.float32
-            )
-            inner = jnp.sum(jnp.where(member, scores * sharp, 0.0), axis=0, keepdims=True)
-            power = jnp.sum(jnp.where(diagonal, gram, 0.0), axis=0, keepdims=True)
-            ref_power = jnp.sum(jnp.where(member, norm[...], 0.0), axis=0, keepdims=True)
-            for at, value in enumerate((inner, power, ref_power)):
-                stats[pl.ds(at * 2 * NY + side * NY + source, 1), :] = value
+            inner = jnp.where(class_of == label, scores * sharp, 0.0)
+            stats[0:1, lanes] = jnp.sum(inner, axis=0, keepdims=True)
+            stats[1:2, lanes] = power
+    norm_row = jnp.sum(jnp.where(diagonal, norm[...], 0.0), axis=0, keepdims=True)
+    stats[0:1, WIDE:] = norm_row
+    stats[1:2, WIDE:] = norm_row
     value = stats[...]
     for i in range(NX * NY):
         out[i] = value
 
 
-def sum_kernel(at_ref, got, own, other, out, weights):
+def sum_kernel(at_ref, got, own, other, out, stats):
     y, core = at_ref[0], at_ref[1]
     total = got[0]
     for i in range(1, NX * NY):
         total = total + got[i]
-    inner, power, ref_power = total[:8], total[8:16], total[16:]
-    weight = jax.nn.sigmoid(inner / jnp.sqrt((power + EPSILON) * (ref_power + EPSILON)))
-    weights[...] = weight.astype(jnp.bfloat16).astype(jnp.float32)
+    stats[...] = total
+    class_of = iota((P_DEV, P_DEV), 0)
+    diagonal = class_of == iota((P_DEV, P_DEV), 1)
+    norm = jnp.sum(jnp.where(diagonal, stats[0:1, WIDE:], 0.0), axis=1, keepdims=True)
     spread = []
     for side, rows in enumerate((own, other)):
         parts = []
         for d in range(NY):
-            source = (y - STEPS[d]) & (NY - 1)
-            member = iota((P_DEV, P_DEV), 0) == labels_of(rows, d * P_DEV, core)
-            weight = weights[pl.ds(side * NY + source, 1), :]
+            lanes = lanes_of(side, (y - STEPS[d]) & (NY - 1))
+            member = class_of == tail_of(rows, d, core)[0]
+            ref_power = jnp.sum(jnp.where(member, norm, 0.0), axis=0, keepdims=True)
+            inner, power = stats[0:1, lanes], stats[1:2, lanes]
+            weight = jax.nn.sigmoid(inner / jnp.sqrt((power + EPSILON) * (ref_power + EPSILON)))
+            weight = weight.astype(jnp.bfloat16).astype(jnp.float32)
             parts.append(jnp.where(member, weight, 0.0).astype(jnp.bfloat16))
         spread.append(jnp.concatenate(parts, axis=1))
     for i in range(R_OWN):
@@ -262,7 +277,7 @@
             pltpu.VMEM((1, 2), jnp.bfloat16),
             pltpu.VMEM((2 * NY, FULL), jnp.float32),
             pltpu.VMEM((R_DEV, P_DEV, A), jnp.bfloat16),
-            pltpu.SemaphoreType.DMA((9,)),
+            pltpu.SemaphoreType.DMA((7,)),
         ],
         300_000_000,
         3_000_000,
@@ -319,8 +334,8 @@
     payload = call(
         score_kernel,
         "score",
-        shape((NX * NY, 6 * NY, P_DEV), jnp.float32),
-        [pltpu.VMEM((6 * NY, P_DEV), jnp.float32)],
+        shape((NX * NY, 2, FULL), jnp.float32),
+        [pltpu.VMEM((2, FULL), jnp.float32)],
         600_000_000,
         2_000_000,
         [SMEM] + [VMEM] * 4,
@@ -331,7 +346,7 @@
         sum_kernel,
         "sum",
         shape((P_DEV, FULL), jnp.bfloat16),
-        [pltpu.VMEM((2 * NY, P_DEV), jnp.float32)],
+        [pltpu.VMEM((2, FULL), jnp.float32)],
         300_000_000,
         3_000_000,
         [SMEM] + [VMEM] * 3,

time: 97.5 us -> 96.5 us (0.990)
  transfers between devices with their start and end apart: 5 -> 5, of which waited for: 1 -> 1; matrix products, arithmetic and copies ran while one was open for 1% -> 1% of each run, Pallas kernels for 2% -> 3%
where the time goes in v11:
time: 96.5 us; the launch traced here: 96.2 us
  blocking collectives  38.6 us (40%)
  starting transfers between devices  31.1 us (32%)
  waiting for transfers between devices  16.4 us (17%)
  Pallas kernels  8.22 us (9%)
    all_to_all x1, blocking collectives, body(): lax.all_to_all(sums.reshape(NY * NZ, 2, FULL), ('y', 'z'), split_axis=0,...  25 us
    all_to_all x1, waiting for transfers between devices, body(): lax.all_to_all(pieces, ('y', 'z'), split_axis=0, concat_axis=0, tiled=True)  16.4 us
    all_to_all x1, starting transfers between devices, body(): lax.all_to_all(pieces, ('y', 'z'), split_axis=0, concat_axis=0, tiled=True)  15.6 us
    all_to_all x1, blocking collectives, body(): lax.all_to_all(payload, ('x', 'y'), split_axis=0, concat_axis=0, tiled=True)  13.7 us
    ppermute x3, starting transfers between devices, body(): blocks.append(lax.ppermute(dealt[d], 'y', pairs))  13.6 us
    pallas_call x1, Pallas kernels, body(): call(align_kernel, 'align', shape((NY * P_DEV, FULL), jnp.bfloat16), [plt...  2.47 us
    pallas_call x1, Pallas kernels, body(): call(deal_kernel, 'deal', [shape((NY * NZ, 2, FULL), jnp.bfloat16)] + [bl...  2.31 us
  transfers between devices with their start and end apart: 5, of which 1 were waited for; matrix products, arithmetic and copies ran while one was open for 1% of the time, Pallas kernels for 3%

profile of v11, /device:TPU:8, one launch (start us, length us, event | category | flops | bytes accessed | tf_op | source)
XLA Modules:
  0.0 96.2 jit_solution(5687241351345341705)
XLA Ops:
  0.6 0.0 copy-start
  0.7 2.3 %deal.1 = (bf16[64,2,1152]{2,1,0:T(2,128)(2,1)}, bf16[128,1152]{1,0:T(8,128)(2,1)S(1)}, bf16[128,1152]{1,0:T(8,128)(2,1)S(1)}, bf16[128,1152]{1,0:T(8,128)(2,1)S(1)}, bf16[128,1152]{1,0:T(8,128)(2,1)S(1)}) custom-call(s32[1]{0:T(128)} %bitcast.y_ref, bf16[2048,256]{1,0:T(8,128)(2,1)} %bitcast.11, bf16[2,16,256]{2,1,0:T(8,128)(2,1)} %refs_hbm.1, ...), custom_call_target="tpu_custom_call" | custom-call | flops 300000000 | bytes 3000000 | tf_op jit(solution)/shard_map/deal/pallas_call | solution.py:269
  3.0 3.5 %collective-permute-start = (bf16[128,1152]{1,0:T(8,128)(2,1)S(1)}, bf16[128,1152]{1,0:T(8,128)(2,1)S(1)}, u32[]{:S(2)}, u32[]{:S(2)}) collective-permute-start(bf16[128,1152]{1,0:T(8,128)(2,1)S(1)} %get-tuple-element.11), channel_id=1, source_target_pairs={{0,128},{128,256},{256,384},{384,0},{1,129},{129,257},{257,385},{3... | collective-permute-start | bytes 884744 | tf_op jit(solution)/shard_map/ppermute | solution.py:303
  6.5 6.2 %collective-permute-start.1 = (bf16[128,1152]{1,0:T(8,128)(2,1)S(1)}, bf16[128,1152]{1,0:T(8,128)(2,1)S(1)}, u32[]{:S(2)}, u32[]{:S(2)}) collective-permute-start(bf16[128,1152]{1,0:T(8,128)(2,1)S(1)} %get-tuple-element.13), channel_id=1, source_target_pairs={{0,384},{128,0},{256,128},{384,256},{1,385},{129,1},{257,129},{385... | collective-permute-start | bytes 884744 | tf_op jit(solution)/shard_map/ppermute | solution.py:303
  12.6 4.0 %collective-permute-start.2 = (bf16[128,1152]{1,0:T(8,128)(2,1)S(1)}, bf16[128,1152]{1,0:T(8,128)(2,1)S(1)}, u32[]{:S(2)}, u32[]{:S(2)}) collective-permute-start(bf16[128,1152]{1,0:T(8,128)(2,1)S(1)} %get-tuple-element.14), channel_id=1, source_target_pairs={{0,256},{128,384},{256,0},{384,128},{1,257},{129,385},{257,1},{385... | collective-permute-start | bytes 884744 | tf_op jit(solution)/shard_map/ppermute | solution.py:303
  16.6 0.5 sine_negate_fusion
  17.2 0.0 collective-permute-done.in1
  17.2 15.6 %all-to-all-start = ((bf16[64,2,1152]{2,1,0:T(2,128)(2,1)}), bf16[64,2,1152]{2,1,0:T(2,128)(2,1)S(1)}, u32[]{:S(2)}, u32[]{:S(2)}) async-start(bf16[64,2,1152]{2,1,0:T(2,128)(2,1)} %get-tuple-element.15), calls=%async_computation | async-start | bytes 589824 | tf_op jit(solution)/shard_map/all_to_all | solution.py:305
  32.8 0.0 copy-done
  32.9 0.0 collective-permute-done.1.in2
  32.9 0.0 collective-permute-done.2.in3
  32.9 2.5 %align.1.own = bf16[512,1152]{1,0:T(8,128)(2,1)S(1)} custom-call(bf16[128,1152]{1,0:T(8,128)(2,1)S(1)} %get-tuple-element.9.in0, bf16[128,1152]{1,0:T(8,128)(2,1)S(1)} %collective-permute-done.in1, bf16[128,1152]{1,0:T(8,128)(2,1)S(1)} %collective-permute-done.1.in2, bf16[128,1152]{1,0:T(8,128)(2,1)S(1)} %collective-permute-done.2.in3, ...), custom_call_target="tpu_custom_call" | custom-call | flops 800000000 | bytes 4000000 | tf_op jit(solution)/shard_map/align/pallas_call | solution.py:310
  35.4 1.9 %collective-permute-start.3 = (bf16[512,1152]{1,0:T(8,128)(2,1)S(1)}, bf16[512,1152]{1,0:T(8,128)(2,1)S(1)}, u32[]{:S(2)}, u32[]{:S(2)}) collective-permute-start(bf16[512,1152]{1,0:T(8,128)(2,1)S(1)} %align.1.own), channel_id=1, source_target_pairs={{0,4},{4,0},{1,5},{5,1},{2,6},{6,2},{3,7},{7,3},{8,12},{12,8},{9,1... | collective-permute-start | bytes 3538952 | tf_op jit(solution)/shard_map/ppermute | solution.py:321
  37.3 16.4 %all-to-all-done = bf16[64,2,1152]{2,1,0:T(2,128)(2,1)S(1)} async-done(((bf16[64,2,1152]{2,1,0:T(2,128)(2,1)}), bf16[64,2,1152]{2,1,0:T(2,128)(2,1)S(1)}, u32[]{:S(2)}, u32[]{:S(2)}) %all-to-all-start) | async-done | bytes 294944 | tf_op jit(solution)/shard_map/all_to_all | solution.py:305
  53.7 0.1 reshape.33.refs
  53.8 0.1 pad_add_fusion.at_ref
  53.8 0.1 norms.1.norm
  54.0 0.0 collective-permute-done.3.other
  54.0 1.3 %score.1 = f32[16,2,1152]{2,1,0:T(2,128)S(1)} custom-call(s32[2]{0:T(128)S(1)} %pad_add_fusion.at_ref, bf16[512,1152]{1,0:T(8,128)(2,1)S(1)} %align.1.own, bf16[512,1152]{1,0:T(8,128)(2,1)S(1)} %collective-permute-done.3.other, bf16[128,1152]{1,0:T(8,128)(2,1)S(1)} %reshape.33.refs, f32[128,128]{1,0:T(8,128)S(1)} %norms.1.norm), custom_call_target="tpu_custom_call" | custom-call | flops 600000000 | bytes 2000000 | tf_op jit(solution)/shard_map/score/pallas_call | solution.py:334
  55.2 13.7 %all_to_all.15.got = f32[16,2,1152]{2,1,0:T(2,128)S(1)} all-to-all(f32[16,2,1152]{2,1,0:T(2,128)S(1)} %score.1), channel_id=1, replica_groups=mesh['y'=4,'z'=16,'core'=2,'x'=4] {'x','y'}, dimensions={0} | all-to-all | bytes 294912 | tf_op jit(solution)/shard_map/all_to_all | solution.py:344
  68.9 1.2 %sum.1 = bf16[128,1152]{1,0:T(8,128)(2,1)S(1)} custom-call(s32[2]{0:T(128)S(1)} %pad_add_fusion.at_ref, f32[16,2,1152]{2,1,0:T(2,128)S(1)} %all_to_all.15.got, bf16[512,1152]{1,0:T(8,128)(2,1)S(1)} %align.1.own, bf16[512,1152]{1,0:T(8,128)(2,1)S(1)} %collective-permute-done.3.other), custom_call_target="tpu_custom_call" | custom-call | flops 300000000 | bytes 3000000 | tf_op jit(solution)/shard_map/sum/pallas_call | solution.py:345
  70.2 0.1 reshape.34
  70.3 25.0 %all_to_all.16 = bf16[64,2,1152]{2,1,0:T(2,128)(2,1)S(1)} all-to-all(bf16[64,2,1152]{2,1,0:T(2,128)(2,1)S(1)} %reshape.34), channel_id=1, replica_groups=mesh['y'=4,'z'=16,'core'=2,'x'=4] {'y','z'}, dimensions={0} | all-to-all | bytes 589824 | tf_op jit(solution)/shard_map/all_to_all | solution.py:355
  95.3 0.1 reshape.35.got
  95.4 0.8 finish.1
  (4 shorter events, 0.1 us)
Async XLA Ops:
  0.6 32.2 %copy-start = (f32[25,16,128]{2,1,0:T(8,128)S(1)}, f32[25,16,128]{2,1,0:T(8,128)}, u32[]{:S(2)}) copy-start(f32[25,16,128]{2,1,0:T(8,128)} %param.13) | copy-start | bytes 614404
  3.0 14.2 %collective-permute-start = (bf16[128,1152]{1,0:T(8,128)(2,1)S(1)}, bf16[128,1152]{1,0:T(8,128)(2,1)S(1)}, u32[]{:S(2)}, u32[]{:S(2)}) collective-permute-start(bf16[128,1152]{1,0:T(8,128)(2,1)S(1)} %get-tuple-element.11), channel_id=1, source_target_pairs={{0,128},{128,256},{256,384},{384,0},{1,129},{129,257},{257,385},{3... | collective-permute-start | bytes 884744 | tf_op jit(solution)/shard_map/ppermute | solution.py:303
  6.5 26.4 %collective-permute-start.1 = (bf16[128,1152]{1,0:T(8,128)(2,1)S(1)}, bf16[128,1152]{1,0:T(8,128)(2,1)S(1)}, u32[]{:S(2)}, u32[]{:S(2)}) collective-permute-start(bf16[128,1152]{1,0:T(8,128)(2,1)S(1)} %get-tuple-element.13), channel_id=1, source_target_pairs={{0,384},{128,0},{256,128},{384,256},{1,385},{129,1},{257,129},{385... | collective-permute-start | bytes 884744 | tf_op jit(solution)/shard_map/ppermute | solution.py:303
  12.6 20.2 %collective-permute-start.2 = (bf16[128,1152]{1,0:T(8,128)(2,1)S(1)}, bf16[128,1152]{1,0:T(8,128)(2,1)S(1)}, u32[]{:S(2)}, u32[]{:S(2)}) collective-permute-start(bf16[128,1152]{1,0:T(8,128)(2,1)S(1)} %get-tuple-element.14), channel_id=1, source_target_pairs={{0,256},{128,384},{256,0},{384,128},{1,257},{129,385},{257,1},{385... | collective-permute-start | bytes 884744 | tf_op jit(solution)/shard_map/ppermute | solution.py:303
  17.2 36.5 %all-to-all-start = ((bf16[64,2,1152]{2,1,0:T(2,128)(2,1)}), bf16[64,2,1152]{2,1,0:T(2,128)(2,1)S(1)}, u32[]{:S(2)}, u32[]{:S(2)}) async-start(bf16[64,2,1152]{2,1,0:T(2,128)(2,1)} %get-tuple-element.15), calls=%async_computation | async-start | bytes 589824 | tf_op jit(solution)/shard_map/all_to_all | solution.py:305
  35.4 18.6 %collective-permute-start.3 = (bf16[512,1152]{1,0:T(8,128)(2,1)S(1)}, bf16[512,1152]{1,0:T(8,128)(2,1)S(1)}, u32[]{:S(2)}, u32[]{:S(2)}) collective-permute-start(bf16[512,1152]{1,0:T(8,128)(2,1)S(1)} %align.1.own), channel_id=1, source_target_pairs={{0,4},{4,0},{1,5},{5,1},{2,6},{6,2},{3,7},{7,3},{8,12},{12,8},{9,1... | collective-permute-start | bytes 3538952 | tf_op jit(solution)/shard_map/ppermute | solution.py:321

commit v12 on v11

--- a/solution.py
+++ b/solution.py
@@ -18,6 +18,8 @@
 R_OWN = R_DEV // NY
 WIDE = R_OWN * A
 FULL = WIDE + 128
+TILES = WIDE // 128
+DEALT = TILES * P_DEV + 16
 SHIFT_ROWS = 32
 STEPS = (0, 1, 3, 2)
 VMEM_LIMIT = 40 * 1024 * 1024
@@ -104,14 +106,14 @@
             grid[r, b * 16 : b * 16 + 16, :] = x[r * 16 : r * 16 + 16]
     label = ints[0:1, :]
     label = ((label >> 1) & 1) * 128 + (label >> 2) * 2 + (label & 1)
-    at = iota((P_DEV, P_DEV), 0)
+    at = iota((16, P_DEV), 0)
     tail = jnp.where(at == 0, label, jnp.where(at == 1, ints[1:2, :], ints[2:3, :]))
     tail = tail.astype(jnp.float32).astype(jnp.bfloat16)
     for step, out in zip(STEPS, (out0, out1, out2, out3)):
         first = ((y + step) & (NY - 1)) * R_OWN
-        for i in range(R_OWN):
-            out[:, i * A : i * A + A] = grid[first + i]
-        out[:, WIDE:] = tail
+        for t in range(TILES):
+            out[t * P_DEV : t * P_DEV + P_DEV, :] = grid[first + t // 2, :, t % 2 * 128 : t % 2 * 128 + 128]
+        out[TILES * P_DEV :, :] = tail
 
 
 def align_kernel(in0, in1, in2, in3, table, phases, out, parts):
@@ -128,7 +130,7 @@
     row, lane = iota((P_DEV, P_DEV), 0), iota((P_DEV, P_DEV), 1)
     for d, block in enumerate((in0, in1, in2, in3)):
         rows = slice(d * P_DEV, d * P_DEV + P_DEV)
-        tail = block[0:16, WIDE:].astype(jnp.float32)
+        tail = block[TILES * P_DEV :, :].astype(jnp.float32)
         rot = jnp.sum(jnp.where(diagonal, tail[1:2], 0.0), axis=1, keepdims=True)
         shift = jnp.sum(jnp.where(diagonal, tail[2:3], 0.0), axis=1, keepdims=True)
         angle = ((rot.astype(jnp.int32) * lane) & (A - 1)).astype(jnp.float32) * (2.0 * math.pi / A)
@@ -138,7 +140,9 @@
         for i in range(R_OWN):
             lanes = slice(i * A, i * A + A)
             turn = jnp.dot(pick, parts[:, lanes], preferred_element_type=jnp.float32)
-            spectra = jnp.dot(block[:, lanes], dft, preferred_element_type=jnp.float32)
+            pair = [block[t * P_DEV : t * P_DEV + P_DEV, :] for t in (2 * i, 2 * i + 1)]
+            angles = jnp.concatenate(pair, axis=1)
+            spectra = jnp.dot(angles, dft, preferred_element_type=jnp.float32)
             cosine = turn[:, :FREQS] * cos_rot - turn[:, FREQS:] * sin_rot
             sine = turn[:, FREQS:] * cos_rot + turn[:, :FREQS] * sin_rot
             real, imag = spectra[:, :FREQS], spectra[:, FREQS:]
@@ -150,8 +154,9 @@
         )
         power = jnp.sum(jnp.where(diagonal, gram, 0.0), axis=0, keepdims=True)
         high = power.astype(jnp.bfloat16).astype(jnp.float32)
-        tail = jnp.where(row == 3, high, jnp.where(row == 4, power - high, block[:, WIDE:].astype(jnp.float32)))
-        out[rows, WIDE:] = tail.astype(jnp.bfloat16)
+        tail = jnp.where(row[:16] == 3, high, jnp.where(row[:16] == 4, power - high, tail))
+        out[d * P_DEV : d * P_DEV + 16, WIDE:] = tail.astype(jnp.bfloat16)
+        out[d * P_DEV + 16 : d * P_DEV + P_DEV, WIDE:] = jnp.zeros((P_DEV - 16, 128), jnp.bfloat16)
 
 
 def norm_kernel(refs, out):
@@ -265,7 +270,7 @@
     core = lax.axis_index("core").astype(jnp.int32)
     shape = jax.ShapeDtypeStruct
 
-    block = shape((P_DEV, FULL), jnp.bfloat16)
+    block = shape((DEALT, 128), jnp.bfloat16)
     pieces, *dealt = call(
         deal_kernel,
         "deal",

time: 96.5 us -> 96.3 us (level)
  starting transfers between devices: 31.1 us -> 30.1 us
    all_to_all x1, starting transfers between devices: 15.6 us -> 14.5 us  [body(): lax.all_to_all(pieces, ('y', 'z'), split_axis=0, concat_axis=0, tiled=True)]
where the time goes in v12:
time: 96.3 us; the launch traced here: 95.9 us
  blocking collectives  38.9 us (40%)
  starting transfers between devices  30.1 us (31%)
  waiting for transfers between devices  16.8 us (17%)
  Pallas kernels  8.27 us (9%)
    all_to_all x1, blocking collectives, body(): lax.all_to_all(sums.reshape(NY * NZ, 2, FULL), ('y', 'z'), split_axis=0,...  25.3 us
    all_to_all x1, waiting for transfers between devices, body(): lax.all_to_all(pieces, ('y', 'z'), split_axis=0, concat_axis=0, tiled=True)  16.8 us
    all_to_all x1, starting transfers between devices, body(): lax.all_to_all(pieces, ('y', 'z'), split_axis=0, concat_axis=0, tiled=True)  14.5 us
    ppermute x3, starting transfers between devices, body(): blocks.append(lax.ppermute(dealt[d], 'y', pairs))  13.6 us
    all_to_all x1, blocking collectives, body(): lax.all_to_all(payload, ('x', 'y'), split_axis=0, concat_axis=0, tiled=True)  13.6 us
    pallas_call x1, Pallas kernels, body(): call(align_kernel, 'align', shape((NY * P_DEV, FULL), jnp.bfloat16), [plt...  2.47 us
    pallas_call x1, Pallas kernels, body(): call(deal_kernel, 'deal', [shape((NY * NZ, 2, FULL), jnp.bfloat16)] + [bl...  2.35 us
  transfers between devices with their start and end apart: 5, of which 1 were waited for; matrix products, arithmetic and copies ran while one was open for 1% of the time, Pallas kernels for 3%

profile of v12, /device:TPU:8, one launch (start us, length us, event | category | flops | bytes accessed | tf_op | source)
XLA Modules:
  0.0 95.9 jit_solution(4820965097522218787)
XLA Ops:
  0.6 0.0 copy-start
  0.7 2.4 %deal.1 = (bf16[64,2,1152]{2,1,0:T(2,128)(2,1)}, bf16[1040,128]{1,0:T(8,128)(2,1)S(1)}, bf16[1040,128]{1,0:T(8,128)(2,1)S(1)}, bf16[1040,128]{1,0:T(8,128)(2,1)S(1)}, bf16[1040,128]{1,0:T(8,128)(2,1)S(1)}) custom-call(s32[1]{0:T(128)} %bitcast.y_ref, bf16[2048,256]{1,0:T(8,128)(2,1)} %bitcast.11, bf16[2,16,256]{2,1,0:T(8,128)(2,1)} %refs_hbm.1, ...), custom_call_target="tpu_custom_call" | custom-call | flops 300000000 | bytes 3000000 | tf_op jit(solution)/shard_map/deal/pallas_call | solution.py:274
  3.0 3.5 %collective-permute-start = (bf16[1040,128]{1,0:T(8,128)(2,1)S(1)}, bf16[1040,128]{1,0:T(8,128)(2,1)S(1)}, u32[]{:S(2)}, u32[]{:S(2)}) collective-permute-start(bf16[1040,128]{1,0:T(8,128)(2,1)S(1)} %get-tuple-element.11), channel_id=1, source_target_pairs={{0,128},{128,256},{256,384},{384,0},{1,129},{129,257},{257,385},{3... | collective-permute-start | bytes 798728 | tf_op jit(solution)/shard_map/ppermute | solution.py:308
  6.5 6.2 %collective-permute-start.1 = (bf16[1040,128]{1,0:T(8,128)(2,1)S(1)}, bf16[1040,128]{1,0:T(8,128)(2,1)S(1)}, u32[]{:S(2)}, u32[]{:S(2)}) collective-permute-start(bf16[1040,128]{1,0:T(8,128)(2,1)S(1)} %get-tuple-element.13), channel_id=1, source_target_pairs={{0,384},{128,0},{256,128},{384,256},{1,385},{129,1},{257,129},{385... | collective-permute-start | bytes 798728 | tf_op jit(solution)/shard_map/ppermute | solution.py:308
  12.7 4.0 %collective-permute-start.2 = (bf16[1040,128]{1,0:T(8,128)(2,1)S(1)}, bf16[1040,128]{1,0:T(8,128)(2,1)S(1)}, u32[]{:S(2)}, u32[]{:S(2)}) collective-permute-start(bf16[1040,128]{1,0:T(8,128)(2,1)S(1)} %get-tuple-element.14), channel_id=1, source_target_pairs={{0,256},{128,384},{256,0},{384,128},{1,257},{129,385},{257,1},{385... | collective-permute-start | bytes 798728 | tf_op jit(solution)/shard_map/ppermute | solution.py:308
  16.7 0.5 sine_negate_fusion
  17.2 0.0 collective-permute-done.in1
  17.2 14.5 %all-to-all-start = ((bf16[64,2,1152]{2,1,0:T(2,128)(2,1)}), bf16[64,2,1152]{2,1,0:T(2,128)(2,1)S(1)}, u32[]{:S(2)}, u32[]{:S(2)}) async-start(bf16[64,2,1152]{2,1,0:T(2,128)(2,1)} %get-tuple-element.15), calls=%async_computation | async-start | bytes 589824 | tf_op jit(solution)/shard_map/all_to_all | solution.py:310
  31.8 0.0 copy-done
  31.8 0.0 collective-permute-done.1.in2
  31.9 0.0 collective-permute-done.2.in3
  31.9 2.5 %align.1.own = bf16[512,1152]{1,0:T(8,128)(2,1)S(1)} custom-call(bf16[1040,128]{1,0:T(8,128)(2,1)S(1)} %get-tuple-element.9.in0, bf16[1040,128]{1,0:T(8,128)(2,1)S(1)} %collective-permute-done.in1, bf16[1040,128]{1,0:T(8,128)(2,1)S(1)} %collective-permute-done.1.in2, bf16[1040,128]{1,0:T(8,128)(2,1)S(1)} %collective-permute-done.2.in3, ...), custom_call_target="tpu_custom_call" | custom-call | flops 800000000 | bytes 4000000 | tf_op jit(solution)/shard_map/align/pallas_call | solution.py:315
  34.3 1.9 %collective-permute-start.3 = (bf16[512,1152]{1,0:T(8,128)(2,1)S(1)}, bf16[512,1152]{1,0:T(8,128)(2,1)S(1)}, u32[]{:S(2)}, u32[]{:S(2)}) collective-permute-start(bf16[512,1152]{1,0:T(8,128)(2,1)S(1)} %align.1.own), channel_id=1, source_target_pairs={{0,4},{4,0},{1,5},{5,1},{2,6},{6,2},{3,7},{7,3},{8,12},{12,8},{9,1... | collective-permute-start | bytes 3538952 | tf_op jit(solution)/shard_map/ppermute | solution.py:326
  36.3 16.8 %all-to-all-done = bf16[64,2,1152]{2,1,0:T(2,128)(2,1)S(1)} async-done(((bf16[64,2,1152]{2,1,0:T(2,128)(2,1)}), bf16[64,2,1152]{2,1,0:T(2,128)(2,1)S(1)}, u32[]{:S(2)}, u32[]{:S(2)}) %all-to-all-start) | async-done | bytes 294944 | tf_op jit(solution)/shard_map/all_to_all | solution.py:310
  53.1 0.1 reshape.33.refs
  53.2 0.1 pad_add_fusion.at_ref
  53.3 0.1 norms.1.norm
  53.4 0.0 collective-permute-done.3.other
  53.4 1.3 %score.1 = f32[16,2,1152]{2,1,0:T(2,128)S(1)} custom-call(s32[2]{0:T(128)S(1)} %pad_add_fusion.at_ref, bf16[512,1152]{1,0:T(8,128)(2,1)S(1)} %align.1.own, bf16[512,1152]{1,0:T(8,128)(2,1)S(1)} %collective-permute-done.3.other, bf16[128,1152]{1,0:T(8,128)(2,1)S(1)} %reshape.33.refs, f32[128,128]{1,0:T(8,128)S(1)} %norms.1.norm), custom_call_target="tpu_custom_call" | custom-call | flops 600000000 | bytes 2000000 | tf_op jit(solution)/shard_map/score/pallas_call | solution.py:339
  54.7 13.6 %all_to_all.15.got = f32[16,2,1152]{2,1,0:T(2,128)S(1)} all-to-all(f32[16,2,1152]{2,1,0:T(2,128)S(1)} %score.1), channel_id=1, replica_groups=mesh['y'=4,'z'=16,'core'=2,'x'=4] {'x','y'}, dimensions={0} | all-to-all | bytes 294912 | tf_op jit(solution)/shard_map/all_to_all | solution.py:349
  68.3 1.2 %sum.1 = bf16[128,1152]{1,0:T(8,128)(2,1)S(1)} custom-call(s32[2]{0:T(128)S(1)} %pad_add_fusion.at_ref, f32[16,2,1152]{2,1,0:T(2,128)S(1)} %all_to_all.15.got, bf16[512,1152]{1,0:T(8,128)(2,1)S(1)} %align.1.own, bf16[512,1152]{1,0:T(8,128)(2,1)S(1)} %collective-permute-done.3.other), custom_call_target="tpu_custom_call" | custom-call | flops 300000000 | bytes 3000000 | tf_op jit(solution)/shard_map/sum/pallas_call | solution.py:350
  69.6 0.1 reshape.34
  69.7 25.3 %all_to_all.16 = bf16[64,2,1152]{2,1,0:T(2,128)(2,1)S(1)} all-to-all(bf16[64,2,1152]{2,1,0:T(2,128)(2,1)S(1)} %reshape.34), channel_id=1, replica_groups=mesh['y'=4,'z'=16,'core'=2,'x'=4] {'y','z'}, dimensions={0} | all-to-all | bytes 589824 | tf_op jit(solution)/shard_map/all_to_all | solution.py:360
  95.0 0.1 reshape.35.got
  95.1 0.8 finish.1
  (4 shorter events, 0.1 us)
Async XLA Ops:
  0.6 31.1 %copy-start = (f32[25,16,128]{2,1,0:T(8,128)S(1)}, f32[25,16,128]{2,1,0:T(8,128)}, u32[]{:S(2)}) copy-start(f32[25,16,128]{2,1,0:T(8,128)} %param.13) | copy-start | bytes 614404
  3.0 14.2 %collective-permute-start = (bf16[1040,128]{1,0:T(8,128)(2,1)S(1)}, bf16[1040,128]{1,0:T(8,128)(2,1)S(1)}, u32[]{:S(2)}, u32[]{:S(2)}) collective-permute-start(bf16[1040,128]{1,0:T(8,128)(2,1)S(1)} %get-tuple-element.11), channel_id=1, source_target_pairs={{0,128},{128,256},{256,384},{384,0},{1,129},{129,257},{257,385},{3... | collective-permute-start | bytes 798728 | tf_op jit(solution)/shard_map/ppermute | solution.py:308
  6.5 25.3 %collective-permute-start.1 = (bf16[1040,128]{1,0:T(8,128)(2,1)S(1)}, bf16[1040,128]{1,0:T(8,128)(2,1)S(1)}, u32[]{:S(2)}, u32[]{:S(2)}) collective-permute-start(bf16[1040,128]{1,0:T(8,128)(2,1)S(1)} %get-tuple-element.13), channel_id=1, source_target_pairs={{0,384},{128,0},{256,128},{384,256},{1,385},{129,1},{257,129},{385... | collective-permute-start | bytes 798728 | tf_op jit(solution)/shard_map/ppermute | solution.py:308
  12.7 19.2 %collective-permute-start.2 = (bf16[1040,128]{1,0:T(8,128)(2,1)S(1)}, bf16[1040,128]{1,0:T(8,128)(2,1)S(1)}, u32[]{:S(2)}, u32[]{:S(2)}) collective-permute-start(bf16[1040,128]{1,0:T(8,128)(2,1)S(1)} %get-tuple-element.14), channel_id=1, source_target_pairs={{0,256},{128,384},{256,0},{384,128},{1,257},{129,385},{257,1},{385... | collective-permute-start | bytes 798728 | tf_op jit(solution)/shard_map/ppermute | solution.py:308
  17.2 35.8 %all-to-all-start = ((bf16[64,2,1152]{2,1,0:T(2,128)(2,1)}), bf16[64,2,1152]{2,1,0:T(2,128)(2,1)S(1)}, u32[]{:S(2)}, u32[]{:S(2)}) async-start(bf16[64,2,1152]{2,1,0:T(2,128)(2,1)} %get-tuple-element.15), calls=%async_computation | async-start | bytes 589824 | tf_op jit(solution)/shard_map/all_to_all | solution.py:310
  34.3 19.1 %collective-permute-start.3 = (bf16[512,1152]{1,0:T(8,128)(2,1)S(1)}, bf16[512,1152]{1,0:T(8,128)(2,1)S(1)}, u32[]{:S(2)}, u32[]{:S(2)}) collective-permute-start(bf16[512,1152]{1,0:T(8,128)(2,1)S(1)} %align.1.own), channel_id=1, source_target_pairs={{0,4},{4,0},{1,5},{5,1},{2,6},{6,2},{3,7},{7,3},{8,12},{12,8},{9,1... | collective-permute-start | bytes 3538952 | tf_op jit(solution)/shard_map/ppermute | solution.py:326

commit v13 on v12

--- a/solution.py
+++ b/solution.py
@@ -302,11 +302,13 @@
             )
         ],
     )
-    blocks = [dealt[0]]
-    for d in range(1, NY):
-        pairs = [(i, (i + STEPS[d]) % NY) for i in range(NY)]
-        blocks.append(lax.ppermute(dealt[d], "y", pairs))
-    pieces, blocks[1] = lax.optimization_barrier((pieces, blocks[1]))
+    def permuted(block, steps):
+        return lax.ppermute(block, "y", [(i, (i + steps) % NY) for i in range(NY)])
+
+    near = [permuted(dealt[d], STEPS[d]) for d in (1, 2)]
+    pieces, near[0] = lax.optimization_barrier((pieces, near[0]))
+    far, near[1] = lax.optimization_barrier((dealt[3], near[1]))
+    blocks = [dealt[0], *near, permuted(far, STEPS[3])]
     panel = lax.all_to_all(
         pieces, ("y", "z"), split_axis=0, concat_axis=0, tiled=True
     )
@@ -331,7 +333,7 @@
         "norms",
         shape((P_DEV, P_DEV), jnp.float32),
         [],
-        300_000,
+        5_000_000_000,
         300_000,
         [VMEM],
         VMEM,

time: 96.3 us -> 104 us (1.080)
  blocking collectives: 38.9 us -> 47 us
  waiting for transfers between devices: 16.8 us -> 14.5 us
  starting transfers between devices: 30.1 us -> 32.4 us
    all_to_all x1, waiting for transfers between devices: 16.8 us -> 5.09 us  [body(): lax.all_to_all(pieces, ('y', 'z'), split_axis=0, concat_axis=0, tiled=True)]
    ppermute x3, waiting for transfers between devices: 0.01 us -> 9.36 us  [permuted(): return lax.ppermute(block, 'y', [(i, (i + steps) % NY) for i in range(NY)])]
    all_to_all x1, blocking collectives: 25.3 us -> 33.4 us  [body(): lax.all_to_all(sums.reshape(NY * NZ, 2, FULL), ('y', 'z'), split_axis=0,...]
    all_to_all x1, starting transfers between devices: 14.5 us -> 16.6 us  [body(): lax.all_to_all(pieces, ('y', 'z'), split_axis=0, concat_axis=0, tiled=True)]
  transfers between devices with their start and end apart: 5 -> 5, of which waited for: 1 -> 3; matrix products, arithmetic and copies ran while one was open for 1% -> 1% of each run, Pallas kernels for 3% -> 2%
where the time goes in v13:
time: 104 us
  blocking collectives  47 us (45%)
  starting transfers between devices  32.4 us (31%)
  waiting for transfers between devices  14.5 us (14%)
  Pallas kernels  8.25 us (8%)
    all_to_all x1, blocking collectives, body(): lax.all_to_all(sums.reshape(NY * NZ, 2, FULL), ('y', 'z'), split_axis=0,...  33.4 us
    all_to_all x1, starting transfers between devices, body(): lax.all_to_all(pieces, ('y', 'z'), split_axis=0, concat_axis=0, tiled=True)  16.6 us
    ppermute x3, starting transfers between devices, permuted(): return lax.ppermute(block, 'y', [(i, (i + steps) % NY) for i in range(NY)])  13.8 us
    all_to_all x1, blocking collectives, body(): lax.all_to_all(payload, ('x', 'y'), split_axis=0, concat_axis=0, tiled=True)  13.6 us
    ppermute x3, waiting for transfers between devices, permuted(): return lax.ppermute(block, 'y', [(i, (i + steps) % NY) for i in range(NY)])  9.36 us
    all_to_all x1, waiting for transfers between devices, body(): lax.all_to_all(pieces, ('y', 'z'), split_axis=0, concat_axis=0, tiled=True)  5.09 us
    pallas_call x1, Pallas kernels, body(): call(align_kernel, 'align', shape((NY * P_DEV, FULL), jnp.bfloat16), [plt...  2.45 us
    pallas_call x1, Pallas kernels, body(): call(deal_kernel, 'deal', [shape((NY * NZ, 2, FULL), jnp.bfloat16)] + [bl...  2.35 us
  transfers between devices with their start and end apart: 5, of which 3 were waited for; matrix products, arithmetic and copies ran while one was open for 1% of the time, Pallas kernels for 2%

profile of v13, /device:TPU:8, one launch (start us, length us, event | category | flops | bytes accessed | tf_op | source)
XLA Modules:
  0.0 103.9 jit_solution(15985757120036607083)
XLA Ops:
  0.6 0.0 copy-start
  0.7 2.4 %deal.1 = (bf16[64,2,1152]{2,1,0:T(2,128)(2,1)}, bf16[1040,128]{1,0:T(8,128)(2,1)S(1)}, bf16[1040,128]{1,0:T(8,128)(2,1)S(1)}, bf16[1040,128]{1,0:T(8,128)(2,1)S(1)}, bf16[1040,128]{1,0:T(8,128)(2,1)S(1)}) custom-call(s32[1]{0:T(128)} %bitcast.y_ref, bf16[2048,256]{1,0:T(8,128)(2,1)} %bitcast.11, bf16[2,16,256]{2,1,0:T(8,128)(2,1)} %refs_hbm.1, ...), custom_call_target="tpu_custom_call" | custom-call | flops 300000000 | bytes 3000000 | tf_op jit(solution)/shard_map/deal/pallas_call | solution.py:274
  3.0 3.5 %collective-permute-start = (bf16[1040,128]{1,0:T(8,128)(2,1)S(1)}, bf16[1040,128]{1,0:T(8,128)(2,1)S(1)}, u32[]{:S(2)}, u32[]{:S(2)}) collective-permute-start(bf16[1040,128]{1,0:T(8,128)(2,1)S(1)} %get-tuple-element.13), channel_id=1, source_target_pairs={{0,128},{128,256},{256,384},{384,0},{1,129},{129,257},{257,385},{3... | collective-permute-start | bytes 798728 | tf_op jit(solution)/shard_map/ppermute | solution.py:306
  6.5 6.2 %collective-permute-start.1 = (bf16[1040,128]{1,0:T(8,128)(2,1)S(1)}, bf16[1040,128]{1,0:T(8,128)(2,1)S(1)}, u32[]{:S(2)}, u32[]{:S(2)}) collective-permute-start(bf16[1040,128]{1,0:T(8,128)(2,1)S(1)} %get-tuple-element.16), channel_id=1, source_target_pairs={{0,384},{128,0},{256,128},{384,256},{1,385},{129,1},{257,129},{385... | collective-permute-start | bytes 798728 | tf_op jit(solution)/shard_map/ppermute | solution.py:306
  12.7 2.5 %collective-permute-done.in1 = bf16[1040,128]{1,0:T(8,128)(2,1)S(1)} collective-permute-done((bf16[1040,128]{1,0:T(8,128)(2,1)S(1)}, bf16[1040,128]{1,0:T(8,128)(2,1)S(1)}, u32[]{:S(2)}, u32[]{:S(2)}) %collective-permute-start) | collective-permute-done | bytes 266272 | tf_op jit(solution)/shard_map/ppermute | solution.py:306
  15.1 16.6 %all-to-all-start = ((bf16[64,2,1152]{2,1,0:T(2,128)(2,1)}), bf16[64,2,1152]{2,1,0:T(2,128)(2,1)S(1)}, u32[]{:S(2)}, u32[]{:S(2)}) async-start(bf16[64,2,1152]{2,1,0:T(2,128)(2,1)} %get-tuple-element.19), calls=%async_computation | async-start | bytes 589824 | tf_op jit(solution)/shard_map/all_to_all | solution.py:312
  31.8 0.0 collective-permute-done.1.in2
  31.8 4.2 %collective-permute-start.2 = (bf16[1040,128]{1,0:T(8,128)(2,1)S(1)}, bf16[1040,128]{1,0:T(8,128)(2,1)S(1)}, u32[]{:S(2)}, u32[]{:S(2)}) collective-permute-start(bf16[1040,128]{1,0:T(8,128)(2,1)S(1)} %get-tuple-element.18), channel_id=1, source_target_pairs={{0,256},{128,384},{256,0},{384,128},{1,257},{129,385},{257,1},{385... | collective-permute-start | bytes 798728 | tf_op jit(solution)/shard_map/ppermute | solution.py:306
  36.0 0.0 copy-done
  36.0 0.5 sine_negate_fusion
  36.6 6.9 %collective-permute-done.2.in3 = bf16[1040,128]{1,0:T(8,128)(2,1)S(1)} collective-permute-done((bf16[1040,128]{1,0:T(8,128)(2,1)S(1)}, bf16[1040,128]{1,0:T(8,128)(2,1)S(1)}, u32[]{:S(2)}, u32[]{:S(2)}) %collective-permute-start.2) | collective-permute-done | bytes 266272 | tf_op jit(solution)/shard_map/ppermute | solution.py:306
  43.5 2.5 %align.1.own = bf16[512,1152]{1,0:T(8,128)(2,1)S(1)} custom-call(bf16[1040,128]{1,0:T(8,128)(2,1)S(1)} %get-tuple-element.11.in0, bf16[1040,128]{1,0:T(8,128)(2,1)S(1)} %collective-permute-done.in1, bf16[1040,128]{1,0:T(8,128)(2,1)S(1)} %collective-permute-done.1.in2, bf16[1040,128]{1,0:T(8,128)(2,1)S(1)} %collective-permute-done.2.in3, ...), custom_call_target="tpu_custom_call" | custom-call | flops 800000000 | bytes 4000000 | tf_op jit(solution)/shard_map/align/pallas_call | solution.py:317
  46.0 1.9 %collective-permute-start.3 = (bf16[512,1152]{1,0:T(8,128)(2,1)S(1)}, bf16[512,1152]{1,0:T(8,128)(2,1)S(1)}, u32[]{:S(2)}, u32[]{:S(2)}) collective-permute-start(bf16[512,1152]{1,0:T(8,128)(2,1)S(1)} %align.1.own), channel_id=1, source_target_pairs={{0,4},{4,0},{1,5},{5,1},{2,6},{6,2},{3,7},{7,3},{8,12},{12,8},{9,1... | collective-permute-start | bytes 3538952 | tf_op jit(solution)/shard_map/ppermute | solution.py:328
  47.9 0.1 pad_add_fusion.at_ref
  48.0 5.1 %all-to-all-done = bf16[64,2,1152]{2,1,0:T(2,128)(2,1)S(1)} async-done(((bf16[64,2,1152]{2,1,0:T(2,128)(2,1)}), bf16[64,2,1152]{2,1,0:T(2,128)(2,1)S(1)}, u32[]{:S(2)}, u32[]{:S(2)}) %all-to-all-start) | async-done | bytes 294944 | tf_op jit(solution)/shard_map/all_to_all | solution.py:312
  53.1 0.1 reshape.33.refs
  53.2 0.1 norms.1.norm
  53.3 0.0 collective-permute-done.3.other
  53.3 1.3 %score.1 = f32[16,2,1152]{2,1,0:T(2,128)S(1)} custom-call(s32[2]{0:T(128)S(1)} %pad_add_fusion.at_ref, bf16[512,1152]{1,0:T(8,128)(2,1)S(1)} %align.1.own, bf16[512,1152]{1,0:T(8,128)(2,1)S(1)} %collective-permute-done.3.other, bf16[128,1152]{1,0:T(8,128)(2,1)S(1)} %reshape.33.refs, f32[128,128]{1,0:T(8,128)S(1)} %norms.1.norm), custom_call_target="tpu_custom_call" | custom-call | flops 600000000 | bytes 2000000 | tf_op jit(solution)/shard_map/score/pallas_call | solution.py:341
  54.6 13.6 %all_to_all.15.got = f32[16,2,1152]{2,1,0:T(2,128)S(1)} all-to-all(f32[16,2,1152]{2,1,0:T(2,128)S(1)} %score.1), channel_id=1, replica_groups=mesh['y'=4,'z'=16,'core'=2,'x'=4] {'x','y'}, dimensions={0} | all-to-all | bytes 294912 | tf_op jit(solution)/shard_map/all_to_all | solution.py:351
  68.2 1.2 %sum.1 = bf16[128,1152]{1,0:T(8,128)(2,1)S(1)} custom-call(s32[2]{0:T(128)S(1)} %pad_add_fusion.at_ref, f32[16,2,1152]{2,1,0:T(2,128)S(1)} %all_to_all.15.got, bf16[512,1152]{1,0:T(8,128)(2,1)S(1)} %align.1.own, bf16[512,1152]{1,0:T(8,128)(2,1)S(1)} %collective-permute-done.3.other), custom_call_target="tpu_custom_call" | custom-call | flops 300000000 | bytes 3000000 | tf_op jit(solution)/shard_map/sum/pallas_call | solution.py:352
  69.5 0.1 reshape.34
  69.6 33.4 %all_to_all.16 = bf16[64,2,1152]{2,1,0:T(2,128)(2,1)S(1)} all-to-all(bf16[64,2,1152]{2,1,0:T(2,128)(2,1)S(1)} %reshape.34), channel_id=1, replica_groups=mesh['y'=4,'z'=16,'core'=2,'x'=4] {'y','z'}, dimensions={0} | all-to-all | bytes 589824 | tf_op jit(solution)/shard_map/all_to_all | solution.py:362
  103.0 0.1 reshape.35.got
  103.1 0.8 finish.1
  (4 shorter events, 0.1 us)
Async XLA Ops:
  0.6 35.3 %copy-start = (f32[25,16,128]{2,1,0:T(8,128)S(1)}, f32[25,16,128]{2,1,0:T(8,128)}, u32[]{:S(2)}) copy-start(f32[25,16,128]{2,1,0:T(8,128)} %param.13) | copy-start | bytes 614404
  3.0 12.1 %collective-permute-start = (bf16[1040,128]{1,0:T(8,128)(2,1)S(1)}, bf16[1040,128]{1,0:T(8,128)(2,1)S(1)}, u32[]{:S(2)}, u32[]{:S(2)}) collective-permute-start(bf16[1040,128]{1,0:T(8,128)(2,1)S(1)} %get-tuple-element.13), channel_id=1, source_target_pairs={{0,128},{128,256},{256,384},{384,0},{1,129},{129,257},{257,385},{3... | collective-permute-start | bytes 798728 | tf_op jit(solution)/shard_map/ppermute | solution.py:306
  6.5 25.3 %collective-permute-start.1 = (bf16[1040,128]{1,0:T(8,128)(2,1)S(1)}, bf16[1040,128]{1,0:T(8,128)(2,1)S(1)}, u32[]{:S(2)}, u32[]{:S(2)}) collective-permute-start(bf16[1040,128]{1,0:T(8,128)(2,1)S(1)} %get-tuple-element.16), channel_id=1, source_target_pairs={{0,384},{128,0},{256,128},{384,256},{1,385},{129,1},{257,129},{385... | collective-permute-start | bytes 798728 | tf_op jit(solution)/shard_map/ppermute | solution.py:306
  15.1 37.9 %all-to-all-start = ((bf16[64,2,1152]{2,1,0:T(2,128)(2,1)}), bf16[64,2,1152]{2,1,0:T(2,128)(2,1)S(1)}, u32[]{:S(2)}, u32[]{:S(2)}) async-start(bf16[64,2,1152]{2,1,0:T(2,128)(2,1)} %get-tuple-element.19), calls=%async_computation | async-start | bytes 589824 | tf_op jit(solution)/shard_map/all_to_all | solution.py:312
  31.8 11.7 %collective-permute-start.2 = (bf16[1040,128]{1,0:T(8,128)(2,1)S(1)}, bf16[1040,128]{1,0:T(8,128)(2,1)S(1)}, u32[]{:S(2)}, u32[]{:S(2)}) collective-permute-start(bf16[1040,128]{1,0:T(8,128)(2,1)S(1)} %get-tuple-element.18), channel_id=1, source_target_pairs={{0,256},{128,384},{256,0},{384,128},{1,257},{129,385},{257,1},{385... | collective-permute-start | bytes 798728 | tf_op jit(solution)/shard_map/ppermute | solution.py:306
  46.0 7.4 %collective-permute-start.3 = (bf16[512,1152]{1,0:T(8,128)(2,1)S(1)}, bf16[512,1152]{1,0:T(8,128)(2,1)S(1)}, u32[]{:S(2)}, u32[]{:S(2)}) collective-permute-start(bf16[512,1152]{1,0:T(8,128)(2,1)S(1)} %align.1.own), channel_id=1, source_target_pairs={{0,4},{4,0},{1,5},{5,1},{2,6},{6,2},{3,7},{7,3},{8,12},{12,8},{9,1... | collective-permute-start | bytes 3538952 | tf_op jit(solution)/shard_map/ppermute | solution.py:328
